TPU v7x, 32 devices: a whole 2x2x4 slice. The times are simulated.
32 devices in a mesh: chan: 32 (over z, y, x, core), tile: 1.
Axes of the slice: x: 2, y: 2, z: 4, core: 2. Of those that a mesh axis runs over, the one named last changes fastest.
Arguments:
- voltage: bfloat16 [1024, 131072], P('tile', 'chan'), may hold values from -6 to 6
- tap_weights: float32 [4, 1024], replicated, may hold values from -3 to 3
Outputs:
- visibility: float32 [512, 1024, 1024], P('chan', 'tile')
All inputs are finite; a program needn't handle non-finite values.
Results may differ from a plain program's by a relative error of at most 0.0047.
Values may be sent and summed in bfloat16 or wider, within the bound.
No kernel may reach another device: no remote copies, remote signals or barrier semaphores. Data moves between devices by JAX's collectives and lax.ppermute only.
A program may use at most 384 MiB of HBM per device.

v0:
```python
import math

import jax
import jax.numpy as jnp
from jax import lax
from jax.sharding import PartitionSpec as P

CHAN = 512
TAPS = 4


def passed_along(block, axis, distance):
    devices = range(lax.axis_size(axis))
    route = [(i - distance, i) for i in devices if i - distance in devices]
    return lax.ppermute(block, axis, route)


def transform_table(frame_len, channels):
    sample_index = lax.iota(jnp.int32, frame_len)
    channel_index = lax.iota(jnp.int32, channels)
    phase_index = channel_index[:, None] * sample_index[None, :] % frame_len
    angle_value = phase_index.astype(jnp.float32) * (2.0 * math.pi / frame_len)
    norm_factor = 1.0 / math.sqrt(frame_len)
    cos_part = jnp.cos(angle_value) * norm_factor
    sin_part = -jnp.sin(angle_value) * norm_factor
    return jnp.concatenate([cos_part, sin_part], 0).astype(jnp.bfloat16)


def stack_operands(turned):
    stacked_re = jnp.concatenate([turned[0], turned[1]], -1)
    stacked_im = jnp.concatenate([turned[1], -turned[0]], -1)
    return jnp.stack([stacked_re, stacked_im], 0)


def pair_products(left_rows, right_cols):
    return jnp.einsum("pcik,cjk->pcij", left_rows, right_cols, preferred_element_type=jnp.float32)


def per_device(voltage, tap_weights):
    frame_len = 2 * CHAN
    local_inputs, samples = voltage.shape
    spec_local = samples // frame_len
    history_tail = voltage[:, samples - (TAPS - 1) * frame_len :]
    earlier = passed_along(history_tail, "chan", 1)
    extended = jnp.concatenate([earlier, voltage], 1).reshape(
        local_inputs, spec_local + TAPS - 1, frame_len
    )
    filtered = jnp.zeros((local_inputs, spec_local, frame_len), jnp.float32)
    for tap_index in range(TAPS):
        shifted = extended[:, TAPS - 1 - tap_index : TAPS - 1 - tap_index + spec_local, :]
        filtered = filtered + tap_weights[tap_index][None, None, :] * shifted.astype(jnp.float32)
    filtered = filtered.astype(jnp.bfloat16).reshape(local_inputs * spec_local, frame_len)
    dft_table = transform_table(frame_len, CHAN)
    spectra = lax.dot_general(
        dft_table, filtered, (((1,), (1,)), ((), ())), preferred_element_type=jnp.float32
    )
    spectra = spectra.astype(jnp.bfloat16).reshape(2, CHAN, local_inputs, spec_local)
    turned = lax.all_to_all(
        lax.all_to_all(spectra, "chan", split_axis=1, concat_axis=3, tiled=True),
        "tile",
        split_axis=1,
        concat_axis=2,
        tiled=True,
    )
    spectra_count = turned.shape[3]
    inputs_all = turned.shape[2]
    stacked = stack_operands(turned)
    right_block = jnp.concatenate([turned[0], turned[1]], -1)
    products = pair_products(stacked, right_block) / spectra_count
    row_index = lax.iota(jnp.int32, inputs_all)[:, None]
    col_index = lax.iota(jnp.int32, inputs_all)[None, :]
    packed = jnp.where((col_index >= row_index)[None], products[0], products[1])
    return lax.all_to_all(packed, "tile", split_axis=1, concat_axis=0, tiled=True)


def solution(mesh):
    in_specs = (P("tile", "chan"), P())
    out_specs = P("chan", "tile", None)
    return jax.shard_map(
        per_device, mesh=mesh, in_specs=in_specs, out_specs=out_specs, check_vma=False
    )
```

profile of v0, /device:TPU:0, one launch (start us, length us, event | category | flops | bytes accessed | tf_op | source)
XLA Modules:
  0.0 634.1 jit_solution(7850734975121697910)
XLA Ops:
  0.0 11.9 %copy.44 = bf16[1024,4096]{0,1:T(8,128)(2,1)} copy(bf16[1024,4096]{1,0:T(8,128)(2,1)} %param.2) | data formatting | bytes 16777216 | tf_op args[0]
  11.9 0.0 copy-start.4
  11.9 0.0 copy-start.1
  11.9 3.7 slice.58
  15.6 2.9 collective-permute-start
  18.5 0.0 copy-done.4
  18.6 9.2 %multiply_convert_fusion = (bf16[512,1024]{1,0:T(8,128)(2,1)S(1)}, bf16[512,1024]{1,0:T(8,128)(2,1)}) fusion(), kind=kLoop, calls=%fused_computation.24 | loop fusion | flops 9961472 | bytes 2097152 | tf_op jit(solution)/shard_map/convert.1
  27.8 0.1 collective-permute-done
  27.9 0.0 copy-done.1
  27.9 19.7 %pad_maximum_fusion = bf16[1024,7168]{0,1:T(8,128)(2,1)S(1)} fusion(bf16[1024,4096]{0,1:T(8,128)(2,1)S(1)} %copy-done.1, bf16[1024,3072]{0,1:T(8,128)(2,1)S(1)} %collective-permute-done), kind=kLoop, calls=%fused_computation.8 | loop fusion | flops 29360128 | bytes 29360128 | tf_op jit(solution)/shard_map/concatenate | solution.py:45
  47.6 11.6 %add_convert_fusion = bf16[1024,4,1024]{0,2,1:T(8,128)(2,1)} fusion(bf16[1024,7,1024]{0,2,1:T(8,128)(2,1)S(1)} %bitcast.39, f32[1024]{0:T(1024)S(1)} %bitcast.45, f32[1024]{0:T(1024)S(1)} %bitcast.46, f32[1024]{0:T(1024)S(1)} %bitcast.44, f32[1024]{0:T(1024)S(1)} %bitcast.43), kind=kLoop, calls=%fused_computation.7 | loop fusion | flops 50331648 | bytes 41959424 | tf_op jit(solution)/shard_map/convert_element_type | solution.py:52
  59.1 14.9 %copy.46 = bf16[1024,4,1024]{2,1,0:T(4,128)(2,1)} copy(bf16[1024,4,1024]{0,2,1:T(8,128)(2,1)} %add_convert_fusion) | data formatting | bytes 16777216 | tf_op jit(solution)/shard_map/convert_element_type | solution.py:52
  74.0 0.0 copy-start.3
  74.0 12.5 %reshape.30 = bf16[4096,1024]{1,0:T(8,128)(2,1)} reshape(bf16[1024,4,1024]{2,1,0:T(4,128)(2,1)} %copy.46) | data formatting | bytes 16777216 | tf_op jit(solution)/shard_map/reshape | solution.py:52
  86.6 0.0 copy-done.3
  86.6 15.3 %convolution_convert_fusion = bf16[1024,4096]{1,0:T(8,128)(2,1)} fusion(bf16[4096,1024]{1,0:T(8,128)(2,1)} %reshape.30, bf16[512,1024]{1,0:T(8,128)(2,1)S(1)} %get-tuple-element.13, bf16[512,1024]{1,0:T(8,128)(2,1)S(1)} %copy-done.3), kind=kOutput, calls=%fused_computation.12 | convolution fusion | flops 8598323200 | bytes 18874368 | tf_op jit(solution)/shard_map/dot_general | solution.py:54
  101.9 11.9 %copy.47 = bf16[1024,4096]{0,1:T(8,128)(2,1)} copy(bf16[1024,4096]{1,0:T(8,128)(2,1)} %convolution_convert_fusion) | data formatting | bytes 16777216 | tf_op jit(solution)/shard_map/convert_element_type | solution.py:57
  113.8 14.5 %reshape.31 = bf16[2,512,1024,4]{1,0,3,2:T(2,128)(2,1)} reshape(bf16[1024,4096]{0,1:T(8,128)(2,1)} %copy.47) | data formatting | bytes 16777216 | tf_op jit(solution)/shard_map/reshape | solution.py:57
  128.3 22.3 %copy.48 = bf16[2,512,1024,4]{2,3,0,1:T(4,128)(2,1)} copy(bf16[2,512,1024,4]{1,0,3,2:T(2,128)(2,1)} %reshape.31) | data formatting | bytes 16777216 | tf_op jit(solution)/shard_map/reshape | solution.py:57
  150.6 67.8 %all-to-all-start = ((bf16[2,512,1024,4]{2,3,0,1:T(4,128)(2,1)}), bf16[2,512,1024,4]{2,3,0,1:T(4,128)(2,1)}, u32[]{:S(2)}, u32[]{:S(2)}) async-start(bf16[2,512,1024,4]{2,3,0,1:T(4,128)(2,1)} %copy.48), calls=%async_computation | async-start | bytes 16777216 | tf_op jit(solution)/shard_map/all_to_all | solution.py:59
  218.4 0.3 iota_compare_fusion
  218.7 185.6 %all-to-all-done = bf16[2,512,1024,4]{2,3,0,1:T(4,128)(2,1)} async-done(((bf16[2,512,1024,4]{2,3,0,1:T(4,128)(2,1)}), bf16[2,512,1024,4]{2,3,0,1:T(4,128)(2,1)}, u32[]{:S(2)}, u32[]{:S(2)}) %all-to-all-start) | async-done | bytes 8388640 | tf_op jit(solution)/shard_map/all_to_all | solution.py:59
  404.4 11.5 %copy.49 = bf16[2,512,1024,4]{2,1,3,0:T(8,128)(2,1)} copy(bf16[2,512,1024,4]{2,3,0,1:T(4,128)(2,1)} %all-to-all-done) | data formatting | bytes 16777216 | tf_op jit(solution)/shard_map/all_to_all | solution.py:59
  415.8 5.4 fusion.17
  421.2 2.5 copy.51
  423.7 6.6 %copy.53 = bf16[16,1024,128]{2,1,0:T(8,128)(2,1)} copy(bf16[16,1024,128]{1,0,2:T(8,128)(2,1)} %bitcast.41) | data formatting | bytes 8388608 | tf_op jit(solution)/shard_map/squeeze | solution.py:68
  430.3 5.0 copy.50
  435.3 6.6 %copy.52 = bf16[16,1024,128]{2,1,0:T(8,128)(2,1)} copy(bf16[16,1024,128]{1,0,2:T(8,128)(2,1)} %bitcast.42) | data formatting | bytes 8388608 | tf_op jit(solution)/shard_map/squeeze | solution.py:68
  441.9 0.0 copy-start
  441.9 0.0 copy-start.2
  441.9 3.5 neg.7
  445.4 0.0 copy-done
  445.4 1.2 copy-done.2
  446.6 6.3 fusion.5
  452.9 54.1 %multiply_bitcast_fusion = f32[2,16,1024,1024]{2,3,0,1:T(8,128)} fusion(bf16[1,16,1024,256]{3,2,0,1:T(8,128)(2,1)} %get-tuple-element.8, bf16[1,16,1024,256]{3,2,0,1:T(8,128)(2,1)} %get-tuple-element.7, bf16[16,1024,128]{2,1,0:T(8,128)(2,1)} %copy.53, bf16[16,1024,128]{2,1,0:T(8,128)(2,1)} %copy.52), kind=kOutput, calls=%fused_computation | convolution fusion | flops 17263755264 | bytes 159383552 | tf_op jit(solution)/shard_map/pcik,cjk->pcij/dot_general | solution.py:36
  507.0 64.3 %fusion = f32[16,1024,1024]{1,2,0:T(8,128)} fusion(f32[2,16,1024,1024]{2,3,0,1:T(8,128)} %multiply_bitcast_fusion, pred[1024,1024]{0,1:T(8,128)(4,1)S(1)} %iota_compare_fusion), kind=kLoop, calls=%fused_computation.2 | loop fusion | flops 16777216 | bytes 202375168 | tf_op jit(solution)/shard_map/jit(_where)/select_n | solution.py:72
  571.2 62.8 %copy.57 = f32[16,1024,1024]{2,1,0:T(8,128)} copy(f32[16,1024,1024]{1,2,0:T(8,128)} %fusion) | data formatting | bytes 134217728 | tf_op jit(solution)/shard_map/jit(_where)/select_n | solution.py:72
  (1 shorter events, 0.0 us)
Async XLA Ops:
  11.9 6.6 %copy-start.4 = (f32[4,1024]{1,0:T(4,128)S(1)}, f32[4,1024]{1,0:T(4,128)}, u32[]{:S(2)}) copy-start(f32[4,1024]{1,0:T(4,128)} %param.3) | copy-start | bytes 49156
  11.9 16.0 %copy-start.1 = (bf16[1024,4096]{0,1:T(8,128)(2,1)S(1)}, bf16[1024,4096]{0,1:T(8,128)(2,1)}, u32[]{:S(2)}) copy-start(bf16[1024,4096]{0,1:T(8,128)(2,1)} %copy.44) | copy-start | bytes 25165828
  15.6 12.3 %collective-permute-start = (bf16[1024,3072]{0,1:T(8,128)(2,1)S(1)}, bf16[1024,3072]{0,1:T(8,128)(2,1)S(1)}, u32[]{:S(2)}, u32[]{:S(2)}) collective-permute-start(bf16[1024,3072]{0,1:T(8,128)(2,1)S(1)} %slice.58), channel_id=1, source_target_pairs={{0,1},{1,2},{2,3},{3,4},{4,5},{5,6},{6,7},{7,8},{8,9},{9,10},{10,1... | collective-permute-start | bytes 18874376 | tf_op jit(solution)/shard_map/ppermute | solution.py:15
  74.0 12.5 %copy-start.3 = (bf16[512,1024]{1,0:T(8,128)(2,1)S(1)}, bf16[512,1024]{1,0:T(8,128)(2,1)}, u32[]{:S(2)}) copy-start(bf16[512,1024]{1,0:T(8,128)(2,1)} %get-tuple-element.14) | copy-start | bytes 3145732
  150.6 253.7 %all-to-all-start = ((bf16[2,512,1024,4]{2,3,0,1:T(4,128)(2,1)}), bf16[2,512,1024,4]{2,3,0,1:T(4,128)(2,1)}, u32[]{:S(2)}, u32[]{:S(2)}) async-start(bf16[2,512,1024,4]{2,3,0,1:T(4,128)(2,1)} %copy.48), calls=%async_computation | async-start | bytes 16777216 | tf_op jit(solution)/shard_map/all_to_all | solution.py:59
  441.9 3.5 copy-start
  441.9 4.7 copy-start.2
where the time goes:
time: 638 us; the launch traced here: 634 us
  local copies, waits for them, and re-layouts  193 us (30%)
  waiting for transfers between devices  186 us (29%)
  other arithmetic  115 us (18%)
  starting transfers between devices  70.7 us (11%)
  matrix products  69.4 us (11%)
    all_to_all x1, waiting for transfers between devices, per_device(): lax.all_to_all(spectra, 'chan', split_axis=1, concat_axis=3, tiled=True)  186 us
    all_to_all x1, starting transfers between devices, per_device(): lax.all_to_all(spectra, 'chan', split_axis=1, concat_axis=3, tiled=True)  67.8 us
    select_n x1, other arithmetic, per_device(): packed = jnp.where((col_index >= row_index)[None], products[0], products[1])  64.3 us
    select_n x1, local copies, waits for them, and re-layouts, per_device(): packed = jnp.where((col_index >= row_index)[None], products[0], products[1])  62.8 us
    dot_general x1, matrix products, pair_products(): jnp.einsum('pcik,cjk->pcij', left_rows, right_cols, preferred_element_typ...  54.1 us
    reshape x2, local copies, waits for them, and re-layouts, per_device(): spectra.astype(jnp.bfloat16).reshape(2, CHAN, local_inputs, spec_local)  36.8 us
    concatenate x1, other arithmetic, per_device(): jnp.concatenate([earlier, voltage], 1)  19.7 us
    dot_general x1, matrix products, per_device(): lax.dot_general(dft_table, filtered, (((1,), (1,)), ((), ())), preferred_...  15.3 us
  transfers between devices with their start and end apart: 2, of which 2 were waited for; matrix products, arithmetic and copies ran while one was open for 2% of the time, Pallas kernels for 0%

commit v1 on v0

--- a/solution.py
+++ b/solution.py
@@ -1,12 +1,20 @@
+import functools
 import math
 
 import jax
 import jax.numpy as jnp
+import ml_dtypes
+import numpy as np
 from jax import lax
+from jax.experimental import pallas as pl
+from jax.experimental.pallas import tpu as pltpu
 from jax.sharding import PartitionSpec as P
 
 CHAN = 512
 TAPS = 4
+VMEM_LIMIT = 56 * 1024 * 1024
+FILTER_ROWS = 32
+LANES = 128
 
 
 def passed_along(block, axis, distance):
@@ -16,14 +24,221 @@
 
 
 def transform_table(frame_len, channels):
-    sample_index = lax.iota(jnp.int32, frame_len)
-    channel_index = lax.iota(jnp.int32, channels)
-    phase_index = channel_index[:, None] * sample_index[None, :] % frame_len
-    angle_value = phase_index.astype(jnp.float32) * (2.0 * math.pi / frame_len)
-    norm_factor = 1.0 / math.sqrt(frame_len)
-    cos_part = jnp.cos(angle_value) * norm_factor
-    sin_part = -jnp.sin(angle_value) * norm_factor
-    return jnp.concatenate([cos_part, sin_part], 0).astype(jnp.bfloat16)
+    phase = np.arange(channels)[:, None] * np.arange(frame_len)[None, :] % frame_len
+    angle = phase * (2.0 * math.pi / frame_len)
+    rows = np.stack([np.cos(angle), -np.sin(angle)], 1) / math.sqrt(frame_len)
+    return rows.reshape(2 * channels, frame_len).astype(np.float32).astype(ml_dtypes.bfloat16)
+
+
+def cost(flops, moved):
+    return pl.CostEstimate(flops=flops, bytes_accessed=moved, transcendentals=0)
+
+
+def filter_transform_kernel(frame_of, spectra, dests, splits, sources, *refs):
+    voltage_refs = refs[:sources]
+    weights_ref, table_ref = refs[sources : sources + 2]
+    out_refs = refs[sources + 2 : -1]
+    filtered_ref = refs[-1]
+    rows, frame_len = filtered_ref.shape[1:]
+    needed = sorted({s - k for s in spectra for k in range(TAPS)})
+
+    for lane in range(0, frame_len, LANES):
+        weights = [
+            jnp.broadcast_to(weights_ref[k : k + 1, lane : lane + LANES], (FILTER_ROWS, LANES))
+            for k in range(TAPS)
+        ]
+
+        def body(step, carry, lane=lane, weights=weights):
+            at = pl.ds(pl.multiple_of(step * FILTER_ROWS, FILTER_ROWS), FILTER_ROWS)
+            frames = {}
+            for f in needed:
+                source, place = frame_of[f]
+                start = place * frame_len + lane
+                frames[f] = voltage_refs[source][at, start : start + LANES].astype(jnp.float32)
+            for slot, s in enumerate(spectra):
+                total = weights[0] * frames[s]
+                for k in range(1, TAPS):
+                    total = total + weights[k] * frames[s - k]
+                filtered_ref[slot, at, lane : lane + LANES] = total.astype(jnp.bfloat16)
+            return carry
+
+        lax.fori_loop(0, rows // FILTER_ROWS, body, 0, unroll=2)
+
+    per_dest = table_ref.shape[0] // dests
+    dest_block = max(1, 256 // per_dest)
+    for slot in range(len(spectra)):
+        filtered = filtered_ref[slot]
+        for first in range(0, dests, dest_block):
+            part = table_ref[first * per_dest : (first + dest_block) * per_dest, :]
+            spectrum = lax.dot_general(
+                part, filtered, (((1,), (1,)), ((), ())), preferred_element_type=jnp.float32
+            )
+            spectrum = spectrum.astype(jnp.bfloat16).reshape(dest_block, per_dest, rows)
+            begin = 0
+            for out_ref, width in zip(out_refs, splits):
+                out_ref[first : first + dest_block, slot] = spectrum[:, begin : begin + width, :]
+                begin += width
+
+
+def filter_transform(arrays, frame_of, spectra, weights, table, dests, splits, rows, first_row=0):
+    frame_len = table.shape[1]
+    block = min(256, rows)
+    per_dest = table.shape[0] // dests
+    count = len(spectra)
+    begin = first_row // block
+    widths = [a.shape[1] for a in arrays]
+    begins = [begin if a.shape[0] > rows else 0 for a in arrays]
+    in_specs = [
+        pl.BlockSpec((block, w), functools.partial(lambda b, i: (i + b, 0), b))
+        for w, b in zip(widths, begins)
+    ]
+    in_specs += [
+        pl.BlockSpec(weights.shape, lambda i: (0, 0)),
+        pl.BlockSpec(table.shape, lambda i: (0, 0)),
+    ]
+    return pl.pallas_call(
+        functools.partial(
+            filter_transform_kernel, frame_of, tuple(spectra), dests, tuple(splits), len(arrays)
+        ),
+        grid=(rows // block,),
+        in_specs=in_specs,
+        out_specs=[pl.BlockSpec((dests, count, w, block), lambda i: (0, 0, 0, i)) for w in splits],
+        out_shape=[
+            jax.ShapeDtypeStruct((dests, count, w, rows), jnp.bfloat16) for w in splits
+        ],
+        scratch_shapes=[pltpu.VMEM((count, block, frame_len), jnp.bfloat16)],
+        compiler_params=pltpu.CompilerParams(vmem_limit_bytes=VMEM_LIMIT),
+        cost_estimate=cost(
+            2 * table.size * rows * count, 2 * (sum(widths) * rows + table.size * (1 + count))
+        ),
+        name="filter_transform",
+    )(*arrays, weights, table)
+
+
+def regroup_kernel(sources, *refs):
+    spectra_refs = refs[:sources]
+    wide_ref, tall_ref, scratch = refs[sources:]
+    rows = spectra_refs[0].shape[2]
+    at = 0
+    for ref in spectra_refs:
+        devices, count, _, lanes = ref.shape
+        for d in range(devices):
+            block = ref[d].reshape(count * rows, lanes).astype(jnp.float32)
+            for tile in range(lanes // LANES):
+                scratch[tile, at : at + count * rows, :] = block[:, tile * LANES : (tile + 1) * LANES]
+            at += count * rows
+    depth = at // rows
+    for channel in range(rows // 2):
+        for part in range(2):
+            deep = slice(part * depth, (part + 1) * depth)
+            for tile in range(scratch.shape[0]):
+                across = slice(tile * LANES, (tile + 1) * LANES)
+                values = scratch[tile, pl.ds(2 * channel + part, depth, stride=rows), :]
+                wide_ref[channel, deep, across] = values.astype(jnp.bfloat16)
+                tall_ref[channel, across, deep] = values.T.astype(jnp.bfloat16)
+
+
+def regroup(arrays, pieces, rows, inputs):
+    block = min(256, inputs)
+    depth = sum(a.shape[0] * a.shape[1] for a in arrays)
+    channels = rows // 2
+    in_specs = [
+        pl.BlockSpec(
+            (a.shape[0], a.shape[1], rows, block),
+            functools.partial(lambda p, i: (0, 0, p, i), p),
+        )
+        for a, p in zip(arrays, pieces)
+    ]
+    return pl.pallas_call(
+        functools.partial(regroup_kernel, len(arrays)),
+        grid=(inputs // block,),
+        in_specs=in_specs,
+        out_specs=[
+            pl.BlockSpec((channels, 2 * depth, block), lambda i: (0, 0, i)),
+            pl.BlockSpec((channels, block, 2 * depth), lambda i: (0, i, 0)),
+        ],
+        out_shape=[
+            jax.ShapeDtypeStruct((channels, 2 * depth, inputs), jnp.bfloat16),
+            jax.ShapeDtypeStruct((channels, inputs, 2 * depth), jnp.bfloat16),
+        ],
+        scratch_shapes=[pltpu.VMEM((block // LANES, depth * rows, LANES), jnp.float32)],
+        compiler_params=pltpu.CompilerParams(vmem_limit_bytes=VMEM_LIMIT),
+        cost_estimate=cost(0, 6 * depth * rows * inputs),
+        name="regroup",
+    )(*arrays)
+
+
+def correlate_kernel(scale, *refs):
+    wide_ref, tall_ref, out_ref = refs[0], refs[1], refs[-1]
+    depth, inputs = wide_ref.shape[1:]
+    half = depth // 2
+    block = min(256, inputs)
+    wide = wide_ref[0]
+    row_index = lax.broadcasted_iota(jnp.int32, (block, block), 0)
+    col_index = lax.broadcasted_iota(jnp.int32, (block, block), 1)
+    upper = col_index >= row_index
+    for first in range(0, inputs, block):
+        re_rows = tall_ref[0, first : first + block, :]
+        im_rows = jnp.concatenate([re_rows[:, half:], -re_rows[:, :half]], 1)
+        end = first + block
+        im = jnp.dot(im_rows, wide[:, :end], preferred_element_type=jnp.float32) * scale
+        re = jnp.dot(re_rows, wide[:, first:], preferred_element_type=jnp.float32) * scale
+        if first:
+            out_ref[0, first:end, :first] = im[:, :first]
+        out_ref[0, first:end, first:end] = jnp.where(upper, re[:, :block], im[:, first:])
+        if end < inputs:
+            out_ref[0, first:end, end:] = re[:, block:]
+
+
+def correlate(wide, tall, total_channels, first_channel, spectra_count, out=None):
+    channels, depth, inputs = wide.shape
+    in_specs = [
+        pl.BlockSpec((1, depth, inputs), lambda c: (c, 0, 0)),
+        pl.BlockSpec((1, inputs, depth), lambda c: (c, 0, 0)),
+    ]
+    args, aliases = [wide, tall], {}
+    if out is not None:
+        in_specs.append(pl.BlockSpec(memory_space=pl.ANY))
+        args.append(out)
+        aliases = {2: 0}
+    return pl.pallas_call(
+        functools.partial(correlate_kernel, 1.0 / spectra_count),
+        grid=(channels,),
+        in_specs=in_specs,
+        out_specs=pl.BlockSpec((1, inputs, inputs), lambda c: (c + first_channel, 0, 0)),
+        out_shape=jax.ShapeDtypeStruct((total_channels, inputs, inputs), jnp.float32),
+        input_output_aliases=aliases,
+        compiler_params=pltpu.CompilerParams(vmem_limit_bytes=VMEM_LIMIT),
+        cost_estimate=cost(
+            2 * channels * depth * inputs * inputs, channels * inputs * (4 * depth + 4 * inputs)
+        ),
+        name="correlate",
+    )(*args)
+
+
+def per_device(voltage, tap_weights):
+    frame_len = 2 * CHAN
+    inputs, samples = voltage.shape
+    spec_local = samples // frame_len
+    devices = lax.axis_size("chan")
+    channels = CHAN // devices
+    table = jnp.asarray(transform_table(frame_len, CHAN))
+    past = TAPS - 1
+    earlier = passed_along(voltage[:, samples - past * frame_len :], "chan", 1)
+    frame_of = {f: (1, f) for f in range(spec_local)}
+    frame_of.update({-1 - k: (0, past - 1 - k) for k in range(past)})
+    splits = [channels, channels]
+    blocks = filter_transform(
+        [earlier, voltage], frame_of, range(spec_local), tap_weights, table, devices, splits, inputs
+    )
+    result = None
+    for piece, block in enumerate(blocks):
+        turned = lax.all_to_all(block, "chan", split_axis=0, concat_axis=0, tiled=True)
+        wide, tall = regroup([turned], [0], channels, inputs)
+        result = correlate(
+            wide, tall, channels, piece * channels // 2, devices * spec_local, result
+        )
+    return result
 
 
 def stack_operands(turned):
@@ -36,7 +251,7 @@
     return jnp.einsum("pcik,cjk->pcij", left_rows, right_cols, preferred_element_type=jnp.float32)
 
 
-def per_device(voltage, tap_weights):
+def per_device_tiled(voltage, tap_weights):
     frame_len = 2 * CHAN
     local_inputs, samples = voltage.shape
     spec_local = samples // frame_len
@@ -50,7 +265,8 @@
         shifted = extended[:, TAPS - 1 - tap_index : TAPS - 1 - tap_index + spec_local, :]
         filtered = filtered + tap_weights[tap_index][None, None, :] * shifted.astype(jnp.float32)
     filtered = filtered.astype(jnp.bfloat16).reshape(local_inputs * spec_local, frame_len)
-    dft_table = transform_table(frame_len, CHAN)
+    dft_table = jnp.asarray(transform_table(frame_len, CHAN)).reshape(CHAN, 2, frame_len)
+    dft_table = dft_table.swapaxes(0, 1).reshape(2 * CHAN, frame_len)
     spectra = lax.dot_general(
         dft_table, filtered, (((1,), (1,)), ((), ())), preferred_element_type=jnp.float32
     )
@@ -76,6 +292,7 @@
 def solution(mesh):
     in_specs = (P("tile", "chan"), P())
     out_specs = P("chan", "tile", None)
+    body = per_device if mesh.shape["tile"] == 1 else per_device_tiled
     return jax.shard_map(
-        per_device, mesh=mesh, in_specs=in_specs, out_specs=out_specs, check_vma=False
-    )
+        body, mesh=mesh, in_specs=in_specs, out_specs=out_specs, check_vma=False
+    )

time: 638 us -> 322 us (0.50)
  local copies, waits for them, and re-layouts: 193 us -> 5.93 us
  blocking collectives: 0 us -> 161 us
  other arithmetic: 115 us -> 0 us
  waiting for transfers between devices: 186 us -> 80.4 us
  matrix products: 69.4 us -> 0 us
  Pallas kernels: 0 us -> 66.7 us
  starting transfers between devices: 70.7 us -> 6.6 us
    all_to_all x0 -> x1, blocking collectives: none -> 161 us  [per_device(): lax.all_to_all(block, 'chan', split_axis=0, concat_axis=0, tiled=True)]
    all_to_all x1, waiting for transfers between devices: 186 us -> 71 us  [per_device(): lax.all_to_all(block, 'chan', split_axis=0, concat_axis=0, tiled=True)]
    dot_general x2 -> x0, matrix products: 69.4 us -> none  [the longest x1 54.1 us: pair_products(): jnp.einsum('pcik,cjk->pcij', left_rows, right_cols, preferred_element_typ...]
    pallas_call x0 -> x5, Pallas kernels: none -> 66.7 us  [the longest x2 30.5 us: correlate(): pl.pallas_call(functools.partial(correlate_kernel, 1.0 / spectra_count),...]
    select_n x1 -> x0, other arithmetic: 64.3 us -> none  [per_device(): packed = jnp.where((col_index >= row_index)[None], products[0], products[1])]
    all_to_all x1, starting transfers between devices: 67.8 us -> 3.84 us  [per_device(): lax.all_to_all(block, 'chan', split_axis=0, concat_axis=0, tiled=True)]
    select_n x1 -> x0, local copies, waits for them, and re-layouts: 62.8 us -> none  [per_device(): packed = jnp.where((col_index >= row_index)[None], products[0], products[1])]
    reshape x3 -> x0, local copies, waits for them, and re-layouts: 49.4 us -> none  [the longest x2 36.8 us: per_device(): spectra.astype(jnp.bfloat16).reshape(2, CHAN, local_inputs, spec_local)]
  transfers between devices with their start and end apart: 2 -> 2, of which waited for: 2 -> 2; matrix products, arithmetic and copies ran while one was open for 2% -> 0% of each run, Pallas kernels for 0% -> 7%
where the time goes in v1:
time: 322 us; the launch traced here: 321 us
  blocking collectives  161 us (50%)
  waiting for transfers between devices  80.4 us (25%)
  Pallas kernels  66.7 us (21%)
  starting transfers between devices  6.6 us (2%)
  local copies, waits for them, and re-layouts  5.93 us (2%)
    all_to_all x1, blocking collectives, per_device(): lax.all_to_all(block, 'chan', split_axis=0, concat_axis=0, tiled=True)  161 us
    all_to_all x1, waiting for transfers between devices, per_device(): lax.all_to_all(block, 'chan', split_axis=0, concat_axis=0, tiled=True)  71 us
    pallas_call x2, Pallas kernels, correlate(): pl.pallas_call(functools.partial(correlate_kernel, 1.0 / spectra_count),...  30.5 us
    pallas_call x1, Pallas kernels, filter_transform(): pl.pallas_call(functools.partial(filter_transform_kernel, frame_of, tuple...  21.1 us
    pallas_call x2, Pallas kernels, regroup(): pl.pallas_call(functools.partial(regroup_kernel, len(arrays)), grid=(inpu...  15.1 us
    ppermute x1, waiting for transfers between devices, passed_along(): return lax.ppermute(block, axis, route)  9.36 us
  transfers between devices with their start and end apart: 2, of which 2 were waited for; matrix products, arithmetic and copies ran while one was open for 0% of the time, Pallas kernels for 7%

profile of v1, /device:TPU:0, one launch (start us, length us, event | category | flops | bytes accessed | tf_op | source)
XLA Modules:
  0.0 320.9 jit_solution(10294962955339203596)
XLA Ops:
  0.0 3.2 %slice.3 = bf16[1024,3072]{1,0:T(8,128)(2,1)S(1)} slice(bf16[1024,4096]{1,0:T(8,128)(2,1)} %refs_1_.1), slice={[0:1024], [1024:4096]} | slice | bytes 12582912 | tf_op jit(solution)/shard_map/slice | solution.py:227
  3.2 2.8 collective-permute-start
  6.0 9.4 %collective-permute-done.refs_0_ = bf16[1024,3072]{1,0:T(8,128)(2,1)S(1)} collective-permute-done((bf16[1024,3072]{1,0:T(8,128)(2,1)S(1)}, bf16[1024,3072]{1,0:T(8,128)(2,1)S(1)}, u32[]{:S(2)}, u32[]{:S(2)}) %collective-permute-start) | collective-permute-done | bytes 6291488 | tf_op jit(solution)/shard_map/ppermute | solution.py:23
  15.4 0.0 copy-start
  15.4 2.7 copy-done
  18.1 21.1 %filter_transform.1 = (bf16[32,4,16,1024]{3,2,1,0:T(8,128)(2,1)}, bf16[32,4,16,1024]{3,2,1,0:T(8,128)(2,1)}) custom-call(bf16[1024,3072]{1,0:T(8,128)(2,1)} %copy-done, bf16[1024,4096]{1,0:T(8,128)(2,1)} %refs_1_.1, f32[4,1024]{1,0:T(4,128)} %refs_2_.1, bf16[1024,1024]{1,0:T(8,128)(2,1)} %constant.2.clone.refs_3_), custom_call_target="tpu_custom_call" | custom-call | flops 8589934592 | bytes 25165824 | tf_op jit(solution)/shard_map/filter_transform/pallas_call | solution.py:99
  39.2 161.2 %all_to_all.10.refs_0_ = bf16[32,4,16,1024]{3,2,1,0:T(8,128)(2,1)} all-to-all(bf16[32,4,16,1024]{3,2,1,0:T(8,128)(2,1)} %get-tuple-element.14), channel_id=1, replica_groups=mesh['chan'=32,'tile'=1] {'chan'}, dimensions={0} | all-to-all | bytes 8388608 | tf_op jit(solution)/shard_map/all_to_all | solution.py:236
  200.4 3.8 %all-to-all-start = ((bf16[32,4,16,1024]{3,2,1,0:T(8,128)(2,1)}), bf16[32,4,16,1024]{3,2,1,0:T(8,128)(2,1)}, u32[]{:S(2)}, u32[]{:S(2)}) async-start(bf16[32,4,16,1024]{3,2,1,0:T(8,128)(2,1)} %get-tuple-element.11), calls=%async_computation | async-start | bytes 8388608 | tf_op jit(solution)/shard_map/all_to_all | solution.py:236
  204.2 7.6 %regroup.3 = (bf16[8,256,1024]{2,1,0:T(8,128)(2,1)}, bf16[8,1024,256]{2,1,0:T(8,128)(2,1)}) custom-call(bf16[32,4,16,1024]{3,2,1,0:T(8,128)(2,1)} %all_to_all.10.refs_0_), custom_call_target="tpu_custom_call" | custom-call | bytes 12582912 | tf_op jit(solution)/shard_map/regroup/pallas_call | solution.py:152
  211.8 15.3 %correlate.2.refs_2_ = f32[16,1024,1024]{2,1,0:T(8,128)} custom-call(bf16[8,256,1024]{2,1,0:T(8,128)(2,1)} %get-tuple-element.15.refs_0_, bf16[8,1024,256]{2,1,0:T(8,128)(2,1)} %get-tuple-element.16.refs_1_), custom_call_target="tpu_custom_call" | custom-call | flops 4294967296 | bytes 41943040 | tf_op jit(solution)/shard_map/correlate/pallas_call | solution.py:204
  227.1 71.0 %all-to-all-done.refs_0_ = bf16[32,4,16,1024]{3,2,1,0:T(8,128)(2,1)} async-done(((bf16[32,4,16,1024]{3,2,1,0:T(8,128)(2,1)}), bf16[32,4,16,1024]{3,2,1,0:T(8,128)(2,1)}, u32[]{:S(2)}, u32[]{:S(2)}) %all-to-all-start) | async-done | bytes 4194336 | tf_op jit(solution)/shard_map/all_to_all | solution.py:236
  298.1 7.5 %regroup.2 = (bf16[8,256,1024]{2,1,0:T(8,128)(2,1)}, bf16[8,1024,256]{2,1,0:T(8,128)(2,1)}) custom-call(bf16[32,4,16,1024]{3,2,1,0:T(8,128)(2,1)} %all-to-all-done.refs_0_), custom_call_target="tpu_custom_call" | custom-call | bytes 12582912 | tf_op jit(solution)/shard_map/regroup/pallas_call | solution.py:152
  305.6 15.3 %correlate.3 = f32[16,1024,1024]{2,1,0:T(8,128)} custom-call(bf16[8,256,1024]{2,1,0:T(8,128)(2,1)} %get-tuple-element.12.refs_0_, bf16[8,1024,256]{2,1,0:T(8,128)(2,1)} %get-tuple-element.13.refs_1_, f32[16,1024,1024]{2,1,0:T(8,128)} %correlate.2.refs_2_), custom_call_target="tpu_custom_call", output_to_operand_aliasing={{}: (2, {})} | custom-call | flops 4294967296 | bytes 41943040 | tf_op jit(solution)/shard_map/correlate/pallas_call | solution.py:204
Async XLA Ops:
  3.2 12.1 %collective-permute-start = (bf16[1024,3072]{1,0:T(8,128)(2,1)S(1)}, bf16[1024,3072]{1,0:T(8,128)(2,1)S(1)}, u32[]{:S(2)}, u32[]{:S(2)}) collective-permute-start(bf16[1024,3072]{1,0:T(8,128)(2,1)S(1)} %slice.3), channel_id=1, source_target_pairs={{0,1},{1,2},{2,3},{3,4},{4,5},{5,6},{6,7},{7,8},{8,9},{9,10},{10,1... | collective-permute-start | bytes 18874376 | tf_op jit(solution)/shard_map/ppermute | solution.py:23
  15.4 2.7 copy-start
  200.4 97.7 %all-to-all-start = ((bf16[32,4,16,1024]{3,2,1,0:T(8,128)(2,1)}), bf16[32,4,16,1024]{3,2,1,0:T(8,128)(2,1)}, u32[]{:S(2)}, u32[]{:S(2)}) async-start(bf16[32,4,16,1024]{3,2,1,0:T(8,128)(2,1)} %get-tuple-element.11), calls=%async_computation | async-start | bytes 8388608 | tf_op jit(solution)/shard_map/all_to_all | solution.py:236

commit v2 on v0

--- a/solution.py
+++ b/solution.py
@@ -1,12 +1,21 @@
+import functools
 import math
 
 import jax
 import jax.numpy as jnp
+import ml_dtypes
+import numpy as np
 from jax import lax
+from jax.experimental import pallas as pl
+from jax.experimental.pallas import tpu as pltpu
 from jax.sharding import PartitionSpec as P
 
 CHAN = 512
 TAPS = 4
+VMEM_LIMIT = 56 * 1024 * 1024
+FILTER_ROWS = 32
+LANES = 128
+PITCH = 8
 
 
 def passed_along(block, axis, distance):
@@ -15,15 +24,409 @@
     return lax.ppermute(block, axis, route)
 
 
+def passed_back_round(block, axis):
+    devices = lax.axis_size(axis)
+    return lax.ppermute(block, axis, [(i, (i - 1) % devices) for i in range(devices)])
+
+
 def transform_table(frame_len, channels):
-    sample_index = lax.iota(jnp.int32, frame_len)
-    channel_index = lax.iota(jnp.int32, channels)
-    phase_index = channel_index[:, None] * sample_index[None, :] % frame_len
-    angle_value = phase_index.astype(jnp.float32) * (2.0 * math.pi / frame_len)
-    norm_factor = 1.0 / math.sqrt(frame_len)
-    cos_part = jnp.cos(angle_value) * norm_factor
-    sin_part = -jnp.sin(angle_value) * norm_factor
-    return jnp.concatenate([cos_part, sin_part], 0).astype(jnp.bfloat16)
+    phase = np.arange(channels)[:, None] * np.arange(frame_len)[None, :] % frame_len
+    angle = phase * (2.0 * math.pi / frame_len)
+    rows = np.stack([np.cos(angle), -np.sin(angle)], 1) / math.sqrt(frame_len)
+    return rows.reshape(2 * channels, frame_len).astype(np.float32).astype(ml_dtypes.bfloat16)
+
+
+def cost(flops, moved):
+    return pl.CostEstimate(flops=flops, bytes_accessed=moved, transcendentals=0)
+
+
+def filter_transform_kernel(variants, local, dests, splits, sources, *refs):
+    follows_ref = refs[0]
+    voltage_refs = refs[1 : sources + 1]
+    weights_ref, table_ref = refs[sources + 1 : sources + 3]
+    out_refs = refs[sources + 3 : -1]
+    filtered_ref = refs[-1]
+    count, rows, frame_len = filtered_ref.shape
+
+    def filtered_block(spectra, frame_of):
+        needed = sorted({s - k for s in spectra for k in range(TAPS)})
+        for lane in range(0, frame_len, LANES):
+            weights = [
+                jnp.broadcast_to(weights_ref[k : k + 1, lane : lane + LANES], (FILTER_ROWS, LANES))
+                for k in range(TAPS)
+            ]
+            kept = [w * follows_ref[0] for w in weights] if max(spectra) >= local else weights
+
+            def body(step, carry, lane=lane, weights=weights, kept=kept):
+                at = pl.ds(pl.multiple_of(step * FILTER_ROWS, FILTER_ROWS), FILTER_ROWS)
+                frames = {}
+                for f in needed:
+                    source, place = frame_of[f]
+                    start = place * frame_len + lane
+                    frames[f] = voltage_refs[source][at, start : start + LANES].astype(jnp.float32)
+                for slot, s in enumerate(spectra):
+                    total = weights[0] * frames[s]
+                    for k in range(1, TAPS):
+                        factor = kept[k] if s >= local > s - k else weights[k]
+                        total = total + factor * frames[s - k]
+                    filtered_ref[slot, at, lane : lane + LANES] = total.astype(jnp.bfloat16)
+                return carry
+
+            lax.fori_loop(0, rows // FILTER_ROWS, body, 0, unroll=True)
+
+    for index, variant in enumerate(variants):
+        if len(variants) == 1:
+            filtered_block(*variant)
+        else:
+            pl.when(pl.program_id(0) == index)(
+                functools.partial(filtered_block, *variant)
+            )
+
+    per_dest = table_ref.shape[0] // dests
+    dest_block = max(1, min(dests, 256 // per_dest))
+    height = dest_block * per_dest
+    for slot in range(count):
+        filtered = filtered_ref[slot]
+        for block in range(dests // dest_block):
+            spectrum = lax.dot_general(
+                table_ref[block * height : (block + 1) * height, :],
+                filtered,
+                (((1,), (1,)), ((), ())),
+                preferred_element_type=jnp.float32,
+            )
+            spectrum = spectrum.astype(jnp.bfloat16).reshape(dest_block, per_dest, rows)
+            begin = 0
+            for out_ref, width in zip(out_refs, splits):
+                out_ref[block * dest_block : (block + 1) * dest_block, slot] = spectrum[
+                    :, begin : begin + width, :
+                ]
+                begin += width
+
+
+def filter_transform(
+    arrays, begins, variants, local, follows, weights, table, dests, splits, rows, block, first=0, outs=()
+):
+    frame_len = table.shape[1]
+    count = len(variants[0][0])
+    in_specs = [pl.BlockSpec(memory_space=pltpu.SMEM)]
+    for a, b in zip(arrays, begins):
+        move = 1 if a.shape[0] > block else 0
+        in_specs.append(
+            pl.BlockSpec((block, a.shape[1]), functools.partial(lambda m, b, i: (i * m + b, 0), move, b))
+        )
+    in_specs += [
+        pl.BlockSpec(weights.shape, lambda i: (0, 0)),
+        pl.BlockSpec(table.shape, lambda i: (0, 0)),
+    ]
+    args = [follows, *arrays, weights, table]
+    aliases = {len(args) + i: i for i in range(len(outs))}
+    in_specs += [pl.BlockSpec(memory_space=pl.ANY)] * len(outs)
+    steps = len(variants) if len(variants) > 1 or len(arrays) > 1 else rows // block
+
+    def kernel(*refs):
+        refs = (*refs[: len(args)], *refs[len(args) + len(outs) :])
+        filter_transform_kernel(variants, local, dests, tuple(splits), len(arrays), *refs)
+
+    return pl.pallas_call(
+        kernel,
+        grid=(steps,),
+        in_specs=in_specs,
+        out_specs=[
+            pl.BlockSpec((dests, count, w, block), lambda i: (0, 0, 0, i + first)) for w in splits
+        ],
+        out_shape=[jax.ShapeDtypeStruct((dests, count, w, rows), jnp.bfloat16) for w in splits],
+        scratch_shapes=[pltpu.VMEM((count, block, frame_len), jnp.bfloat16)],
+        input_output_aliases=aliases,
+        compiler_params=pltpu.CompilerParams(vmem_limit_bytes=VMEM_LIMIT),
+        cost_estimate=cost(
+            2 * table.size * steps * block * count,
+            2 * (sum(a.shape[1] for a in arrays) * steps * block + table.size * (1 + count)),
+        ),
+        name="filter_transform",
+    )(*args, *outs)
+
+
+def spread(spectra_refs, rolled, scratch):
+    base = 0
+    tiles = scratch.shape[0]
+    for ref, moves in zip(spectra_refs, rolled):
+        devices, count, rows, _ = ref.shape
+        pitch = rows + PITCH
+        for slot in range(count):
+            for d in range(devices):
+                block = ref[d, slot].astype(jnp.float32)
+                for tile in range(tiles):
+                    move = moves[slot][tile * len(moves[slot]) // tiles]
+                    at = (base + (d + move) % devices) * pitch
+                    scratch[tile, at : at + rows, :] = block[:, tile * LANES : (tile + 1) * LANES]
+            base += devices
+
+
+def spread_shape(arrays, lanes):
+    depth = sum(a.shape[0] * a.shape[1] for a in arrays)
+    return depth, pltpu.VMEM((lanes // LANES, depth * (arrays[0].shape[2] + PITCH), LANES), jnp.float32)
+
+
+def regroup_kernel(rolled, *refs):
+    sources = len(rolled)
+    wide_ref, tall_ref, scratch = refs[sources:]
+    rows = refs[0].shape[2]
+    depth = wide_ref.shape[1] // 2
+    spread(refs[:sources], rolled, scratch)
+    for channel in range(rows // 2):
+        for part in range(2):
+            deep = slice(part * depth, (part + 1) * depth)
+            for tile in range(scratch.shape[0]):
+                across = slice(tile * LANES, (tile + 1) * LANES)
+                values = scratch[tile, pl.ds(2 * channel + part, depth, stride=rows + PITCH), :]
+                wide_ref[channel, deep, across] = values.astype(jnp.bfloat16)
+                tall_ref[channel, across, deep] = values.T.astype(jnp.bfloat16)
+
+
+def regroup(arrays, rolled, inputs, block):
+    rows = arrays[0].shape[2]
+    channels = rows // 2
+    depth, scratch = spread_shape(arrays, block)
+    in_specs = [pl.BlockSpec((*a.shape[:3], block), lambda i: (0, 0, 0, i)) for a in arrays]
+    return pl.pallas_call(
+        functools.partial(regroup_kernel, rolled),
+        grid=(inputs // block,),
+        in_specs=in_specs,
+        out_specs=[
+            pl.BlockSpec((channels, 2 * depth, block), lambda i: (0, 0, i)),
+            pl.BlockSpec((channels, block, 2 * depth), lambda i: (0, i, 0)),
+        ],
+        out_shape=[
+            jax.ShapeDtypeStruct((channels, 2 * depth, inputs), jnp.bfloat16),
+            jax.ShapeDtypeStruct((channels, inputs, 2 * depth), jnp.bfloat16),
+        ],
+        scratch_shapes=[scratch],
+        compiler_params=pltpu.CompilerParams(vmem_limit_bytes=VMEM_LIMIT),
+        cost_estimate=cost(0, 6 * depth * rows * inputs),
+        name="regroup",
+    )(*arrays)
+
+
+def packed_square(scale, block, wide, tall, store):
+    half = wide.shape[0] // 2
+    inputs = wide.shape[1]
+    row_index = lax.broadcasted_iota(jnp.int32, (block, block), 0)
+    col_index = lax.broadcasted_iota(jnp.int32, (block, block), 1)
+    upper = col_index >= row_index
+    for first in range(0, inputs, block):
+        end = first + block
+        re_rows = tall[first:end]
+        im_rows = imaginary_rows(re_rows, half)
+        im = jnp.dot(im_rows, wide[:, :end], preferred_element_type=jnp.float32) * scale
+        re = jnp.dot(re_rows, wide[:, first:], preferred_element_type=jnp.float32) * scale
+        if first:
+            store(first, 0, im[:, :first])
+        store(first, first, jnp.where(upper, re[:, :block], im[:, first:]))
+        if end < inputs:
+            store(first, end, re[:, block:])
+
+
+def imaginary_rows(rows, half):
+    return jnp.concatenate([rows[:, half:], -rows[:, :half]], 1)
+
+
+def correlate_first_kernel(scale, block, wide_ref, tall_ref, out_ref):
+    for channel in range(out_ref.shape[0]):
+
+        def store(row, col, values, channel=channel):
+            height, width = values.shape
+            out_ref[channel, row : row + height, col : col + width] = values
+
+        packed_square(scale, block, wide_ref[channel], tall_ref[channel], store)
+
+
+def correlate_first(wide, tall, block, total, spectra_count):
+    channels, depth, inputs = wide.shape
+    return pl.pallas_call(
+        functools.partial(correlate_first_kernel, 1.0 / spectra_count, block),
+        grid=(channels // 2,),
+        in_specs=[
+            pl.BlockSpec((2, depth, inputs), lambda c: (c, 0, 0)),
+            pl.BlockSpec((2, inputs, depth), lambda c: (c, 0, 0)),
+        ],
+        out_specs=pl.BlockSpec((2, inputs, inputs), lambda c: (c, 0, 0)),
+        out_shape=jax.ShapeDtypeStruct((channels, total, total), jnp.float32),
+        compiler_params=pltpu.CompilerParams(vmem_limit_bytes=VMEM_LIMIT),
+        cost_estimate=cost(
+            2 * channels * depth * inputs * inputs, channels * inputs * (4 * depth + 4 * inputs)
+        ),
+        name="correlate_first",
+    )(wide, tall)
+
+
+def correlate_rest_kernel(scale, block, first_channel, rolled, *refs):
+    sources = len(rolled)
+    wide_ref, tall_ref = refs[:2]
+    spectra_refs = refs[2 : 2 + sources]
+    out_ref, scratch, right, below, sems = refs[3 + sources :]
+    rows = spectra_refs[0].shape[2]
+    depth = wide_ref.shape[1] // 2
+    before = wide_ref.shape[2]
+    step = pl.program_id(0)
+    slot = step % 2
+
+    @pl.when(step == 0)
+    def _():
+        spread(spectra_refs, rolled, scratch)
+
+    def copies(slot, channel):
+        return (
+            pltpu.make_async_copy(
+                right.at[slot], out_ref.at[channel, pl.ds(0, before), pl.ds(before, right.shape[2])], sems.at[slot, 0]
+            ),
+            pltpu.make_async_copy(
+                below.at[slot], out_ref.at[channel, pl.ds(before, below.shape[1]), :], sems.at[slot, 1]
+            ),
+        )
+
+    @pl.when(step >= 2)
+    def _():
+        for copy in copies(slot, first_channel + step - 2):
+            copy.wait()
+
+    parts = [
+        [
+            scratch[tile, pl.ds(2 * step + part, depth, stride=rows + PITCH), :]
+            for tile in range(scratch.shape[0])
+        ]
+        for part in range(2)
+    ]
+    wide = jnp.concatenate([jnp.concatenate(p, 1) for p in parts], 0).astype(jnp.bfloat16)
+    tall = jnp.concatenate([jnp.concatenate([t.T for t in p], 0) for p in parts], 1).astype(jnp.bfloat16)
+
+    right[slot] = jnp.dot(tall_ref[0], wide, preferred_element_type=jnp.float32) * scale
+    im_rows = imaginary_rows(tall, depth)
+    below[slot, :, :before] = jnp.dot(im_rows, wide_ref[0], preferred_element_type=jnp.float32) * scale
+
+    def store(row, col, values):
+        height, width = values.shape
+        below[slot, row : row + height, before + col : before + col + width] = values
+
+    packed_square(scale, block, wide, tall, store)
+    for copy in copies(slot, first_channel + step):
+        copy.start()
+
+    @pl.when(step == pl.num_programs(0) - 1)
+    def _():
+        for copy in copies(1 - slot, first_channel + step - 1):
+            copy.wait()
+        for copy in copies(slot, first_channel + step):
+            copy.wait()
+
+
+def correlate_rest(wide, tall, arrays, pieces, rolled, block, first_channel, spectra_count, out):
+    _, double, before = wide.shape
+    rows, inputs = arrays[-1].shape[2:]
+    channels = rows // 2
+    shapes = [(*a.shape[:2], rows) for a in arrays]
+    in_specs = [
+        pl.BlockSpec((1, double, before), lambda c: (c + first_channel, 0, 0)),
+        pl.BlockSpec((1, before, double), lambda c: (c + first_channel, 0, 0)),
+    ]
+    in_specs += [
+        pl.BlockSpec((*shape, inputs), functools.partial(lambda p, c: (0, 0, p, 0), p))
+        for shape, p in zip(shapes, pieces)
+    ]
+    in_specs.append(pl.BlockSpec(memory_space=pl.ANY))
+    scratch = pltpu.VMEM((inputs // LANES, double // 2 * (rows + PITCH), LANES), jnp.float32)
+    return pl.pallas_call(
+        functools.partial(correlate_rest_kernel, 1.0 / spectra_count, block, first_channel, rolled),
+        grid=(channels,),
+        in_specs=in_specs,
+        out_specs=pl.BlockSpec(memory_space=pl.ANY),
+        out_shape=jax.ShapeDtypeStruct(out.shape, out.dtype),
+        scratch_shapes=[
+            scratch,
+            pltpu.VMEM((2, before, inputs), jnp.float32),
+            pltpu.VMEM((2, inputs, before + inputs), jnp.float32),
+            pltpu.SemaphoreType.DMA((2, 2)),
+        ],
+        input_output_aliases={2 + len(arrays): 0},
+        compiler_params=pltpu.CompilerParams(vmem_limit_bytes=VMEM_LIMIT),
+        cost_estimate=cost(
+            2 * channels * double * inputs * (2 * before + inputs),
+            channels * inputs * (4 * double + 8 * before + 4 * inputs),
+        ),
+        name="correlate_rest",
+    )(wide, tall, *arrays, out)
+
+
+def turn(block):
+    return lax.all_to_all(block, "chan", split_axis=0, concat_axis=0, tiled=True)
+
+
+def after(value, earlier):
+    return lax.optimization_barrier((value, earlier))[0]
+
+
+def per_device(voltage, tap_weights):
+    frame_len = 2 * CHAN
+    inputs, samples = voltage.shape
+    local = samples // frame_len
+    devices = lax.axis_size("chan")
+    channels = CHAN // devices
+    count = devices * local
+    table = jnp.asarray(transform_table(frame_len, CHAN))
+    past = TAPS - 1
+    blocks = 4
+    block = inputs // blocks
+    later = [1, 1, 2, 2]
+    follows = jnp.where(lax.axis_index("chan") == devices - 1, 0.0, 1.0).astype(jnp.float32)[None]
+    own = {f: (0, f) for f in range(local)}
+    inner = [(tuple(range(past, local)), own)]
+    groups = [0], [1, 2, 3]
+    rolled = [
+        (((0,),) * (local - past), ((0,), tuple(int(later[b] == 2) for b in some), (0,)))
+        for some in groups
+    ]
+
+    def around(voltage, some):
+        ahead, back, variants = [], [], []
+        for b in some:
+            rows = voltage[b * block : (b + 1) * block]
+            frame_of = dict(own)
+            for f in range(later[b] - past, 0):
+                frame_of[f] = (1, len(ahead))
+                ahead.append(rows[:, (local + f) * frame_len : (local + f + 1) * frame_len])
+            for f in range(later[b]):
+                frame_of[local + f] = (2, len(back))
+                back.append(rows[:, f * frame_len : (f + 1) * frame_len])
+            made = tuple(s + local if s < later[b] else s for s in range(past))
+            variants.append((made, frame_of))
+        return (jnp.concatenate(ahead, 1), jnp.concatenate(back, 1)), variants
+
+    def neighbours(ahead, back):
+        return passed_along(ahead, "chan", 1), passed_back_round(back, "chan")
+
+    def spectra(arrays, begins, variants, splits, rows, *into):
+        return filter_transform(
+            arrays, begins, variants, local, follows, tap_weights, table, devices, splits, rows, block, *into
+        )
+
+    whole, halves = [2 * channels], [channels, channels]
+    first_sent, first_variants = around(voltage, groups[0])
+    first_around = neighbours(*first_sent)
+    second_sent, second_variants = around(after(voltage, first_sent), groups[1])
+    second_around = neighbours(*after(second_sent, first_around))
+    inner_turned = turn(after(spectra([voltage], [0], inner, whole, inputs)[0], first_around))
+    first = spectra([voltage, *first_around], [0, 0, 0], first_variants, whole, block)[0]
+    turned = turn(after(first, (inner_turned, second_around)))
+    parts = spectra([voltage, *second_around], [1, 0, 0], second_variants, halves, inputs - block)
+    wide, tall = regroup([inner_turned, turned], rolled[0], block, block)
+    result = correlate_first(wide, tall, block, inputs, count)
+    inner_rest = inner_turned[..., block:]
+    for piece, part in enumerate(parts):
+        turned = turn(after(part, turned))
+        result = correlate_rest(
+            wide, tall, [inner_rest, turned], [piece, 0], rolled[1], block,
+            piece * channels // 2, count, result,
+        )
+    return result
 
 
 def stack_operands(turned):
@@ -36,7 +439,7 @@
     return jnp.einsum("pcik,cjk->pcij", left_rows, right_cols, preferred_element_type=jnp.float32)
 
 
-def per_device(voltage, tap_weights):
+def per_device_tiled(voltage, tap_weights):
     frame_len = 2 * CHAN
     local_inputs, samples = voltage.shape
     spec_local = samples // frame_len
@@ -50,7 +453,8 @@
         shifted = extended[:, TAPS - 1 - tap_index : TAPS - 1 - tap_index + spec_local, :]
         filtered = filtered + tap_weights[tap_index][None, None, :] * shifted.astype(jnp.float32)
     filtered = filtered.astype(jnp.bfloat16).reshape(local_inputs * spec_local, frame_len)
-    dft_table = transform_table(frame_len, CHAN)
+    dft_table = jnp.asarray(transform_table(frame_len, CHAN)).reshape(CHAN, 2, frame_len)
+    dft_table = dft_table.swapaxes(0, 1).reshape(2 * CHAN, frame_len)
     spectra = lax.dot_general(
         dft_table, filtered, (((1,), (1,)), ((), ())), preferred_element_type=jnp.float32
     )
@@ -76,6 +480,7 @@
 def solution(mesh):
     in_specs = (P("tile", "chan"), P())
     out_specs = P("chan", "tile", None)
+    body = per_device if mesh.shape["tile"] == 1 else per_device_tiled
     return jax.shard_map(
-        per_device, mesh=mesh, in_specs=in_specs, out_specs=out_specs, check_vma=False
+        body, mesh=mesh, in_specs=in_specs, out_specs=out_specs, check_vma=False
     )

time: 638 us -> 283 us (0.44)
  local copies, waits for them, and re-layouts: 193 us -> 8.17 us
  other arithmetic: 115 us -> 0.4 us
  waiting for transfers between devices: 186 us -> 97 us
  matrix products: 69.4 us -> 0 us
  Pallas kernels: 0 us -> 68.9 us
  blocking collectives: 0 us -> 59.6 us
  starting transfers between devices: 70.7 us -> 47.5 us
    all_to_all x1 -> x3, waiting for transfers between devices: 186 us -> 50.8 us  [turn(): lax.all_to_all(block, 'chan', split_axis=0, concat_axis=0, tiled=True)]
    dot_general x2 -> x0, matrix products: 69.4 us -> none  [the longest x1 54.1 us: pair_products(): jnp.einsum('pcik,cjk->pcij', left_rows, right_cols, preferred_element_typ...]
    pallas_call x0 -> x7, Pallas kernels: none -> 68.9 us  [the longest x3 28.3 us: filter_transform(): pl.pallas_call(kernel, grid=(steps,), in_specs=in_specs, out_specs=[pl.Bl...]
    select_n x1 -> x0, other arithmetic: 64.3 us -> none  [per_device(): packed = jnp.where((col_index >= row_index)[None], products[0], products[1])]
    select_n x1 -> x0, local copies, waits for them, and re-layouts: 62.8 us -> none  [per_device(): packed = jnp.where((col_index >= row_index)[None], products[0], products[1])]
    all_to_all x0 -> x1, blocking collectives: none -> 59.6 us  [turn(): lax.all_to_all(block, 'chan', split_axis=0, concat_axis=0, tiled=True)]
    reshape x3 -> x0, local copies, waits for them, and re-layouts: 49.4 us -> none  [the longest x2 36.8 us: per_device(): spectra.astype(jnp.bfloat16).reshape(2, CHAN, local_inputs, spec_local)]
    ppermute x0 -> x2, waiting for transfers between devices: none -> 46.2 us  [passed_back_round(): lax.ppermute(block, axis, [(i, (i - 1) % devices) for i in range(devices)])]
  transfers between devices with their start and end apart: 2 -> 7, of which waited for: 2 -> 3; matrix products, arithmetic and copies ran while one was open for 2% -> 2% of each run, Pallas kernels for 0% -> 19%
where the time goes in v2:
time: 283 us; the launch traced here: 282 us
  waiting for transfers between devices  97 us (34%)
  Pallas kernels  68.9 us (24%)
  blocking collectives  59.6 us (21%)
  starting transfers between devices  47.5 us (17%)
  local copies, waits for them, and re-layouts  8.17 us (3%)
    all_to_all x1, blocking collectives, turn(): lax.all_to_all(block, 'chan', split_axis=0, concat_axis=0, tiled=True)  59.6 us
    all_to_all x3, waiting for transfers between devices, turn(): lax.all_to_all(block, 'chan', split_axis=0, concat_axis=0, tiled=True)  50.8 us
    ppermute x2, waiting for transfers between devices, passed_back_round(): lax.ppermute(block, axis, [(i, (i - 1) % devices) for i in range(devices)])  46.2 us
    all_to_all x3, starting transfers between devices, turn(): lax.all_to_all(block, 'chan', split_axis=0, concat_axis=0, tiled=True)  31.8 us
    pallas_call x3, Pallas kernels, filter_transform(): pl.pallas_call(kernel, grid=(steps,), in_specs=in_specs, out_specs=[pl.Bl...  28.3 us
    pallas_call x2, Pallas kernels, correlate_rest(): pl.pallas_call(functools.partial(correlate_rest_kernel, 1.0 / spectra_cou...  28.3 us
    ppermute x2, starting transfers between devices, passed_back_round(): lax.ppermute(block, axis, [(i, (i - 1) % devices) for i in range(devices)])  10.6 us
    pallas_call x1, Pallas kernels, correlate_first(): pl.pallas_call(functools.partial(correlate_first_kernel, 1.0 / spectra_co...  7.44 us
  transfers between devices with their start and end apart: 7, of which 3 were waited for; matrix products, arithmetic and copies ran while one was open for 2% of the time, Pallas kernels for 19%

profile of v2, /device:TPU:0, one launch (start us, length us, event | category | flops | bytes accessed | tf_op | source)
XLA Modules:
  0.0 281.8 jit_solution(18137654724990694134)
XLA Ops:
  0.0 1.3 concatenate.11
  1.3 2.4 collective-permute-start
  3.7 1.1 slice.49
  4.8 5.3 %collective-permute-start.1 = (bf16[256,1024]{1,0:T(8,128)(2,1)S(1)}, bf16[256,1024]{1,0:T(8,128)(2,1)S(1)}, u32[]{:S(2)}, u32[]{:S(2)}) collective-permute-start(bf16[256,1024]{1,0:T(8,128)(2,1)S(1)} %slice.49), channel_id=1, source_target_pairs={{0,31},{1,0},{2,1},{3,2},{4,3},{5,4},{6,5},{7,6},{8,7},{9,8},{10,9... | collective-permute-start | bytes 1572872 | tf_op jit(solution)/shard_map/ppermute | solution.py:29
  10.1 8.2 %filter_transform.3 = bf16[32,1,32,1024]{3,2,1,0:T(8,128)(2,1)} custom-call(f32[1]{0:T(128)} %bitcast.refs_0_, bf16[1024,4096]{1,0:T(8,128)(2,1)} %refs_1_.5, f32[4,1024]{1,0:T(4,128)} %refs_4_.3, bf16[1024,1024]{1,0:T(8,128)(2,1)} %constant.12.clone.refs_3_.refs_5_), custom_call_target="tpu_custom_call" | custom-call | flops 2147483648 | bytes 12582912 | tf_op jit(solution)/shard_map/filter_transform/pallas_call | solution.py:130
  18.3 0.0 collective-permute-done.1.refs_3_
  18.3 0.0 copy-start.2
  18.3 0.0 collective-permute-done.refs_2_
  18.3 0.0 copy-start.1
  18.3 0.8 copy-done.2
  19.1 11.7 %all-to-all-start = ((bf16[32,1,32,1024]{3,2,1,0:T(8,128)(2,1)}), bf16[32,1,32,1024]{3,2,1,0:T(8,128)(2,1)S(1)}, u32[]{:S(2)}, u32[]{:S(2)}) async-start(bf16[32,1,32,1024]{3,2,1,0:T(8,128)(2,1)} %filter_transform.3), calls=%async_computation | async-start | bytes 4194304 | tf_op jit(solution)/shard_map/all_to_all | solution.py:360
  30.8 2.1 fusion.1
  32.9 0.0 copy-done.1
  33.0 1.5 fusion
  34.4 0.2 pad_maximum_fusion.1
  34.6 0.2 pad_maximum_fusion
  34.9 5.3 %collective-permute-start.3 = (bf16[256,5120]{1,0:T(8,128)(2,1)S(1)}, bf16[256,5120]{1,0:T(8,128)(2,1)}, u32[]{:S(2)}, u32[]{:S(2)}) collective-permute-start(bf16[256,5120]{1,0:T(8,128)(2,1)S(1)} %pad_maximum_fusion), channel_id=1, source_target_pairs={{0,31},{1,0},{2,1},{3,2},{4,3},{5,4},{6,5},{7,6},{8,7},{9,8},{10,9... | collective-permute-start | bytes 7864328 | tf_op jit(solution)/shard_map/ppermute | solution.py:29
  40.1 2.6 collective-permute-start.2
  42.8 6.5 %filter_transform.4 = bf16[32,3,32,256]{3,2,1,0:T(8,128)(2,1)} custom-call(f32[1]{0:T(128)} %bitcast.refs_0_, bf16[1024,4096]{1,0:T(8,128)(2,1)} %refs_1_.5, bf16[256,2048]{1,0:T(8,128)(2,1)} %copy-done.1, bf16[256,1024]{1,0:T(8,128)(2,1)} %copy-done.2, f32[4,1024]{1,0:T(4,128)} %refs_4_.3, bf16[1024,1024]{1,0:T(8,128)(2,1)} %constant.12.clone.refs_3_.refs_5_), custom_call_target="tpu_custom_call" | custom-call | flops 1610612736 | bytes 12058624 | tf_op jit(solution)/shard_map/filter_transform/pallas_call | solution.py:130
  49.3 0.0 collective-permute-done.2.refs_2_
  49.3 46.2 %collective-permute-done.3.refs_3_ = bf16[256,5120]{1,0:T(8,128)(2,1)} collective-permute-done((bf16[256,5120]{1,0:T(8,128)(2,1)S(1)}, bf16[256,5120]{1,0:T(8,128)(2,1)}, u32[]{:S(2)}, u32[]{:S(2)}) %collective-permute-start.3) | collective-permute-done | bytes 2621472 | tf_op jit(solution)/shard_map/ppermute | solution.py:29
  95.5 0.0 all-to-all-done.refs_0_
  95.5 0.0 copy-start
  95.5 16.5 %all-to-all-start.1 = ((bf16[32,3,32,256]{3,2,1,0:T(8,128)(2,1)}), bf16[32,3,32,256]{3,2,1,0:T(8,128)(2,1)}, u32[]{:S(2)}, u32[]{:S(2)}) async-start(bf16[32,3,32,256]{3,2,1,0:T(8,128)(2,1)} %filter_transform.4), calls=%async_computation.1 | async-start | bytes 3145728 | tf_op jit(solution)/shard_map/all_to_all | solution.py:360
  112.0 13.6 %filter_transform.5 = (bf16[32,3,16,768]{3,2,1,0:T(8,128)(2,1)}, bf16[32,3,16,768]{3,2,1,0:T(8,128)(2,1)}) custom-call(f32[1]{0:T(128)} %bitcast.refs_0_, bf16[1024,4096]{1,0:T(8,128)(2,1)} %refs_1_.5, bf16[256,4096]{1,0:T(8,128)(2,1)} %collective-permute-done.2.refs_2_, bf16[256,5120]{1,0:T(8,128)(2,1)} %collective-permute-done.3.refs_3_, ...), custom_call_target="tpu_custom_call" | custom-call | flops 4831838208 | bytes 28835840 | tf_op jit(solution)/shard_map/filter_transform/pallas_call | solution.py:130
  125.6 24.1 %all-to-all-done.1.refs_1_ = bf16[32,3,32,256]{3,2,1,0:T(8,128)(2,1)} async-done(((bf16[32,3,32,256]{3,2,1,0:T(8,128)(2,1)}), bf16[32,3,32,256]{3,2,1,0:T(8,128)(2,1)}, u32[]{:S(2)}, u32[]{:S(2)}) %all-to-all-start.1) | async-done | bytes 1572896 | tf_op jit(solution)/shard_map/all_to_all | solution.py:360
  149.7 59.6 %all_to_all.20.refs_3_ = bf16[32,3,16,768]{3,2,1,0:T(8,128)(2,1)} all-to-all(bf16[32,3,16,768]{3,2,1,0:T(8,128)(2,1)} %get-tuple-element.25), channel_id=1, replica_groups=mesh['chan'=32,'tile'=1] {'chan'}, dimensions={0} | all-to-all | bytes 4718592 | tf_op jit(solution)/shard_map/all_to_all | solution.py:360
  209.3 3.7 %all-to-all-start.3 = ((bf16[32,3,16,768]{3,2,1,0:T(8,128)(2,1)}), bf16[32,3,16,768]{3,2,1,0:T(8,128)(2,1)}, u32[]{:S(2)}, u32[]{:S(2)}) async-start(bf16[32,3,16,768]{3,2,1,0:T(8,128)(2,1)} %get-tuple-element.26), calls=%async_computation.3 | async-start | bytes 4718592 | tf_op jit(solution)/shard_map/all_to_all | solution.py:360
  213.0 0.0 copy-done
  213.0 1.4 slice.57.refs_2_
  214.4 4.9 %regroup.1 = (bf16[16,256,256]{2,1,0:T(8,128)(2,1)}, bf16[16,256,256]{2,1,0:T(8,128)(2,1)}) custom-call(bf16[32,1,32,1024]{3,2,1,0:T(8,128)(2,1)} %copy-done, bf16[32,3,32,256]{3,2,1,0:T(8,128)(2,1)} %all-to-all-done.1.refs_1_), custom_call_target="tpu_custom_call" | custom-call | bytes 6291456 | tf_op jit(solution)/shard_map/regroup/pallas_call | solution.py:191
  219.3 7.4 %correlate_first.1.refs_4_ = f32[16,1024,1024]{2,1,0:T(8,128)} custom-call(bf16[16,256,256]{2,1,0:T(8,128)(2,1)} %get-tuple-element.21.wide_ref.refs_0_, bf16[16,256,256]{2,1,0:T(8,128)(2,1)} %get-tuple-element.22.tall_ref.refs_1_), custom_call_target="tpu_custom_call" | custom-call | flops 536870912 | bytes 8388608 | tf_op jit(solution)/shard_map/correlate_first/pallas_call | solution.py:245
  226.7 14.1 %correlate_rest.2.refs_4_ = f32[16,1024,1024]{2,1,0:T(8,128)} custom-call(bf16[16,256,256]{2,1,0:T(8,128)(2,1)} %get-tuple-element.21.wide_ref.refs_0_, bf16[16,256,256]{2,1,0:T(8,128)(2,1)} %get-tuple-element.22.tall_ref.refs_1_, bf16[32,1,32,768]{3,2,1,0:T(8,128)(2,1)} %slice.57.refs_2_, ...), custom_call_target="tpu_custom_call", output_to_operand_aliasing={{}: (4, {})} | custom-call | flops 4026531840 | bytes 37748736 | tf_op jit(solution)/shard_map/correlate_rest/pallas_call | solution.py:337
  240.8 26.7 %all-to-all-done.3.refs_3_ = bf16[32,3,16,768]{3,2,1,0:T(8,128)(2,1)} async-done(((bf16[32,3,16,768]{3,2,1,0:T(8,128)(2,1)}), bf16[32,3,16,768]{3,2,1,0:T(8,128)(2,1)}, u32[]{:S(2)}, u32[]{:S(2)}) %all-to-all-start.3) | async-done | bytes 2359328 | tf_op jit(solution)/shard_map/all_to_all | solution.py:360
  267.5 14.1 %correlate_rest.3 = f32[16,1024,1024]{2,1,0:T(8,128)} custom-call(bf16[16,256,256]{2,1,0:T(8,128)(2,1)} %get-tuple-element.21.wide_ref.refs_0_, bf16[16,256,256]{2,1,0:T(8,128)(2,1)} %get-tuple-element.22.tall_ref.refs_1_, bf16[32,1,32,768]{3,2,1,0:T(8,128)(2,1)} %slice.57.refs_2_, ...), custom_call_target="tpu_custom_call", output_to_operand_aliasing={{}: (4, {})} | custom-call | flops 4026531840 | bytes 37748736 | tf_op jit(solution)/shard_map/correlate_rest/pallas_call | solution.py:337
Async XLA Ops:
  1.3 17.0 %collective-permute-start = (bf16[256,2048]{1,0:T(8,128)(2,1)S(1)}, bf16[256,2048]{1,0:T(8,128)(2,1)S(1)}, u32[]{:S(2)}, u32[]{:S(2)}) collective-permute-start(bf16[256,2048]{1,0:T(8,128)(2,1)S(1)} %concatenate.11), channel_id=1, source_target_pairs={{0,1},{1,2},{2,3},{3,4},{4,5},{5,6},{6,7},{7,8},{8,9},{9,10},{10,1... | collective-permute-start | bytes 3145736 | tf_op jit(solution)/shard_map/ppermute | solution.py:24
  4.8 13.5 %collective-permute-start.1 = (bf16[256,1024]{1,0:T(8,128)(2,1)S(1)}, bf16[256,1024]{1,0:T(8,128)(2,1)S(1)}, u32[]{:S(2)}, u32[]{:S(2)}) collective-permute-start(bf16[256,1024]{1,0:T(8,128)(2,1)S(1)} %slice.49), channel_id=1, source_target_pairs={{0,31},{1,0},{2,1},{3,2},{4,3},{5,4},{6,5},{7,6},{8,7},{9,8},{10,9... | collective-permute-start | bytes 1572872 | tf_op jit(solution)/shard_map/ppermute | solution.py:29
  18.3 0.8 copy-start.2
  18.3 14.6 %copy-start.1 = (bf16[256,2048]{1,0:T(8,128)(2,1)}, bf16[256,2048]{1,0:T(8,128)(2,1)S(1)}, u32[]{:S(2)}) copy-start(bf16[256,2048]{1,0:T(8,128)(2,1)S(1)} %collective-permute-done.refs_2_) | copy-start | bytes 3145732
  19.1 76.4 %all-to-all-start = ((bf16[32,1,32,1024]{3,2,1,0:T(8,128)(2,1)}), bf16[32,1,32,1024]{3,2,1,0:T(8,128)(2,1)S(1)}, u32[]{:S(2)}, u32[]{:S(2)}) async-start(bf16[32,1,32,1024]{3,2,1,0:T(8,128)(2,1)} %filter_transform.3), calls=%async_computation | async-start | bytes 4194304 | tf_op jit(solution)/shard_map/all_to_all | solution.py:360
  34.9 60.6 %collective-permute-start.3 = (bf16[256,5120]{1,0:T(8,128)(2,1)S(1)}, bf16[256,5120]{1,0:T(8,128)(2,1)}, u32[]{:S(2)}, u32[]{:S(2)}) collective-permute-start(bf16[256,5120]{1,0:T(8,128)(2,1)S(1)} %pad_maximum_fusion), channel_id=1, source_target_pairs={{0,31},{1,0},{2,1},{3,2},{4,3},{5,4},{6,5},{7,6},{8,7},{9,8},{10,9... | collective-permute-start | bytes 7864328 | tf_op jit(solution)/shard_map/ppermute | solution.py:29
  40.1 9.2 %collective-permute-start.2 = (bf16[256,4096]{1,0:T(8,128)(2,1)S(1)}, bf16[256,4096]{1,0:T(8,128)(2,1)}, u32[]{:S(2)}, u32[]{:S(2)}) collective-permute-start(bf16[256,4096]{1,0:T(8,128)(2,1)S(1)} %pad_maximum_fusion.1), channel_id=1, source_target_pairs={{0,1},{1,2},{2,3},{3,4},{4,5},{5,6},{6,7},{7,8},{8,9},{9,10},{10,1... | collective-permute-start | bytes 6291464 | tf_op jit(solution)/shard_map/ppermute | solution.py:24
  95.5 117.5 %copy-start = (bf16[32,1,32,1024]{3,2,1,0:T(8,128)(2,1)}, bf16[32,1,32,1024]{3,2,1,0:T(8,128)(2,1)S(1)}, u32[]{:S(2)}) copy-start(bf16[32,1,32,1024]{3,2,1,0:T(8,128)(2,1)S(1)} %all-to-all-done.refs_0_) | copy-start | bytes 6291460
  95.5 54.2 %all-to-all-start.1 = ((bf16[32,3,32,256]{3,2,1,0:T(8,128)(2,1)}), bf16[32,3,32,256]{3,2,1,0:T(8,128)(2,1)}, u32[]{:S(2)}, u32[]{:S(2)}) async-start(bf16[32,3,32,256]{3,2,1,0:T(8,128)(2,1)} %filter_transform.4), calls=%async_computation.1 | async-start | bytes 3145728 | tf_op jit(solution)/shard_map/all_to_all | solution.py:360
  209.3 58.2 %all-to-all-start.3 = ((bf16[32,3,16,768]{3,2,1,0:T(8,128)(2,1)}), bf16[32,3,16,768]{3,2,1,0:T(8,128)(2,1)}, u32[]{:S(2)}, u32[]{:S(2)}) async-start(bf16[32,3,16,768]{3,2,1,0:T(8,128)(2,1)} %get-tuple-element.26), calls=%async_computation.3 | async-start | bytes 4718592 | tf_op jit(solution)/shard_map/all_to_all | solution.py:360

commit v3 on v2

--- a/solution.py
+++ b/solution.py
@@ -16,6 +16,7 @@
 FILTER_ROWS = 32
 LANES = 128
 PITCH = 8
+PLANE = 8
 
 
 def passed_along(block, axis, distance):
@@ -40,11 +41,11 @@
     return pl.CostEstimate(flops=flops, bytes_accessed=moved, transcendentals=0)
 
 
-def filter_transform_kernel(variants, local, dests, splits, sources, *refs):
-    follows_ref = refs[0]
-    voltage_refs = refs[1 : sources + 1]
-    weights_ref, table_ref = refs[sources + 1 : sources + 3]
-    out_refs = refs[sources + 3 : -1]
+def filter_transform_kernel(variants, local, dests, splits, planes, sources, *refs):
+    follows_ref, place_ref = refs[:2]
+    voltage_refs = refs[2 : sources + 2]
+    weights_ref, table_ref = refs[sources + 2 : sources + 4]
+    out_refs = refs[sources + 4 : -1]
     filtered_ref = refs[-1]
     count, rows, frame_len = filtered_ref.shape
 
@@ -83,18 +84,25 @@
             )
 
     per_dest = table_ref.shape[0] // dests
-    dest_block = max(1, min(dests, 256 // per_dest))
+    dest_block = dests // planes if planes else max(1, min(dests, 256 // per_dest))
     height = dest_block * per_dest
     for slot in range(count):
         filtered = filtered_ref[slot]
         for block in range(dests // dest_block):
+            start = block * height
+            if planes:
+                start = pl.multiple_of((block ^ place_ref[0]) * height, height)
             spectrum = lax.dot_general(
-                table_ref[block * height : (block + 1) * height, :],
+                table_ref[pl.ds(start, height), :],
                 filtered,
                 (((1,), (1,)), ((), ())),
                 preferred_element_type=jnp.float32,
             )
             spectrum = spectrum.astype(jnp.bfloat16).reshape(dest_block, per_dest, rows)
+            if planes:
+                for dest in range(dest_block):
+                    out_refs[block][dest ^ place_ref[1], slot] = spectrum[dest]
+                continue
             begin = 0
             for out_ref, width in zip(out_refs, splits):
                 out_ref[block * dest_block : (block + 1) * dest_block, slot] = spectrum[
@@ -104,46 +112,43 @@
 
 
 def filter_transform(
-    arrays, begins, variants, local, follows, weights, table, dests, splits, rows, block, first=0, outs=()
+    arrays, begins, variants, local, follows, place, weights, table, dests, splits, planes, rows, block
 ):
     frame_len = table.shape[1]
     count = len(variants[0][0])
-    in_specs = [pl.BlockSpec(memory_space=pltpu.SMEM)]
-    for a, b in zip(arrays, begins):
+    per_dest = table.shape[0] // dests
+    in_specs = [pl.BlockSpec(memory_space=pltpu.SMEM)] * 2
+    for source, (a, b) in enumerate(zip(arrays, begins)):
         move = 1 if a.shape[0] > block else 0
+        used = [at for _, frame_of in variants for of, at in frame_of.values() if of == source]
+        width = (max(used) + 1) * frame_len
         in_specs.append(
-            pl.BlockSpec((block, a.shape[1]), functools.partial(lambda m, b, i: (i * m + b, 0), move, b))
+            pl.BlockSpec((block, width), functools.partial(lambda m, b, i: (i * m + b, 0), move, b))
         )
     in_specs += [
         pl.BlockSpec(weights.shape, lambda i: (0, 0)),
         pl.BlockSpec(table.shape, lambda i: (0, 0)),
     ]
-    args = [follows, *arrays, weights, table]
-    aliases = {len(args) + i: i for i in range(len(outs))}
-    in_specs += [pl.BlockSpec(memory_space=pl.ANY)] * len(outs)
-    steps = len(variants) if len(variants) > 1 or len(arrays) > 1 else rows // block
-
-    def kernel(*refs):
-        refs = (*refs[: len(args)], *refs[len(args) + len(outs) :])
-        filter_transform_kernel(variants, local, dests, tuple(splits), len(arrays), *refs)
-
+    if planes:
+        shapes = [(dests // planes, count, per_dest)] * planes
+    else:
+        shapes = [(dests, count, w) for w in splits]
     return pl.pallas_call(
-        kernel,
-        grid=(steps,),
+        functools.partial(
+            filter_transform_kernel, variants, local, dests, tuple(splits), planes, len(arrays)
+        ),
+        grid=(rows // block,),
         in_specs=in_specs,
-        out_specs=[
-            pl.BlockSpec((dests, count, w, block), lambda i: (0, 0, 0, i + first)) for w in splits
-        ],
-        out_shape=[jax.ShapeDtypeStruct((dests, count, w, rows), jnp.bfloat16) for w in splits],
+        out_specs=[pl.BlockSpec((*shape, block), lambda i: (0, 0, 0, i)) for shape in shapes],
+        out_shape=[jax.ShapeDtypeStruct((*shape, rows), jnp.bfloat16) for shape in shapes],
         scratch_shapes=[pltpu.VMEM((count, block, frame_len), jnp.bfloat16)],
-        input_output_aliases=aliases,
         compiler_params=pltpu.CompilerParams(vmem_limit_bytes=VMEM_LIMIT),
         cost_estimate=cost(
-            2 * table.size * steps * block * count,
-            2 * (sum(a.shape[1] for a in arrays) * steps * block + table.size * (1 + count)),
+            2 * table.size * rows * count,
+            2 * (sum(a.shape[1] for a in arrays) * rows + table.size * (1 + count)),
         ),
         name="filter_transform",
-    )(*args, *outs)
+    )(follows, place, *arrays, weights, table)
 
 
 def spread(spectra_refs, rolled, scratch):
@@ -183,11 +188,14 @@
                 tall_ref[channel, across, deep] = values.T.astype(jnp.bfloat16)
 
 
-def regroup(arrays, rolled, inputs, block):
+def regroup(arrays, begins, rolled, inputs, block):
     rows = arrays[0].shape[2]
     channels = rows // 2
     depth, scratch = spread_shape(arrays, block)
-    in_specs = [pl.BlockSpec((*a.shape[:3], block), lambda i: (0, 0, 0, i)) for a in arrays]
+    in_specs = [
+        pl.BlockSpec((*a.shape[:3], block), functools.partial(lambda b, i: (0, 0, 0, i + b), b))
+        for a, b in zip(arrays, begins)
+    ]
     return pl.pallas_call(
         functools.partial(regroup_kernel, rolled),
         grid=(inputs // block,),
@@ -230,7 +238,7 @@
     return jnp.concatenate([rows[:, half:], -rows[:, :half]], 1)
 
 
-def correlate_first_kernel(scale, block, wide_ref, tall_ref, out_ref):
+def correlate_last_kernel(scale, block, wide_ref, tall_ref, out_ref):
     for channel in range(out_ref.shape[0]):
 
         def store(row, col, values, channel=channel):
@@ -240,22 +248,22 @@
         packed_square(scale, block, wide_ref[channel], tall_ref[channel], store)
 
 
-def correlate_first(wide, tall, block, total, spectra_count):
+def correlate_last(wide, tall, block, total, spectra_count):
     channels, depth, inputs = wide.shape
     return pl.pallas_call(
-        functools.partial(correlate_first_kernel, 1.0 / spectra_count, block),
+        functools.partial(correlate_last_kernel, 1.0 / spectra_count, block),
         grid=(channels // 2,),
         in_specs=[
             pl.BlockSpec((2, depth, inputs), lambda c: (c, 0, 0)),
             pl.BlockSpec((2, inputs, depth), lambda c: (c, 0, 0)),
         ],
-        out_specs=pl.BlockSpec((2, inputs, inputs), lambda c: (c, 0, 0)),
+        out_specs=pl.BlockSpec((2, inputs, inputs), lambda c: (c, total // inputs - 1, total // inputs - 1)),
         out_shape=jax.ShapeDtypeStruct((channels, total, total), jnp.float32),
         compiler_params=pltpu.CompilerParams(vmem_limit_bytes=VMEM_LIMIT),
         cost_estimate=cost(
             2 * channels * depth * inputs * inputs, channels * inputs * (4 * depth + 4 * inputs)
         ),
-        name="correlate_first",
+        name="correlate_last",
     )(wide, tall)
 
 
@@ -263,10 +271,11 @@
     sources = len(rolled)
     wide_ref, tall_ref = refs[:2]
     spectra_refs = refs[2 : 2 + sources]
-    out_ref, scratch, right, below, sems = refs[3 + sources :]
+    out_ref, scratch, above, corner, sems = refs[3 + sources :]
     rows = spectra_refs[0].shape[2]
     depth = wide_ref.shape[1] // 2
-    before = wide_ref.shape[2]
+    after = wide_ref.shape[2]
+    inputs = above.shape[1]
     step = pl.program_id(0)
     slot = step % 2
 
@@ -277,10 +286,10 @@
     def copies(slot, channel):
         return (
             pltpu.make_async_copy(
-                right.at[slot], out_ref.at[channel, pl.ds(0, before), pl.ds(before, right.shape[2])], sems.at[slot, 0]
+                above.at[slot], out_ref.at[channel, pl.ds(0, inputs), :], sems.at[slot, 0]
             ),
             pltpu.make_async_copy(
-                below.at[slot], out_ref.at[channel, pl.ds(before, below.shape[1]), :], sems.at[slot, 1]
+                corner.at[slot], out_ref.at[channel, pl.ds(inputs, after), pl.ds(0, inputs)], sems.at[slot, 1]
             ),
         )
 
@@ -299,13 +308,13 @@
     wide = jnp.concatenate([jnp.concatenate(p, 1) for p in parts], 0).astype(jnp.bfloat16)
     tall = jnp.concatenate([jnp.concatenate([t.T for t in p], 0) for p in parts], 1).astype(jnp.bfloat16)
 
-    right[slot] = jnp.dot(tall_ref[0], wide, preferred_element_type=jnp.float32) * scale
-    im_rows = imaginary_rows(tall, depth)
-    below[slot, :, :before] = jnp.dot(im_rows, wide_ref[0], preferred_element_type=jnp.float32) * scale
+    above[slot, :, inputs:] = jnp.dot(tall, wide_ref[0], preferred_element_type=jnp.float32) * scale
+    im_rows = imaginary_rows(tall_ref[0], depth)
+    corner[slot] = jnp.dot(im_rows, wide, preferred_element_type=jnp.float32) * scale
 
     def store(row, col, values):
         height, width = values.shape
-        below[slot, row : row + height, before + col : before + col + width] = values
+        above[slot, row : row + height, col : col + width] = values
 
     packed_square(scale, block, wide, tall, store)
     for copy in copies(slot, first_channel + step):
@@ -320,13 +329,13 @@
 
 
 def correlate_rest(wide, tall, arrays, pieces, rolled, block, first_channel, spectra_count, out):
-    _, double, before = wide.shape
+    _, double, last = wide.shape
     rows, inputs = arrays[-1].shape[2:]
     channels = rows // 2
     shapes = [(*a.shape[:2], rows) for a in arrays]
     in_specs = [
-        pl.BlockSpec((1, double, before), lambda c: (c + first_channel, 0, 0)),
-        pl.BlockSpec((1, before, double), lambda c: (c + first_channel, 0, 0)),
+        pl.BlockSpec((1, double, last), lambda c: (c + first_channel, 0, 0)),
+        pl.BlockSpec((1, last, double), lambda c: (c + first_channel, 0, 0)),
     ]
     in_specs += [
         pl.BlockSpec((*shape, inputs), functools.partial(lambda p, c: (0, 0, p, 0), p))
@@ -342,15 +351,15 @@
         out_shape=jax.ShapeDtypeStruct(out.shape, out.dtype),
         scratch_shapes=[
             scratch,
-            pltpu.VMEM((2, before, inputs), jnp.float32),
-            pltpu.VMEM((2, inputs, before + inputs), jnp.float32),
+            pltpu.VMEM((2, inputs, inputs + last), jnp.float32),
+            pltpu.VMEM((2, last, inputs), jnp.float32),
             pltpu.SemaphoreType.DMA((2, 2)),
         ],
         input_output_aliases={2 + len(arrays): 0},
         compiler_params=pltpu.CompilerParams(vmem_limit_bytes=VMEM_LIMIT),
         cost_estimate=cost(
-            2 * channels * double * inputs * (2 * before + inputs),
-            channels * inputs * (4 * double + 8 * before + 4 * inputs),
+            2 * channels * double * inputs * (2 * last + inputs),
+            channels * inputs * (4 * double + 8 * last + 4 * inputs),
         ),
         name="correlate_rest",
     )(wide, tall, *arrays, out)
@@ -358,6 +367,11 @@
 
 def turn(block):
     return lax.all_to_all(block, "chan", split_axis=0, concat_axis=0, tiled=True)
+
+
+def exchanged(block, distance):
+    route = [(i, i ^ distance) for i in range(lax.axis_size("chan"))]
+    return lax.ppermute(block, "chan", route)
 
 
 def after(value, earlier):
@@ -376,16 +390,18 @@
     blocks = 4
     block = inputs // blocks
     later = [1, 1, 2, 2]
-    follows = jnp.where(lax.axis_index("chan") == devices - 1, 0.0, 1.0).astype(jnp.float32)[None]
+    me = lax.axis_index("chan")
+    follows = jnp.where(me == devices - 1, 0.0, 1.0).astype(jnp.float32)[None]
+    place = jnp.stack([me // PLANE, me % PLANE]).astype(jnp.int32)
     own = {f: (0, f) for f in range(local)}
     inner = [(tuple(range(past, local)), own)]
-    groups = [0], [1, 2, 3]
+    groups = [3], [0, 1, 2]
     rolled = [
-        (((0,),) * (local - past), ((0,), tuple(int(later[b] == 2) for b in some), (0,)))
+        (((0,),) * (local - past),) * PLANE + (((0,), tuple(int(later[b] == 2) for b in some), (0,)),)
         for some in groups
     ]
 
-    def around(voltage, some):
+    def around(some):
         ahead, back, variants = [], [], []
         for b in some:
             rows = voltage[b * block : (b + 1) * block]
@@ -403,27 +419,27 @@
     def neighbours(ahead, back):
         return passed_along(ahead, "chan", 1), passed_back_round(back, "chan")
 
-    def spectra(arrays, begins, variants, splits, rows, *into):
+    def spectra(arrays, begins, variants, splits, rows, planes=0):
         return filter_transform(
-            arrays, begins, variants, local, follows, tap_weights, table, devices, splits, rows, block, *into
+            arrays, begins, variants, local, follows, place, tap_weights, table, devices, splits, planes, rows, block
         )
 
     whole, halves = [2 * channels], [channels, channels]
-    first_sent, first_variants = around(voltage, groups[0])
-    first_around = neighbours(*first_sent)
-    second_sent, second_variants = around(after(voltage, first_sent), groups[1])
-    second_around = neighbours(*after(second_sent, first_around))
-    inner_turned = turn(after(spectra([voltage], [0], inner, whole, inputs)[0], first_around))
-    first = spectra([voltage, *first_around], [0, 0, 0], first_variants, whole, block)[0]
-    turned = turn(after(first, (inner_turned, second_around)))
-    parts = spectra([voltage, *second_around], [1, 0, 0], second_variants, halves, inputs - block)
-    wide, tall = regroup([inner_turned, turned], rolled[0], block, block)
-    result = correlate_first(wide, tall, block, inputs, count)
-    inner_rest = inner_turned[..., block:]
+    sent, variants = around([3, 0, 1, 2])
+    arounds = neighbours(*sent)
+    inner_blocks = spectra([voltage], [0], inner, whole, inputs, devices // PLANE)
+    arrived = [b if k == 0 else exchanged(b, k * PLANE) for k, b in enumerate(inner_blocks)]
+    first = spectra([voltage, *arounds], [3, 0, 0], variants[:1], whole, block)[0]
+    turned = turn(after(first, arrived))
+    stacks = [jnp.concatenate([a[j : j + 1] for a in arrived], 0) for j in range(PLANE)]
+    inner_turned = [s if j == 0 else exchanged(s, j) for j, s in enumerate(stacks)]
+    parts = spectra([voltage, *arounds], [0, 0, 0], variants[1:], halves, inputs - block)
+    wide, tall = regroup([*inner_turned, turned], [3] * PLANE + [0], rolled[0], block, block)
+    result = correlate_last(wide, tall, block, inputs, count)
     for piece, part in enumerate(parts):
-        turned = turn(after(part, turned))
+        turned = turn(after(part, (turned, inner_turned if piece else ())))
         result = correlate_rest(
-            wide, tall, [inner_rest, turned], [piece, 0], rolled[1], block,
+            wide, tall, [*inner_turned, turned], [piece] * PLANE + [0], rolled[1], block,
             piece * channels // 2, count, result,
         )
     return result
@@ -480,7 +496,10 @@
 def solution(mesh):
     in_specs = (P("tile", "chan"), P())
     out_specs = P("chan", "tile", None)
-    body = per_device if mesh.shape["tile"] == 1 else per_device_tiled
+    devices = mesh.shape["chan"]
+    planes = devices // PLANE
+    fits = devices == planes * PLANE and planes and planes & (planes - 1) == 0
+    body = per_device if mesh.shape["tile"] == 1 and fits else per_device_tiled
     return jax.shard_map(
         body, mesh=mesh, in_specs=in_specs, out_specs=out_specs, check_vma=False
     )

time: 283 us -> 271 us (0.958)
  blocking collectives: 59.6 us -> 0 us
  waiting for transfers between devices: 97 us -> 146 us
  starting transfers between devices: 47.5 us -> 38.9 us
  other arithmetic: 0.4 us -> 3.74 us
    all_to_all x1 -> x0, blocking collectives: 59.6 us -> none  [turn(): lax.all_to_all(block, 'chan', split_axis=0, concat_axis=0, tiled=True)]
    ppermute x0 -> x10, waiting for transfers between devices: none -> 53.5 us  [exchanged(): return lax.ppermute(block, 'chan', route)]
    all_to_all x3, starting transfers between devices: 31.8 us -> 15.4 us  [turn(): lax.all_to_all(block, 'chan', split_axis=0, concat_axis=0, tiled=True)]
    ppermute x0 -> x10, starting transfers between devices: none -> 15.9 us  [exchanged(): return lax.ppermute(block, 'chan', route)]
    ppermute x2 -> x1, waiting for transfers between devices: 46.2 us -> 38.9 us  [passed_back_round(): lax.ppermute(block, axis, [(i, (i - 1) % devices) for i in range(devices)])]
    ppermute x2 -> x1, starting transfers between devices: 10.6 us -> 3.7 us  [passed_back_round(): lax.ppermute(block, axis, [(i, (i - 1) % devices) for i in range(devices)])]
    all_to_all x3, waiting for transfers between devices: 50.8 us -> 53.9 us  [turn(): lax.all_to_all(block, 'chan', split_axis=0, concat_axis=0, tiled=True)]
  transfers between devices with their start and end apart: 7 -> 15, of which waited for: 3 -> 10; matrix products, arithmetic and copies ran while one was open for 2% -> 2% of each run, Pallas kernels for 19% -> 21%
where the time goes in v3:
time: 271 us; the launch traced here: 270 us
  waiting for transfers between devices  146 us (54%)
  Pallas kernels  70.5 us (26%)
  starting transfers between devices  38.9 us (14%)
  local copies, waits for them, and re-layouts  9.73 us (4%)
  other arithmetic  3.74 us (1%)
    all_to_all x3, waiting for transfers between devices, turn(): lax.all_to_all(block, 'chan', split_axis=0, concat_axis=0, tiled=True)  53.9 us
    ppermute x10, waiting for transfers between devices, exchanged(): return lax.ppermute(block, 'chan', route)  53.5 us
    ppermute x1, waiting for transfers between devices, passed_back_round(): lax.ppermute(block, axis, [(i, (i - 1) % devices) for i in range(devices)])  38.9 us
    pallas_call x2, Pallas kernels, correlate_rest(): pl.pallas_call(functools.partial(correlate_rest_kernel, 1.0 / spectra_cou...  29.3 us
    pallas_call x3, Pallas kernels, filter_transform(): pl.pallas_call(functools.partial(filter_transform_kernel, variants, local...  28.7 us
    ppermute x10, starting transfers between devices, exchanged(): return lax.ppermute(block, 'chan', route)  15.9 us
    all_to_all x3, starting transfers between devices, turn(): lax.all_to_all(block, 'chan', split_axis=0, concat_axis=0, tiled=True)  15.4 us
    pallas_call x1, Pallas kernels, correlate_last(): pl.pallas_call(functools.partial(correlate_last_kernel, 1.0 / spectra_cou...  7.45 us
  transfers between devices with their start and end apart: 15, of which 10 were waited for; matrix products, arithmetic and copies ran while one was open for 2% of the time, Pallas kernels for 21%

profile of v3, /device:TPU:0, one launch (start us, length us, event | category | flops | bytes accessed | tf_op | source)
XLA Modules:
  0.0 269.6 jit_solution(4747958424723875731)
XLA Ops:
  0.0 1.7 fusion.1
  1.7 2.8 %fusion = (bf16[256,2048]{1,0:T(8,128)(2,1)S(1)}, bf16[256,2048]{1,0:T(8,128)(2,1)S(1)}, bf16[256,2048]{1,0:T(8,128)(2,1)S(1)}, bf16[256,2048]{1,0:T(8,128)(2,1)S(1)}) fusion(bf16[1024,4096]{1,0:T(8,128)(2,1)} %refs_2_.5), kind=kLoop, calls=%fused_computation.11 | loop fusion | bytes 8388608 | tf_op jit(solution)/shard_map/slice | solution.py:414
  4.5 0.4 pad_maximum_fusion
  4.8 4.0 %collective-permute-start.10 = (bf16[256,6144]{1,0:T(8,128)(2,1)S(1)}, bf16[256,6144]{1,0:T(8,128)(2,1)}, u32[]{:S(2)}, u32[]{:S(2)}) collective-permute-start(bf16[256,6144]{1,0:T(8,128)(2,1)S(1)} %pad_maximum_fusion), channel_id=1, source_target_pairs={{0,1},{1,2},{2,3},{3,4},{4,5},{5,6},{6,7},{7,8},{8,9},{9,10},{10,1... | collective-permute-start | bytes 9437192 | tf_op jit(solution)/shard_map/ppermute | solution.py:25
  8.8 1.8 pad_maximum_fusion.1
  10.6 3.7 %collective-permute-start.11 = (bf16[256,6144]{1,0:T(8,128)(2,1)}, bf16[256,6144]{1,0:T(8,128)(2,1)}, u32[]{:S(2)}, u32[]{:S(2)}) collective-permute-start(bf16[256,6144]{1,0:T(8,128)(2,1)} %pad_maximum_fusion.1), channel_id=1, source_target_pairs={{0,31},{1,0},{2,1},{3,2},{4,3},{5,4},{6,5},{7,6},{8,7},{9,8},{10,9... | collective-permute-start | bytes 9437192 | tf_op jit(solution)/shard_map/ppermute | solution.py:30
  14.3 0.6 pad_add_fusion.refs_1_
  14.9 8.1 %filter_transform.3 = (bf16[8,1,32,1024]{3,2,1,0:T(8,128)(2,1)}, bf16[8,1,32,1024]{3,2,1,0:T(8,128)(2,1)}, bf16[8,1,32,1024]{3,2,1,0:T(8,128)(2,1)}, bf16[8,1,32,1024]{3,2,1,0:T(8,128)(2,1)}) custom-call(f32[1]{0:T(128)} %bitcast.refs_0_, s32[2]{0:T(128)} %pad_add_fusion.refs_1_, bf16[1024,4096]{1,0:T(8,128)(2,1)} %refs_2_.5, f32[4,1024]{1,0:T(4,128)} %refs_5_.3, ...), custom_call_target="tpu_custom_call" | custom-call | flops 2147483648 | bytes 12582912 | tf_op jit(solution)/shard_map/filter_transform/pallas_call | solution.py:136
  23.0 0.8 collective-permute-start
  23.8 2.6 collective-permute-start.1
  26.4 1.0 collective-permute-start.2
  27.3 0.0 collective-permute-done.10.refs_3_
  27.3 38.9 %collective-permute-done.11.refs_4_ = bf16[256,6144]{1,0:T(8,128)(2,1)} collective-permute-done((bf16[256,6144]{1,0:T(8,128)(2,1)}, bf16[256,6144]{1,0:T(8,128)(2,1)}, u32[]{:S(2)}, u32[]{:S(2)}) %collective-permute-start.11) | collective-permute-done | bytes 3145760 | tf_op jit(solution)/shard_map/ppermute | solution.py:30
  66.3 6.5 %filter_transform.4 = bf16[32,3,32,256]{3,2,1,0:T(8,128)(2,1)} custom-call(f32[1]{0:T(128)} %bitcast.refs_0_, s32[2]{0:T(128)} %pad_add_fusion.refs_1_, bf16[1024,4096]{1,0:T(8,128)(2,1)} %refs_2_.5, bf16[256,6144]{1,0:T(8,128)(2,1)} %collective-permute-done.10.refs_3_, bf16[256,6144]{1,0:T(8,128)(2,1)} %collective-permute-done.11.refs_4_, ...), custom_call_target="tpu_custom_call" | custom-call | flops 1610612736 | bytes 16777216 | tf_op jit(solution)/shard_map/filter_transform/pallas_call | solution.py:136
  72.8 0.4 collective-permute-done
  73.2 17.9 %collective-permute-done.1 = bf16[8,1,32,1024]{3,2,1,0:T(8,128)(2,1)} collective-permute-done((bf16[8,1,32,1024]{3,2,1,0:T(8,128)(2,1)}, bf16[8,1,32,1024]{3,2,1,0:T(8,128)(2,1)}, u32[]{:S(2)}, u32[]{:S(2)}) %collective-permute-start.1) | collective-permute-done | bytes 524320 | tf_op jit(solution)/shard_map/ppermute | solution.py:374
  91.1 0.0 collective-permute-done.2
  91.1 7.7 %all-to-all-start = ((bf16[32,3,32,256]{3,2,1,0:T(8,128)(2,1)}), bf16[32,3,32,256]{3,2,1,0:T(8,128)(2,1)S(1)}, u32[]{:S(2)}, u32[]{:S(2)}) async-start(bf16[32,3,32,256]{3,2,1,0:T(8,128)(2,1)} %filter_transform.4), calls=%async_computation | async-start | bytes 3145728 | tf_op jit(solution)/shard_map/all_to_all | solution.py:369
  98.8 14.1 %filter_transform.5 = (bf16[32,3,16,768]{3,2,1,0:T(8,128)(2,1)}, bf16[32,3,16,768]{3,2,1,0:T(8,128)(2,1)}) custom-call(f32[1]{0:T(128)} %bitcast.refs_0_, s32[2]{0:T(128)} %pad_add_fusion.refs_1_, bf16[1024,4096]{1,0:T(8,128)(2,1)} %refs_2_.5, bf16[256,6144]{1,0:T(8,128)(2,1)} %collective-permute-done.10.refs_3_, ...), custom_call_target="tpu_custom_call" | custom-call | flops 4831838208 | bytes 33554432 | tf_op jit(solution)/shard_map/filter_transform/pallas_call | solution.py:136
  112.8 0.0 copy-start.8
  112.8 23.7 %all-to-all-done.refs_8_ = bf16[32,3,32,256]{3,2,1,0:T(8,128)(2,1)S(1)} async-done(((bf16[32,3,32,256]{3,2,1,0:T(8,128)(2,1)}), bf16[32,3,32,256]{3,2,1,0:T(8,128)(2,1)S(1)}, u32[]{:S(2)}, u32[]{:S(2)}) %all-to-all-start) | async-done | bytes 1572896 | tf_op jit(solution)/shard_map/all_to_all | solution.py:369
  136.5 0.0 copy-start.1
  136.5 1.2 copy-done.1
  137.7 3.8 %all-to-all-start.1 = ((bf16[32,3,16,768]{3,2,1,0:T(8,128)(2,1)}), bf16[32,3,16,768]{3,2,1,0:T(8,128)(2,1)S(1)}, u32[]{:S(2)}, u32[]{:S(2)}) async-start(bf16[32,3,16,768]{3,2,1,0:T(8,128)(2,1)} %get-tuple-element.25), calls=%async_computation.1 | async-start | bytes 4718592 | tf_op jit(solution)/shard_map/all_to_all | solution.py:369
  141.5 0.0 copy-done.8
  141.5 1.1 fusion.3
  142.7 1.1 fusion.4
  143.8 1.1 fusion.5
  144.9 0.3 collective-permute-start.3
  145.3 1.7 collective-permute-start.4
  147.1 0.1 collective-permute-start.5
  147.2 1.7 collective-permute-start.6
  149.0 0.2 collective-permute-start.7
  149.2 0.0 collective-permute-done.3.refs_1_.refs_3_
  149.2 0.0 copy-start.2
  149.2 2.6 collective-permute-start.8
  151.9 13.6 %collective-permute-done.4.refs_2_.refs_4_ = bf16[4,1,32,1024]{3,2,1,0:T(8,128)(2,1)S(1)} collective-permute-done((bf16[4,1,32,1024]{3,2,1,0:T(8,128)(2,1)S(1)}, bf16[4,1,32,1024]{3,2,1,0:T(8,128)(2,1)S(1)}, u32[]{:S(2)}, u32[]{:S(2)}) %collective-permute-start.4) | collective-permute-done | bytes 262176 | tf_op jit(solution)/shard_map/ppermute | solution.py:374
  165.5 0.0 copy-start.3
  165.5 4.8 %collective-permute-start.9 = (bf16[4,1,32,1024]{3,2,1,0:T(8,128)(2,1)S(1)}, bf16[4,1,32,1024]{3,2,1,0:T(8,128)(2,1)}, u32[]{:S(2)}, u32[]{:S(2)}) collective-permute-start(bf16[4,1,32,1024]{3,2,1,0:T(8,128)(2,1)S(1)} %pad_maximum_fusion.9), channel_id=1, source_target_pairs={{0,7},{1,6},{2,5},{3,4},{4,3},{5,2},{6,1},{7,0},{8,15},{9,14},{10,... | collective-permute-start | bytes 786440 | tf_op jit(solution)/shard_map/ppermute | solution.py:374
  170.3 0.7 pad_maximum_fusion.2.refs_0_.refs_2_
  171.1 6.2 %collective-permute-done.5.refs_3_.refs_5_ = bf16[4,1,32,1024]{3,2,1,0:T(8,128)(2,1)S(1)} collective-permute-done((bf16[4,1,32,1024]{3,2,1,0:T(8,128)(2,1)S(1)}, bf16[4,1,32,1024]{3,2,1,0:T(8,128)(2,1)S(1)}, u32[]{:S(2)}, u32[]{:S(2)}) %collective-permute-start.5) | collective-permute-done | bytes 262176 | tf_op jit(solution)/shard_map/ppermute | solution.py:374
  177.2 0.0 copy-start.4
  177.2 0.0 collective-permute-done.6.refs_4_.refs_6_
  177.2 0.0 copy-start.5
  177.2 0.0 collective-permute-done.7.refs_5_.refs_7_
  177.2 0.0 copy-start.6
  177.2 8.3 %collective-permute-done.8.refs_6_.refs_8_ = bf16[4,1,32,1024]{3,2,1,0:T(8,128)(2,1)S(1)} collective-permute-done((bf16[4,1,32,1024]{3,2,1,0:T(8,128)(2,1)S(1)}, bf16[4,1,32,1024]{3,2,1,0:T(8,128)(2,1)S(1)}, u32[]{:S(2)}, u32[]{:S(2)}) %collective-permute-start.8) | collective-permute-done | bytes 262176 | tf_op jit(solution)/shard_map/ppermute | solution.py:374
  185.5 0.0 copy-done.6
  185.5 0.0 copy-start.7
  185.5 0.7 copy-done.7
  186.2 7.2 %collective-permute-done.9.refs_7_.refs_9_ = bf16[4,1,32,1024]{3,2,1,0:T(8,128)(2,1)} collective-permute-done((bf16[4,1,32,1024]{3,2,1,0:T(8,128)(2,1)S(1)}, bf16[4,1,32,1024]{3,2,1,0:T(8,128)(2,1)}, u32[]{:S(2)}, u32[]{:S(2)}) %collective-permute-start.9) | collective-permute-done | bytes 262176 | tf_op jit(solution)/shard_map/ppermute | solution.py:374
  193.4 3.1 %all-to-all-done.1.refs_10_ = bf16[32,3,16,768]{3,2,1,0:T(8,128)(2,1)S(1)} async-done(((bf16[32,3,16,768]{3,2,1,0:T(8,128)(2,1)}), bf16[32,3,16,768]{3,2,1,0:T(8,128)(2,1)S(1)}, u32[]{:S(2)}, u32[]{:S(2)}) %all-to-all-start.1) | async-done | bytes 2359328 | tf_op jit(solution)/shard_map/all_to_all | solution.py:369
  196.4 0.0 copy-start
  196.4 3.9 %all-to-all-start.2 = ((bf16[32,3,16,768]{3,2,1,0:T(8,128)(2,1)}), bf16[32,3,16,768]{3,2,1,0:T(8,128)(2,1)}, u32[]{:S(2)}, u32[]{:S(2)}) async-start(bf16[32,3,16,768]{3,2,1,0:T(8,128)(2,1)} %get-tuple-element.26), calls=%async_computation.2 | async-start | bytes 4718592 | tf_op jit(solution)/shard_map/all_to_all | solution.py:369
  200.4 0.0 copy-done.2
  200.4 0.0 copy-done.3
  200.4 0.0 copy-done.4
  200.4 0.0 copy-done.5
  200.4 5.1 %regroup.1 = (bf16[16,256,256]{2,1,0:T(8,128)(2,1)}, bf16[16,256,256]{2,1,0:T(8,128)(2,1)}) custom-call(bf16[4,1,32,1024]{3,2,1,0:T(8,128)(2,1)} %pad_maximum_fusion.2.refs_0_.refs_2_, bf16[4,1,32,1024]{3,2,1,0:T(8,128)(2,1)} %copy-done.2, bf16[4,1,32,1024]{3,2,1,0:T(8,128)(2,1)} %copy-done.3, bf16[4,1,32,1024]{3,2,1,0:T(8,128)(2,1)} %copy-done.4, ...), custom_call_target="tpu_custom_call" | custom-call | bytes 6291456 | tf_op jit(solution)/shard_map/regroup/pallas_call | solution.py:199
  205.5 0.0 copy-done
  205.5 7.4 %correlate_last.1.refs_11_ = f32[16,1024,1024]{2,1,0:T(8,128)} custom-call(bf16[16,256,256]{2,1,0:T(8,128)(2,1)} %get-tuple-element.21.wide_ref.refs_0_, bf16[16,256,256]{2,1,0:T(8,128)(2,1)} %get-tuple-element.22.tall_ref.refs_1_), custom_call_target="tpu_custom_call" | custom-call | flops 536870912 | bytes 8388608 | tf_op jit(solution)/shard_map/correlate_last/pallas_call | solution.py:253
  212.9 14.7 %correlate_rest.2.refs_11_ = f32[16,1024,1024]{2,1,0:T(8,128)} custom-call(bf16[16,256,256]{2,1,0:T(8,128)(2,1)} %get-tuple-element.21.wide_ref.refs_0_, bf16[16,256,256]{2,1,0:T(8,128)(2,1)} %get-tuple-element.22.tall_ref.refs_1_, bf16[4,1,32,1024]{3,2,1,0:T(8,128)(2,1)} %pad_maximum_fusion.2.refs_0_.refs_2_, ...), custom_call_target="tpu_custom_call", output_to_operand_aliasing={{}: (11, {})} | custom-call | flops 4026531840 | bytes 37748736 | tf_op jit(solution)/shard_map/correlate_rest/pallas_call | solution.py:346
  227.6 27.2 %all-to-all-done.2.refs_10_ = bf16[32,3,16,768]{3,2,1,0:T(8,128)(2,1)} async-done(((bf16[32,3,16,768]{3,2,1,0:T(8,128)(2,1)}), bf16[32,3,16,768]{3,2,1,0:T(8,128)(2,1)}, u32[]{:S(2)}, u32[]{:S(2)}) %all-to-all-start.2) | async-done | bytes 2359328 | tf_op jit(solution)/shard_map/all_to_all | solution.py:369
  254.8 14.6 %correlate_rest.3 = f32[16,1024,1024]{2,1,0:T(8,128)} custom-call(bf16[16,256,256]{2,1,0:T(8,128)(2,1)} %get-tuple-element.21.wide_ref.refs_0_, bf16[16,256,256]{2,1,0:T(8,128)(2,1)} %get-tuple-element.22.tall_ref.refs_1_, bf16[4,1,32,1024]{3,2,1,0:T(8,128)(2,1)} %pad_maximum_fusion.2.refs_0_.refs_2_, ...), custom_call_target="tpu_custom_call", output_to_operand_aliasing={{}: (11, {})} | custom-call | flops 4026531840 | bytes 37748736 | tf_op jit(solution)/shard_map/correlate_rest/pallas_call | solution.py:346
  (8 shorter events, 0.3 us)
Async XLA Ops:
  4.8 22.5 %collective-permute-start.10 = (bf16[256,6144]{1,0:T(8,128)(2,1)S(1)}, bf16[256,6144]{1,0:T(8,128)(2,1)}, u32[]{:S(2)}, u32[]{:S(2)}) collective-permute-start(bf16[256,6144]{1,0:T(8,128)(2,1)S(1)} %pad_maximum_fusion), channel_id=1, source_target_pairs={{0,1},{1,2},{2,3},{3,4},{4,5},{5,6},{6,7},{7,8},{8,9},{9,10},{10,1... | collective-permute-start | bytes 9437192 | tf_op jit(solution)/shard_map/ppermute | solution.py:25
  10.6 55.7 %collective-permute-start.11 = (bf16[256,6144]{1,0:T(8,128)(2,1)}, bf16[256,6144]{1,0:T(8,128)(2,1)}, u32[]{:S(2)}, u32[]{:S(2)}) collective-permute-start(bf16[256,6144]{1,0:T(8,128)(2,1)} %pad_maximum_fusion.1), channel_id=1, source_target_pairs={{0,31},{1,0},{2,1},{3,2},{4,3},{5,4},{6,5},{7,6},{8,7},{9,8},{10,9... | collective-permute-start | bytes 9437192 | tf_op jit(solution)/shard_map/ppermute | solution.py:30
  23.0 50.2 %collective-permute-start = (bf16[8,1,32,1024]{3,2,1,0:T(8,128)(2,1)}, bf16[8,1,32,1024]{3,2,1,0:T(8,128)(2,1)}, u32[]{:S(2)}, u32[]{:S(2)}) collective-permute-start(bf16[8,1,32,1024]{3,2,1,0:T(8,128)(2,1)} %get-tuple-element.17), channel_id=1, source_target_pairs={{0,8},{1,9},{2,10},{3,11},{4,12},{5,13},{6,14},{7,15},{8,0},{9,1},... | collective-permute-start | bytes 1572872 | tf_op jit(solution)/shard_map/ppermute | solution.py:374
  23.8 67.3 %collective-permute-start.1 = (bf16[8,1,32,1024]{3,2,1,0:T(8,128)(2,1)}, bf16[8,1,32,1024]{3,2,1,0:T(8,128)(2,1)}, u32[]{:S(2)}, u32[]{:S(2)}) collective-permute-start(bf16[8,1,32,1024]{3,2,1,0:T(8,128)(2,1)} %get-tuple-element.18), channel_id=1, source_target_pairs={{0,16},{1,17},{2,18},{3,19},{4,20},{5,21},{6,22},{7,23},{8,24},{9,... | collective-permute-start | bytes 1572872 | tf_op jit(solution)/shard_map/ppermute | solution.py:374
  26.4 64.7 %collective-permute-start.2 = (bf16[8,1,32,1024]{3,2,1,0:T(8,128)(2,1)}, bf16[8,1,32,1024]{3,2,1,0:T(8,128)(2,1)}, u32[]{:S(2)}, u32[]{:S(2)}) collective-permute-start(bf16[8,1,32,1024]{3,2,1,0:T(8,128)(2,1)} %get-tuple-element.19), channel_id=1, source_target_pairs={{0,24},{1,25},{2,26},{3,27},{4,28},{5,29},{6,30},{7,31},{8,16},{9,... | collective-permute-start | bytes 1572872 | tf_op jit(solution)/shard_map/ppermute | solution.py:374
  91.1 45.4 %all-to-all-start = ((bf16[32,3,32,256]{3,2,1,0:T(8,128)(2,1)}), bf16[32,3,32,256]{3,2,1,0:T(8,128)(2,1)S(1)}, u32[]{:S(2)}, u32[]{:S(2)}) async-start(bf16[32,3,32,256]{3,2,1,0:T(8,128)(2,1)} %filter_transform.4), calls=%async_computation | async-start | bytes 3145728 | tf_op jit(solution)/shard_map/all_to_all | solution.py:369
  112.8 28.6 %copy-start.8 = (bf16[8,1,32,1024]{3,2,1,0:T(8,128)(2,1)S(1)}, bf16[8,1,32,1024]{3,2,1,0:T(8,128)(2,1)}, u32[]{:S(2)}) copy-start(bf16[8,1,32,1024]{3,2,1,0:T(8,128)(2,1)} %get-tuple-element.16) | copy-start | bytes 1572868
  136.5 1.2 copy-start.1
  137.7 58.7 %all-to-all-start.1 = ((bf16[32,3,16,768]{3,2,1,0:T(8,128)(2,1)}), bf16[32,3,16,768]{3,2,1,0:T(8,128)(2,1)S(1)}, u32[]{:S(2)}, u32[]{:S(2)}) async-start(bf16[32,3,16,768]{3,2,1,0:T(8,128)(2,1)} %get-tuple-element.25), calls=%async_computation.1 | async-start | bytes 4718592 | tf_op jit(solution)/shard_map/all_to_all | solution.py:369
  144.9 4.3 %collective-permute-start.3 = (bf16[4,1,32,1024]{3,2,1,0:T(8,128)(2,1)S(1)}, bf16[4,1,32,1024]{3,2,1,0:T(8,128)(2,1)S(1)}, u32[]{:S(2)}, u32[]{:S(2)}) collective-permute-start(bf16[4,1,32,1024]{3,2,1,0:T(8,128)(2,1)S(1)} %pad_maximum_fusion.3), channel_id=1, source_target_pairs={{0,1},{1,0},{2,3},{3,2},{4,5},{5,4},{6,7},{7,6},{8,9},{9,8},{10,11... | collective-permute-start | bytes 786440 | tf_op jit(solution)/shard_map/ppermute | solution.py:374
  145.3 20.3 %collective-permute-start.4 = (bf16[4,1,32,1024]{3,2,1,0:T(8,128)(2,1)S(1)}, bf16[4,1,32,1024]{3,2,1,0:T(8,128)(2,1)S(1)}, u32[]{:S(2)}, u32[]{:S(2)}) collective-permute-start(bf16[4,1,32,1024]{3,2,1,0:T(8,128)(2,1)S(1)} %pad_maximum_fusion.4), channel_id=1, source_target_pairs={{0,2},{1,3},{2,0},{3,1},{4,6},{5,7},{6,4},{7,5},{8,10},{9,11},{10,... | collective-permute-start | bytes 786440 | tf_op jit(solution)/shard_map/ppermute | solution.py:374
  147.1 30.2 %collective-permute-start.5 = (bf16[4,1,32,1024]{3,2,1,0:T(8,128)(2,1)S(1)}, bf16[4,1,32,1024]{3,2,1,0:T(8,128)(2,1)S(1)}, u32[]{:S(2)}, u32[]{:S(2)}) collective-permute-start(bf16[4,1,32,1024]{3,2,1,0:T(8,128)(2,1)S(1)} %pad_maximum_fusion.5), channel_id=1, source_target_pairs={{0,3},{1,2},{2,1},{3,0},{4,7},{5,6},{6,5},{7,4},{8,11},{9,10},{10,... | collective-permute-start | bytes 786440 | tf_op jit(solution)/shard_map/ppermute | solution.py:374
  147.2 30.0 %collective-permute-start.6 = (bf16[4,1,32,1024]{3,2,1,0:T(8,128)(2,1)S(1)}, bf16[4,1,32,1024]{3,2,1,0:T(8,128)(2,1)S(1)}, u32[]{:S(2)}, u32[]{:S(2)}) collective-permute-start(bf16[4,1,32,1024]{3,2,1,0:T(8,128)(2,1)S(1)} %pad_maximum_fusion.6), channel_id=1, source_target_pairs={{0,4},{1,5},{2,6},{3,7},{4,0},{5,1},{6,2},{7,3},{8,12},{9,13},{10,... | collective-permute-start | bytes 786440 | tf_op jit(solution)/shard_map/ppermute | solution.py:374
  149.0 28.3 %collective-permute-start.7 = (bf16[4,1,32,1024]{3,2,1,0:T(8,128)(2,1)S(1)}, bf16[4,1,32,1024]{3,2,1,0:T(8,128)(2,1)S(1)}, u32[]{:S(2)}, u32[]{:S(2)}) collective-permute-start(bf16[4,1,32,1024]{3,2,1,0:T(8,128)(2,1)S(1)} %pad_maximum_fusion.7), channel_id=1, source_target_pairs={{0,5},{1,4},{2,7},{3,6},{4,1},{5,0},{6,3},{7,2},{8,13},{9,12},{10,... | collective-permute-start | bytes 786440 | tf_op jit(solution)/shard_map/ppermute | solution.py:374
  149.2 51.2 %copy-start.2 = (bf16[4,1,32,1024]{3,2,1,0:T(8,128)(2,1)}, bf16[4,1,32,1024]{3,2,1,0:T(8,128)(2,1)S(1)}, u32[]{:S(2)}) copy-start(bf16[4,1,32,1024]{3,2,1,0:T(8,128)(2,1)S(1)} %collective-permute-done.3.refs_1_.refs_3_) | copy-start | bytes 786436
  149.2 36.3 %collective-permute-start.8 = (bf16[4,1,32,1024]{3,2,1,0:T(8,128)(2,1)S(1)}, bf16[4,1,32,1024]{3,2,1,0:T(8,128)(2,1)S(1)}, u32[]{:S(2)}, u32[]{:S(2)}) collective-permute-start(bf16[4,1,32,1024]{3,2,1,0:T(8,128)(2,1)S(1)} %pad_maximum_fusion.8), channel_id=1, source_target_pairs={{0,6},{1,7},{2,4},{3,5},{4,2},{5,3},{6,0},{7,1},{8,14},{9,15},{10,... | collective-permute-start | bytes 786440 | tf_op jit(solution)/shard_map/ppermute | solution.py:374
  165.5 34.9 %copy-start.3 = (bf16[4,1,32,1024]{3,2,1,0:T(8,128)(2,1)}, bf16[4,1,32,1024]{3,2,1,0:T(8,128)(2,1)S(1)}, u32[]{:S(2)}) copy-start(bf16[4,1,32,1024]{3,2,1,0:T(8,128)(2,1)S(1)} %collective-permute-done.4.refs_2_.refs_4_) | copy-start | bytes 786436
  165.5 27.9 %collective-permute-start.9 = (bf16[4,1,32,1024]{3,2,1,0:T(8,128)(2,1)S(1)}, bf16[4,1,32,1024]{3,2,1,0:T(8,128)(2,1)}, u32[]{:S(2)}, u32[]{:S(2)}) collective-permute-start(bf16[4,1,32,1024]{3,2,1,0:T(8,128)(2,1)S(1)} %pad_maximum_fusion.9), channel_id=1, source_target_pairs={{0,7},{1,6},{2,5},{3,4},{4,3},{5,2},{6,1},{7,0},{8,15},{9,14},{10,... | collective-permute-start | bytes 786440 | tf_op jit(solution)/shard_map/ppermute | solution.py:374
  177.2 23.2 %copy-start.4 = (bf16[4,1,32,1024]{3,2,1,0:T(8,128)(2,1)}, bf16[4,1,32,1024]{3,2,1,0:T(8,128)(2,1)S(1)}, u32[]{:S(2)}) copy-start(bf16[4,1,32,1024]{3,2,1,0:T(8,128)(2,1)S(1)} %collective-permute-done.5.refs_3_.refs_5_) | copy-start | bytes 786436
  177.2 23.2 %copy-start.5 = (bf16[4,1,32,1024]{3,2,1,0:T(8,128)(2,1)}, bf16[4,1,32,1024]{3,2,1,0:T(8,128)(2,1)S(1)}, u32[]{:S(2)}) copy-start(bf16[4,1,32,1024]{3,2,1,0:T(8,128)(2,1)S(1)} %collective-permute-done.6.refs_4_.refs_6_) | copy-start | bytes 786436
  177.2 8.3 %copy-start.6 = (bf16[4,1,32,1024]{3,2,1,0:T(8,128)(2,1)}, bf16[4,1,32,1024]{3,2,1,0:T(8,128)(2,1)S(1)}, u32[]{:S(2)}) copy-start(bf16[4,1,32,1024]{3,2,1,0:T(8,128)(2,1)S(1)} %collective-permute-done.7.refs_5_.refs_7_) | copy-start | bytes 786436
  185.5 0.7 copy-start.7
  196.4 9.0 %copy-start = (bf16[32,3,16,768]{3,2,1,0:T(8,128)(2,1)}, bf16[32,3,16,768]{3,2,1,0:T(8,128)(2,1)S(1)}, u32[]{:S(2)}) copy-start(bf16[32,3,16,768]{3,2,1,0:T(8,128)(2,1)S(1)} %all-to-all-done.1.refs_10_) | copy-start | bytes 7077892
  196.4 58.3 %all-to-all-start.2 = ((bf16[32,3,16,768]{3,2,1,0:T(8,128)(2,1)}), bf16[32,3,16,768]{3,2,1,0:T(8,128)(2,1)}, u32[]{:S(2)}, u32[]{:S(2)}) async-start(bf16[32,3,16,768]{3,2,1,0:T(8,128)(2,1)} %get-tuple-element.26), calls=%async_computation.2 | async-start | bytes 4718592 | tf_op jit(solution)/shard_map/all_to_all | solution.py:369

commit v4 on v3

--- a/solution.py
+++ b/solution.py
@@ -15,7 +15,6 @@
 VMEM_LIMIT = 56 * 1024 * 1024
 FILTER_ROWS = 32
 LANES = 128
-PITCH = 8
 PLANE = 8
 
 
@@ -98,16 +97,15 @@
                 (((1,), (1,)), ((), ())),
                 preferred_element_type=jnp.float32,
             )
-            spectrum = spectrum.astype(jnp.bfloat16).reshape(dest_block, per_dest, rows)
+            spectrum = spectrum.reshape(dest_block, per_dest, rows)
             if planes:
                 for dest in range(dest_block):
-                    out_refs[block][dest ^ place_ref[1], slot] = spectrum[dest]
+                    out_refs[block][dest ^ place_ref[1], slot] = spectrum[dest].astype(jnp.bfloat16)
                 continue
             begin = 0
             for out_ref, width in zip(out_refs, splits):
-                out_ref[block * dest_block : (block + 1) * dest_block, slot] = spectrum[
-                    :, begin : begin + width, :
-                ]
+                part = spectrum[:, begin : begin + width, :].astype(jnp.bfloat16)
+                out_ref[block * dest_block : (block + 1) * dest_block, slot] = part
                 begin += width
 
 
@@ -151,12 +149,16 @@
     )(follows, place, *arrays, weights, table)
 
 
+def pitch_of(rows):
+    return (rows // 8 | 1) * 8
+
+
 def spread(spectra_refs, rolled, scratch):
     base = 0
     tiles = scratch.shape[0]
     for ref, moves in zip(spectra_refs, rolled):
         devices, count, rows, _ = ref.shape
-        pitch = rows + PITCH
+        pitch = pitch_of(rows)
         for slot in range(count):
             for d in range(devices):
                 block = ref[d, slot].astype(jnp.float32)
@@ -169,7 +171,7 @@
 
 def spread_shape(arrays, lanes):
     depth = sum(a.shape[0] * a.shape[1] for a in arrays)
-    return depth, pltpu.VMEM((lanes // LANES, depth * (arrays[0].shape[2] + PITCH), LANES), jnp.float32)
+    return depth, pltpu.VMEM((lanes // LANES, depth * pitch_of(arrays[0].shape[2]), LANES), jnp.float32)
 
 
 def regroup_kernel(rolled, *refs):
@@ -183,7 +185,7 @@
             deep = slice(part * depth, (part + 1) * depth)
             for tile in range(scratch.shape[0]):
                 across = slice(tile * LANES, (tile + 1) * LANES)
-                values = scratch[tile, pl.ds(2 * channel + part, depth, stride=rows + PITCH), :]
+                values = scratch[tile, pl.ds(2 * channel + part, depth, stride=pitch_of(rows)), :]
                 wide_ref[channel, deep, across] = values.astype(jnp.bfloat16)
                 tall_ref[channel, across, deep] = values.T.astype(jnp.bfloat16)
 
@@ -271,8 +273,10 @@
     sources = len(rolled)
     wide_ref, tall_ref = refs[:2]
     spectra_refs = refs[2 : 2 + sources]
-    out_ref, scratch, above, corner, sems = refs[3 + sources :]
-    rows = spectra_refs[0].shape[2]
+    out_ref, *scratches, above, corner, sems = refs[3 + sources :]
+    sets = spectra_refs[:-1], spectra_refs[-1:]
+    heights = [refs_of[0].shape[2] for refs_of in sets]
+    firsts = first_channel, 0
     depth = wide_ref.shape[1] // 2
     after = wide_ref.shape[2]
     inputs = above.shape[1]
@@ -281,7 +285,16 @@
 
     @pl.when(step == 0)
     def _():
-        spread(spectra_refs, rolled, scratch)
+        spread(sets[0], rolled[:-1], scratches[0])
+        spread(sets[1], rolled[-1:], scratches[1])
+
+    def values(tile, part):
+        pieces = []
+        for scratch, rows, first in zip(scratches, heights, firsts):
+            pitch = pitch_of(rows)
+            start = 2 * (first + step) + part
+            pieces.append(scratch[tile, pl.ds(start, scratch.shape[1] // pitch, stride=pitch), :])
+        return jnp.concatenate(pieces, 0)
 
     def copies(slot, channel):
         return (
@@ -298,13 +311,7 @@
         for copy in copies(slot, first_channel + step - 2):
             copy.wait()
 
-    parts = [
-        [
-            scratch[tile, pl.ds(2 * step + part, depth, stride=rows + PITCH), :]
-            for tile in range(scratch.shape[0])
-        ]
-        for part in range(2)
-    ]
+    parts = [[values(tile, part) for tile in range(scratches[0].shape[0])] for part in range(2)]
     wide = jnp.concatenate([jnp.concatenate(p, 1) for p in parts], 0).astype(jnp.bfloat16)
     tall = jnp.concatenate([jnp.concatenate([t.T for t in p], 0) for p in parts], 1).astype(jnp.bfloat16)
 
@@ -328,21 +335,17 @@
             copy.wait()
 
 
-def correlate_rest(wide, tall, arrays, pieces, rolled, block, first_channel, spectra_count, out):
+def correlate_rest(wide, tall, arrays, rolled, block, first_channel, spectra_count, out):
     _, double, last = wide.shape
     rows, inputs = arrays[-1].shape[2:]
     channels = rows // 2
-    shapes = [(*a.shape[:2], rows) for a in arrays]
     in_specs = [
         pl.BlockSpec((1, double, last), lambda c: (c + first_channel, 0, 0)),
         pl.BlockSpec((1, last, double), lambda c: (c + first_channel, 0, 0)),
     ]
-    in_specs += [
-        pl.BlockSpec((*shape, inputs), functools.partial(lambda p, c: (0, 0, p, 0), p))
-        for shape, p in zip(shapes, pieces)
-    ]
+    in_specs += [pl.BlockSpec((*a.shape[:3], inputs), lambda c: (0, 0, 0, 0)) for a in arrays]
     in_specs.append(pl.BlockSpec(memory_space=pl.ANY))
-    scratch = pltpu.VMEM((inputs // LANES, double // 2 * (rows + PITCH), LANES), jnp.float32)
+    scratches = [spread_shape(some, inputs)[1] for some in (arrays[:-1], arrays[-1:])]
     return pl.pallas_call(
         functools.partial(correlate_rest_kernel, 1.0 / spectra_count, block, first_channel, rolled),
         grid=(channels,),
@@ -350,7 +353,7 @@
         out_specs=pl.BlockSpec(memory_space=pl.ANY),
         out_shape=jax.ShapeDtypeStruct(out.shape, out.dtype),
         scratch_shapes=[
-            scratch,
+            *scratches,
             pltpu.VMEM((2, inputs, inputs + last), jnp.float32),
             pltpu.VMEM((2, last, inputs), jnp.float32),
             pltpu.SemaphoreType.DMA((2, 2)),
@@ -424,7 +427,8 @@
             arrays, begins, variants, local, follows, place, tap_weights, table, devices, splits, planes, rows, block
         )
 
-    whole, halves = [2 * channels], [channels, channels]
+    whole = [2 * channels]
+    shares = [channels - channels // 4, channels // 4]
     sent, variants = around([3, 0, 1, 2])
     arounds = neighbours(*sent)
     inner_blocks = spectra([voltage], [0], inner, whole, inputs, devices // PLANE)
@@ -433,15 +437,18 @@
     turned = turn(after(first, arrived))
     stacks = [jnp.concatenate([a[j : j + 1] for a in arrived], 0) for j in range(PLANE)]
     inner_turned = [s if j == 0 else exchanged(s, j) for j, s in enumerate(stacks)]
-    parts = spectra([voltage, *arounds], [0, 0, 0], variants[1:], halves, inputs - block)
+    parts = spectra([voltage, *arounds], [0, 0, 0], variants[1:], [2 * c for c in shares], inputs - block)
     wide, tall = regroup([*inner_turned, turned], [3] * PLANE + [0], rolled[0], block, block)
     result = correlate_last(wide, tall, block, inputs, count)
-    for piece, part in enumerate(parts):
-        turned = turn(after(part, (turned, inner_turned if piece else ())))
+    first_turned = turn(after(parts[0], turned))
+    part, result, first_turned = lax.optimization_barrier((parts[1], result, first_turned))
+    second_turned = turn(part)
+    begin = 0
+    for share, turned in zip(shares, (first_turned, second_turned)):
         result = correlate_rest(
-            wide, tall, [*inner_turned, turned], [piece] * PLANE + [0], rolled[1], block,
-            piece * channels // 2, count, result,
+            wide, tall, [*inner_turned, turned], rolled[1], block, begin, count, result
         )
+        begin += share
     return result
 
 

time: 271 us -> 265 us (0.978)
  waiting for transfers between devices: 146 us -> 140 us
    all_to_all x3, waiting for transfers between devices: 53.9 us -> 39.4 us  [turn(): lax.all_to_all(block, 'chan', split_axis=0, concat_axis=0, tiled=True)]
    ppermute x10, waiting for transfers between devices: 53.5 us -> 62 us  [exchanged(): return lax.ppermute(block, 'chan', route)]
  transfers between devices with their start and end apart: 15 -> 15, of which waited for: 10 -> 10; matrix products, arithmetic and copies ran while one was open for 2% -> 3% of each run, Pallas kernels for 21% -> 23%
where the time goes in v4:
time: 265 us; the launch traced here: 264 us
  waiting for transfers between devices  140 us (53%)
  Pallas kernels  70.9 us (27%)
  starting transfers between devices  37.6 us (14%)
  local copies, waits for them, and re-layouts  10.7 us (4%)
  other arithmetic  3.77 us (1%)
    ppermute x10, waiting for transfers between devices, exchanged(): return lax.ppermute(block, 'chan', route)  62 us
    all_to_all x3, waiting for transfers between devices, turn(): lax.all_to_all(block, 'chan', split_axis=0, concat_axis=0, tiled=True)  39.4 us
    ppermute x1, waiting for transfers between devices, passed_back_round(): lax.ppermute(block, axis, [(i, (i - 1) % devices) for i in range(devices)])  38.9 us
    pallas_call x2, Pallas kernels, correlate_rest(): pl.pallas_call(functools.partial(correlate_rest_kernel, 1.0 / spectra_cou...  29.8 us
    pallas_call x3, Pallas kernels, filter_transform(): pl.pallas_call(functools.partial(filter_transform_kernel, variants, local...  28.7 us
    all_to_all x3, starting transfers between devices, turn(): lax.all_to_all(block, 'chan', split_axis=0, concat_axis=0, tiled=True)  15.4 us
    ppermute x10, starting transfers between devices, exchanged(): return lax.ppermute(block, 'chan', route)  14.5 us
    pallas_call x1, Pallas kernels, correlate_last(): pl.pallas_call(functools.partial(correlate_last_kernel, 1.0 / spectra_cou...  7.44 us
  transfers between devices with their start and end apart: 15, of which 10 were waited for; matrix products, arithmetic and copies ran while one was open for 3% of the time, Pallas kernels for 23%

profile of v4, /device:TPU:0, one launch (start us, length us, event | category | flops | bytes accessed | tf_op | source)
XLA Modules:
  0.0 263.6 jit_solution(16521420915952244573)
XLA Ops:
  0.0 1.7 fusion.1
  1.7 2.8 %fusion = (bf16[256,2048]{1,0:T(8,128)(2,1)S(1)}, bf16[256,2048]{1,0:T(8,128)(2,1)S(1)}, bf16[256,2048]{1,0:T(8,128)(2,1)S(1)}, bf16[256,2048]{1,0:T(8,128)(2,1)S(1)}) fusion(bf16[1024,4096]{1,0:T(8,128)(2,1)} %refs_2_.5), kind=kLoop, calls=%fused_computation.11 | loop fusion | bytes 8388608 | tf_op jit(solution)/shard_map/slice | solution.py:417
  4.5 0.4 pad_maximum_fusion
  4.8 4.0 %collective-permute-start.10 = (bf16[256,6144]{1,0:T(8,128)(2,1)S(1)}, bf16[256,6144]{1,0:T(8,128)(2,1)}, u32[]{:S(2)}, u32[]{:S(2)}) collective-permute-start(bf16[256,6144]{1,0:T(8,128)(2,1)S(1)} %pad_maximum_fusion), channel_id=1, source_target_pairs={{0,1},{1,2},{2,3},{3,4},{4,5},{5,6},{6,7},{7,8},{8,9},{9,10},{10,1... | collective-permute-start | bytes 9437192 | tf_op jit(solution)/shard_map/ppermute | solution.py:24
  8.8 1.8 pad_maximum_fusion.1
  10.6 3.7 %collective-permute-start.11 = (bf16[256,6144]{1,0:T(8,128)(2,1)}, bf16[256,6144]{1,0:T(8,128)(2,1)}, u32[]{:S(2)}, u32[]{:S(2)}) collective-permute-start(bf16[256,6144]{1,0:T(8,128)(2,1)} %pad_maximum_fusion.1), channel_id=1, source_target_pairs={{0,31},{1,0},{2,1},{3,2},{4,3},{5,4},{6,5},{7,6},{8,7},{9,8},{10,9... | collective-permute-start | bytes 9437192 | tf_op jit(solution)/shard_map/ppermute | solution.py:29
  14.3 0.6 pad_add_fusion.refs_1_
  15.0 8.1 %filter_transform.3 = (bf16[8,1,32,1024]{3,2,1,0:T(8,128)(2,1)}, bf16[8,1,32,1024]{3,2,1,0:T(8,128)(2,1)}, bf16[8,1,32,1024]{3,2,1,0:T(8,128)(2,1)}, bf16[8,1,32,1024]{3,2,1,0:T(8,128)(2,1)}) custom-call(f32[1]{0:T(128)} %bitcast.refs_0_, s32[2]{0:T(128)} %pad_add_fusion.refs_1_, bf16[1024,4096]{1,0:T(8,128)(2,1)} %refs_2_.5, f32[4,1024]{1,0:T(4,128)} %refs_5_.3, ...), custom_call_target="tpu_custom_call" | custom-call | flops 2147483648 | bytes 12582912 | tf_op jit(solution)/shard_map/filter_transform/pallas_call | solution.py:134
  23.0 0.8 collective-permute-start
  23.8 2.6 collective-permute-start.1
  26.4 1.0 collective-permute-start.2
  27.4 0.0 collective-permute-done.10.refs_3_
  27.4 38.9 %collective-permute-done.11.refs_4_ = bf16[256,6144]{1,0:T(8,128)(2,1)} collective-permute-done((bf16[256,6144]{1,0:T(8,128)(2,1)}, bf16[256,6144]{1,0:T(8,128)(2,1)}, u32[]{:S(2)}, u32[]{:S(2)}) %collective-permute-start.11) | collective-permute-done | bytes 3145760 | tf_op jit(solution)/shard_map/ppermute | solution.py:29
  66.3 6.5 %filter_transform.4 = bf16[32,3,32,256]{3,2,1,0:T(8,128)(2,1)} custom-call(f32[1]{0:T(128)} %bitcast.refs_0_, s32[2]{0:T(128)} %pad_add_fusion.refs_1_, bf16[1024,4096]{1,0:T(8,128)(2,1)} %refs_2_.5, bf16[256,6144]{1,0:T(8,128)(2,1)} %collective-permute-done.10.refs_3_, bf16[256,6144]{1,0:T(8,128)(2,1)} %collective-permute-done.11.refs_4_, ...), custom_call_target="tpu_custom_call" | custom-call | flops 1610612736 | bytes 16777216 | tf_op jit(solution)/shard_map/filter_transform/pallas_call | solution.py:134
  72.8 0.4 collective-permute-done
  73.2 17.9 %collective-permute-done.1 = bf16[8,1,32,1024]{3,2,1,0:T(8,128)(2,1)} collective-permute-done((bf16[8,1,32,1024]{3,2,1,0:T(8,128)(2,1)}, bf16[8,1,32,1024]{3,2,1,0:T(8,128)(2,1)}, u32[]{:S(2)}, u32[]{:S(2)}) %collective-permute-start.1) | collective-permute-done | bytes 524320 | tf_op jit(solution)/shard_map/ppermute | solution.py:377
  91.1 0.0 collective-permute-done.2
  91.1 7.7 %all-to-all-start = ((bf16[32,3,32,256]{3,2,1,0:T(8,128)(2,1)}), bf16[32,3,32,256]{3,2,1,0:T(8,128)(2,1)S(1)}, u32[]{:S(2)}, u32[]{:S(2)}) async-start(bf16[32,3,32,256]{3,2,1,0:T(8,128)(2,1)} %filter_transform.4), calls=%async_computation | async-start | bytes 3145728 | tf_op jit(solution)/shard_map/all_to_all | solution.py:372
  98.8 14.2 %filter_transform.5 = (bf16[32,3,24,768]{3,2,1,0:T(8,128)(2,1)}, bf16[32,3,8,768]{3,2,1,0:T(8,128)(2,1)}) custom-call(f32[1]{0:T(128)} %bitcast.refs_0_, s32[2]{0:T(128)} %pad_add_fusion.refs_1_, bf16[1024,4096]{1,0:T(8,128)(2,1)} %refs_2_.5, bf16[256,6144]{1,0:T(8,128)(2,1)} %collective-permute-done.10.refs_3_, ...), custom_call_target="tpu_custom_call" | custom-call | flops 4831838208 | bytes 33554432 | tf_op jit(solution)/shard_map/filter_transform/pallas_call | solution.py:134
  112.9 23.6 %all-to-all-done.refs_8_ = bf16[32,3,32,256]{3,2,1,0:T(8,128)(2,1)S(1)} async-done(((bf16[32,3,32,256]{3,2,1,0:T(8,128)(2,1)}), bf16[32,3,32,256]{3,2,1,0:T(8,128)(2,1)S(1)}, u32[]{:S(2)}, u32[]{:S(2)}) %all-to-all-start) | async-done | bytes 1572896 | tf_op jit(solution)/shard_map/all_to_all | solution.py:372
  136.5 0.0 copy-start.1
  136.5 1.1 copy-done.1
  137.6 4.0 %all-to-all-start.1 = ((bf16[32,3,24,768]{3,2,1,0:T(8,128)(2,1)}), bf16[32,3,24,768]{3,2,1,0:T(8,128)(2,1)S(1)}, u32[]{:S(2)}, u32[]{:S(2)}) async-start(bf16[32,3,24,768]{3,2,1,0:T(8,128)(2,1)} %get-tuple-element.27), calls=%async_computation.1 | async-start | bytes 7077888 | tf_op jit(solution)/shard_map/all_to_all | solution.py:372
  141.6 1.1 fusion.2
  142.7 1.1 fusion.3
  143.8 1.1 fusion.4
  144.9 1.1 fusion.5
  146.1 0.1 collective-permute-start.3
  146.3 1.7 collective-permute-start.4
  148.0 0.2 collective-permute-start.5
  148.3 1.6 collective-permute-start.6
  149.9 0.2 collective-permute-start.7
  150.2 0.0 collective-permute-done.3.refs_1_.refs_3_
  150.2 0.0 copy-start.2
  150.2 2.6 %collective-permute-start.8 = (bf16[4,1,32,1024]{3,2,1,0:T(8,128)(2,1)S(1)}, bf16[4,1,32,1024]{3,2,1,0:T(8,128)(2,1)S(1)}, u32[]{:S(2)}, u32[]{:S(2)}) collective-permute-start(bf16[4,1,32,1024]{3,2,1,0:T(8,128)(2,1)S(1)} %pad_maximum_fusion.8), channel_id=1, source_target_pairs={{0,6},{1,7},{2,4},{3,5},{4,2},{5,3},{6,0},{7,1},{8,14},{9,15},{10,... | collective-permute-start | bytes 786440 | tf_op jit(solution)/shard_map/ppermute | solution.py:377
  152.9 20.0 %collective-permute-done.4.refs_2_.refs_4_ = bf16[4,1,32,1024]{3,2,1,0:T(8,128)(2,1)S(1)} collective-permute-done((bf16[4,1,32,1024]{3,2,1,0:T(8,128)(2,1)S(1)}, bf16[4,1,32,1024]{3,2,1,0:T(8,128)(2,1)S(1)}, u32[]{:S(2)}, u32[]{:S(2)}) %collective-permute-start.4) | collective-permute-done | bytes 262176 | tf_op jit(solution)/shard_map/ppermute | solution.py:377
  172.9 0.0 copy-start.3
  172.9 3.5 %collective-permute-start.9 = (bf16[4,1,32,1024]{3,2,1,0:T(8,128)(2,1)S(1)}, bf16[4,1,32,1024]{3,2,1,0:T(8,128)(2,1)S(1)}, u32[]{:S(2)}, u32[]{:S(2)}) collective-permute-start(bf16[4,1,32,1024]{3,2,1,0:T(8,128)(2,1)S(1)} %pad_maximum_fusion.9), channel_id=1, source_target_pairs={{0,7},{1,6},{2,5},{3,4},{4,3},{5,2},{6,1},{7,0},{8,15},{9,14},{10,... | collective-permute-start | bytes 786440 | tf_op jit(solution)/shard_map/ppermute | solution.py:377
  176.4 0.7 pad_maximum_fusion.2.refs_0_.refs_2_
  177.2 9.0 %collective-permute-done.5.refs_3_.refs_5_ = bf16[4,1,32,1024]{3,2,1,0:T(8,128)(2,1)S(1)} collective-permute-done((bf16[4,1,32,1024]{3,2,1,0:T(8,128)(2,1)S(1)}, bf16[4,1,32,1024]{3,2,1,0:T(8,128)(2,1)S(1)}, u32[]{:S(2)}, u32[]{:S(2)}) %collective-permute-start.5) | collective-permute-done | bytes 262176 | tf_op jit(solution)/shard_map/ppermute | solution.py:377
  186.2 0.0 copy-start.4
  186.2 0.0 collective-permute-done.6.refs_4_.refs_6_
  186.2 0.0 copy-start.5
  186.2 0.0 collective-permute-done.7.refs_5_.refs_7_
  186.2 0.0 copy-start.6
  186.2 9.5 %collective-permute-done.8.refs_6_.refs_8_ = bf16[4,1,32,1024]{3,2,1,0:T(8,128)(2,1)S(1)} collective-permute-done((bf16[4,1,32,1024]{3,2,1,0:T(8,128)(2,1)S(1)}, bf16[4,1,32,1024]{3,2,1,0:T(8,128)(2,1)S(1)}, u32[]{:S(2)}, u32[]{:S(2)}) %collective-permute-start.8) | collective-permute-done | bytes 262176 | tf_op jit(solution)/shard_map/ppermute | solution.py:377
  195.8 0.0 copy-start.7
  195.8 5.2 %collective-permute-done.9.refs_7_.refs_9_ = bf16[4,1,32,1024]{3,2,1,0:T(8,128)(2,1)S(1)} collective-permute-done((bf16[4,1,32,1024]{3,2,1,0:T(8,128)(2,1)S(1)}, bf16[4,1,32,1024]{3,2,1,0:T(8,128)(2,1)S(1)}, u32[]{:S(2)}, u32[]{:S(2)}) %collective-permute-start.9) | collective-permute-done | bytes 262176 | tf_op jit(solution)/shard_map/ppermute | solution.py:377
  200.9 0.0 copy-done.2
  200.9 0.0 copy-done.3
  200.9 0.0 copy-done.4
  200.9 0.0 copy-done.5
  200.9 0.0 copy-done.6
  201.0 0.0 copy-done.7
  201.0 0.0 copy-start.8
  201.0 0.7 copy-done.8
  201.7 5.0 %regroup.1 = (bf16[16,256,256]{2,1,0:T(8,128)(2,1)}, bf16[16,256,256]{2,1,0:T(8,128)(2,1)}) custom-call(bf16[4,1,32,1024]{3,2,1,0:T(8,128)(2,1)} %pad_maximum_fusion.2.refs_0_.refs_2_, bf16[4,1,32,1024]{3,2,1,0:T(8,128)(2,1)} %copy-done.2, bf16[4,1,32,1024]{3,2,1,0:T(8,128)(2,1)} %copy-done.3, bf16[4,1,32,1024]{3,2,1,0:T(8,128)(2,1)} %copy-done.4, ...), custom_call_target="tpu_custom_call" | custom-call | bytes 6291456 | tf_op jit(solution)/shard_map/regroup/pallas_call | solution.py:201
  206.6 7.4 %correlate_last.1.refs_11_ = f32[16,1024,1024]{2,1,0:T(8,128)} custom-call(bf16[16,256,256]{2,1,0:T(8,128)(2,1)} %get-tuple-element.23.wide_ref.refs_0_, bf16[16,256,256]{2,1,0:T(8,128)(2,1)} %get-tuple-element.24.tall_ref.refs_1_), custom_call_target="tpu_custom_call" | custom-call | flops 536870912 | bytes 8388608 | tf_op jit(solution)/shard_map/correlate_last/pallas_call | solution.py:255
  214.1 7.5 %all-to-all-done.1.refs_10_ = bf16[32,3,24,768]{3,2,1,0:T(8,128)(2,1)S(1)} async-done(((bf16[32,3,24,768]{3,2,1,0:T(8,128)(2,1)}), bf16[32,3,24,768]{3,2,1,0:T(8,128)(2,1)S(1)}, u32[]{:S(2)}, u32[]{:S(2)}) %all-to-all-start.1) | async-done | bytes 3538976 | tf_op jit(solution)/shard_map/all_to_all | solution.py:372
  221.6 3.8 %all-to-all-start.2 = ((bf16[32,3,8,768]{3,2,1,0:T(8,128)(2,1)}), bf16[32,3,8,768]{3,2,1,0:T(8,128)(2,1)}, u32[]{:S(2)}, u32[]{:S(2)}) async-start(bf16[32,3,8,768]{3,2,1,0:T(8,128)(2,1)} %get-tuple-element.28), calls=%async_computation.2 | async-start | bytes 2359296 | tf_op jit(solution)/shard_map/all_to_all | solution.py:372
  225.4 0.0 copy-done
  225.4 20.8 %correlate_rest.2.refs_11_ = f32[16,1024,1024]{2,1,0:T(8,128)} custom-call(bf16[16,256,256]{2,1,0:T(8,128)(2,1)} %get-tuple-element.23.wide_ref.refs_0_, bf16[16,256,256]{2,1,0:T(8,128)(2,1)} %get-tuple-element.24.tall_ref.refs_1_, bf16[4,1,32,1024]{3,2,1,0:T(8,128)(2,1)} %pad_maximum_fusion.2.refs_0_.refs_2_, ...), custom_call_target="tpu_custom_call", output_to_operand_aliasing={{}: (11, {})} | custom-call | flops 6039797760 | bytes 56623104 | tf_op jit(solution)/shard_map/correlate_rest/pallas_call | solution.py:349
  246.2 8.3 %all-to-all-done.2.refs_10_ = bf16[32,3,8,768]{3,2,1,0:T(8,128)(2,1)} async-done(((bf16[32,3,8,768]{3,2,1,0:T(8,128)(2,1)}), bf16[32,3,8,768]{3,2,1,0:T(8,128)(2,1)}, u32[]{:S(2)}, u32[]{:S(2)}) %all-to-all-start.2) | async-done | bytes 1179680 | tf_op jit(solution)/shard_map/all_to_all | solution.py:372
  254.4 9.0 %correlate_rest.3 = f32[16,1024,1024]{2,1,0:T(8,128)} custom-call(bf16[16,256,256]{2,1,0:T(8,128)(2,1)} %get-tuple-element.23.wide_ref.refs_0_, bf16[16,256,256]{2,1,0:T(8,128)(2,1)} %get-tuple-element.24.tall_ref.refs_1_, bf16[4,1,32,1024]{3,2,1,0:T(8,128)(2,1)} %pad_maximum_fusion.2.refs_0_.refs_2_, ...), custom_call_target="tpu_custom_call", output_to_operand_aliasing={{}: (11, {})} | custom-call | flops 2013265920 | bytes 18874368 | tf_op jit(solution)/shard_map/correlate_rest/pallas_call | solution.py:349
  (8 shorter events, 0.3 us)
Async XLA Ops:
  4.8 22.6 %collective-permute-start.10 = (bf16[256,6144]{1,0:T(8,128)(2,1)S(1)}, bf16[256,6144]{1,0:T(8,128)(2,1)}, u32[]{:S(2)}, u32[]{:S(2)}) collective-permute-start(bf16[256,6144]{1,0:T(8,128)(2,1)S(1)} %pad_maximum_fusion), channel_id=1, source_target_pairs={{0,1},{1,2},{2,3},{3,4},{4,5},{5,6},{6,7},{7,8},{8,9},{9,10},{10,1... | collective-permute-start | bytes 9437192 | tf_op jit(solution)/shard_map/ppermute | solution.py:24
  10.6 55.6 %collective-permute-start.11 = (bf16[256,6144]{1,0:T(8,128)(2,1)}, bf16[256,6144]{1,0:T(8,128)(2,1)}, u32[]{:S(2)}, u32[]{:S(2)}) collective-permute-start(bf16[256,6144]{1,0:T(8,128)(2,1)} %pad_maximum_fusion.1), channel_id=1, source_target_pairs={{0,31},{1,0},{2,1},{3,2},{4,3},{5,4},{6,5},{7,6},{8,7},{9,8},{10,9... | collective-permute-start | bytes 9437192 | tf_op jit(solution)/shard_map/ppermute | solution.py:29
  23.0 50.2 %collective-permute-start = (bf16[8,1,32,1024]{3,2,1,0:T(8,128)(2,1)}, bf16[8,1,32,1024]{3,2,1,0:T(8,128)(2,1)}, u32[]{:S(2)}, u32[]{:S(2)}) collective-permute-start(bf16[8,1,32,1024]{3,2,1,0:T(8,128)(2,1)} %get-tuple-element.19), channel_id=1, source_target_pairs={{0,8},{1,9},{2,10},{3,11},{4,12},{5,13},{6,14},{7,15},{8,0},{9,1},... | collective-permute-start | bytes 1572872 | tf_op jit(solution)/shard_map/ppermute | solution.py:377
  23.8 67.2 %collective-permute-start.1 = (bf16[8,1,32,1024]{3,2,1,0:T(8,128)(2,1)}, bf16[8,1,32,1024]{3,2,1,0:T(8,128)(2,1)}, u32[]{:S(2)}, u32[]{:S(2)}) collective-permute-start(bf16[8,1,32,1024]{3,2,1,0:T(8,128)(2,1)} %get-tuple-element.20), channel_id=1, source_target_pairs={{0,16},{1,17},{2,18},{3,19},{4,20},{5,21},{6,22},{7,23},{8,24},{9,... | collective-permute-start | bytes 1572872 | tf_op jit(solution)/shard_map/ppermute | solution.py:377
  26.4 64.7 %collective-permute-start.2 = (bf16[8,1,32,1024]{3,2,1,0:T(8,128)(2,1)}, bf16[8,1,32,1024]{3,2,1,0:T(8,128)(2,1)}, u32[]{:S(2)}, u32[]{:S(2)}) collective-permute-start(bf16[8,1,32,1024]{3,2,1,0:T(8,128)(2,1)} %get-tuple-element.21), channel_id=1, source_target_pairs={{0,24},{1,25},{2,26},{3,27},{4,28},{5,29},{6,30},{7,31},{8,16},{9,... | collective-permute-start | bytes 1572872 | tf_op jit(solution)/shard_map/ppermute | solution.py:377
  91.1 45.4 %all-to-all-start = ((bf16[32,3,32,256]{3,2,1,0:T(8,128)(2,1)}), bf16[32,3,32,256]{3,2,1,0:T(8,128)(2,1)S(1)}, u32[]{:S(2)}, u32[]{:S(2)}) async-start(bf16[32,3,32,256]{3,2,1,0:T(8,128)(2,1)} %filter_transform.4), calls=%async_computation | async-start | bytes 3145728 | tf_op jit(solution)/shard_map/all_to_all | solution.py:372
  136.5 1.1 copy-start.1
  137.6 84.0 %all-to-all-start.1 = ((bf16[32,3,24,768]{3,2,1,0:T(8,128)(2,1)}), bf16[32,3,24,768]{3,2,1,0:T(8,128)(2,1)S(1)}, u32[]{:S(2)}, u32[]{:S(2)}) async-start(bf16[32,3,24,768]{3,2,1,0:T(8,128)(2,1)} %get-tuple-element.27), calls=%async_computation.1 | async-start | bytes 7077888 | tf_op jit(solution)/shard_map/all_to_all | solution.py:372
  146.1 4.1 %collective-permute-start.3 = (bf16[4,1,32,1024]{3,2,1,0:T(8,128)(2,1)S(1)}, bf16[4,1,32,1024]{3,2,1,0:T(8,128)(2,1)S(1)}, u32[]{:S(2)}, u32[]{:S(2)}) collective-permute-start(bf16[4,1,32,1024]{3,2,1,0:T(8,128)(2,1)S(1)} %pad_maximum_fusion.3), channel_id=1, source_target_pairs={{0,1},{1,0},{2,3},{3,2},{4,5},{5,4},{6,7},{7,6},{8,9},{9,8},{10,11... | collective-permute-start | bytes 786440 | tf_op jit(solution)/shard_map/ppermute | solution.py:377
  146.3 26.6 %collective-permute-start.4 = (bf16[4,1,32,1024]{3,2,1,0:T(8,128)(2,1)S(1)}, bf16[4,1,32,1024]{3,2,1,0:T(8,128)(2,1)S(1)}, u32[]{:S(2)}, u32[]{:S(2)}) collective-permute-start(bf16[4,1,32,1024]{3,2,1,0:T(8,128)(2,1)S(1)} %pad_maximum_fusion.4), channel_id=1, source_target_pairs={{0,2},{1,3},{2,0},{3,1},{4,6},{5,7},{6,4},{7,5},{8,10},{9,11},{10,... | collective-permute-start | bytes 786440 | tf_op jit(solution)/shard_map/ppermute | solution.py:377
  148.0 38.2 %collective-permute-start.5 = (bf16[4,1,32,1024]{3,2,1,0:T(8,128)(2,1)S(1)}, bf16[4,1,32,1024]{3,2,1,0:T(8,128)(2,1)S(1)}, u32[]{:S(2)}, u32[]{:S(2)}) collective-permute-start(bf16[4,1,32,1024]{3,2,1,0:T(8,128)(2,1)S(1)} %pad_maximum_fusion.5), channel_id=1, source_target_pairs={{0,3},{1,2},{2,1},{3,0},{4,7},{5,6},{6,5},{7,4},{8,11},{9,10},{10,... | collective-permute-start | bytes 786440 | tf_op jit(solution)/shard_map/ppermute | solution.py:377
  148.3 37.9 %collective-permute-start.6 = (bf16[4,1,32,1024]{3,2,1,0:T(8,128)(2,1)S(1)}, bf16[4,1,32,1024]{3,2,1,0:T(8,128)(2,1)S(1)}, u32[]{:S(2)}, u32[]{:S(2)}) collective-permute-start(bf16[4,1,32,1024]{3,2,1,0:T(8,128)(2,1)S(1)} %pad_maximum_fusion.6), channel_id=1, source_target_pairs={{0,4},{1,5},{2,6},{3,7},{4,0},{5,1},{6,2},{7,3},{8,12},{9,13},{10,... | collective-permute-start | bytes 786440 | tf_op jit(solution)/shard_map/ppermute | solution.py:377
  149.9 36.3 %collective-permute-start.7 = (bf16[4,1,32,1024]{3,2,1,0:T(8,128)(2,1)S(1)}, bf16[4,1,32,1024]{3,2,1,0:T(8,128)(2,1)S(1)}, u32[]{:S(2)}, u32[]{:S(2)}) collective-permute-start(bf16[4,1,32,1024]{3,2,1,0:T(8,128)(2,1)S(1)} %pad_maximum_fusion.7), channel_id=1, source_target_pairs={{0,5},{1,4},{2,7},{3,6},{4,1},{5,0},{6,3},{7,2},{8,13},{9,12},{10,... | collective-permute-start | bytes 786440 | tf_op jit(solution)/shard_map/ppermute | solution.py:377
  150.2 50.7 %copy-start.2 = (bf16[4,1,32,1024]{3,2,1,0:T(8,128)(2,1)}, bf16[4,1,32,1024]{3,2,1,0:T(8,128)(2,1)S(1)}, u32[]{:S(2)}) copy-start(bf16[4,1,32,1024]{3,2,1,0:T(8,128)(2,1)S(1)} %collective-permute-done.3.refs_1_.refs_3_) | copy-start | bytes 786436
  150.2 45.5 %collective-permute-start.8 = (bf16[4,1,32,1024]{3,2,1,0:T(8,128)(2,1)S(1)}, bf16[4,1,32,1024]{3,2,1,0:T(8,128)(2,1)S(1)}, u32[]{:S(2)}, u32[]{:S(2)}) collective-permute-start(bf16[4,1,32,1024]{3,2,1,0:T(8,128)(2,1)S(1)} %pad_maximum_fusion.8), channel_id=1, source_target_pairs={{0,6},{1,7},{2,4},{3,5},{4,2},{5,3},{6,0},{7,1},{8,14},{9,15},{10,... | collective-permute-start | bytes 786440 | tf_op jit(solution)/shard_map/ppermute | solution.py:377
  172.9 28.0 %copy-start.3 = (bf16[4,1,32,1024]{3,2,1,0:T(8,128)(2,1)}, bf16[4,1,32,1024]{3,2,1,0:T(8,128)(2,1)S(1)}, u32[]{:S(2)}) copy-start(bf16[4,1,32,1024]{3,2,1,0:T(8,128)(2,1)S(1)} %collective-permute-done.4.refs_2_.refs_4_) | copy-start | bytes 786436
  172.9 28.0 %collective-permute-start.9 = (bf16[4,1,32,1024]{3,2,1,0:T(8,128)(2,1)S(1)}, bf16[4,1,32,1024]{3,2,1,0:T(8,128)(2,1)S(1)}, u32[]{:S(2)}, u32[]{:S(2)}) collective-permute-start(bf16[4,1,32,1024]{3,2,1,0:T(8,128)(2,1)S(1)} %pad_maximum_fusion.9), channel_id=1, source_target_pairs={{0,7},{1,6},{2,5},{3,4},{4,3},{5,2},{6,1},{7,0},{8,15},{9,14},{10,... | collective-permute-start | bytes 786440 | tf_op jit(solution)/shard_map/ppermute | solution.py:377
  186.2 14.7 %copy-start.4 = (bf16[4,1,32,1024]{3,2,1,0:T(8,128)(2,1)}, bf16[4,1,32,1024]{3,2,1,0:T(8,128)(2,1)S(1)}, u32[]{:S(2)}) copy-start(bf16[4,1,32,1024]{3,2,1,0:T(8,128)(2,1)S(1)} %collective-permute-done.5.refs_3_.refs_5_) | copy-start | bytes 786436
  186.2 14.7 %copy-start.5 = (bf16[4,1,32,1024]{3,2,1,0:T(8,128)(2,1)}, bf16[4,1,32,1024]{3,2,1,0:T(8,128)(2,1)S(1)}, u32[]{:S(2)}) copy-start(bf16[4,1,32,1024]{3,2,1,0:T(8,128)(2,1)S(1)} %collective-permute-done.6.refs_4_.refs_6_) | copy-start | bytes 786436
  186.2 14.7 %copy-start.6 = (bf16[4,1,32,1024]{3,2,1,0:T(8,128)(2,1)}, bf16[4,1,32,1024]{3,2,1,0:T(8,128)(2,1)S(1)}, u32[]{:S(2)}) copy-start(bf16[4,1,32,1024]{3,2,1,0:T(8,128)(2,1)S(1)} %collective-permute-done.7.refs_5_.refs_7_) | copy-start | bytes 786436
  195.8 5.2 %copy-start.7 = (bf16[4,1,32,1024]{3,2,1,0:T(8,128)(2,1)}, bf16[4,1,32,1024]{3,2,1,0:T(8,128)(2,1)S(1)}, u32[]{:S(2)}) copy-start(bf16[4,1,32,1024]{3,2,1,0:T(8,128)(2,1)S(1)} %collective-permute-done.8.refs_6_.refs_8_) | copy-start | bytes 786436
  201.0 0.7 copy-start.8
  221.6 3.8 %copy-start = (bf16[32,3,24,768]{3,2,1,0:T(8,128)(2,1)}, bf16[32,3,24,768]{3,2,1,0:T(8,128)(2,1)S(1)}, u32[]{:S(2)}) copy-start(bf16[32,3,24,768]{3,2,1,0:T(8,128)(2,1)S(1)} %all-to-all-done.1.refs_10_) | copy-start | bytes 10616836
  221.6 32.8 %all-to-all-start.2 = ((bf16[32,3,8,768]{3,2,1,0:T(8,128)(2,1)}), bf16[32,3,8,768]{3,2,1,0:T(8,128)(2,1)}, u32[]{:S(2)}, u32[]{:S(2)}) async-start(bf16[32,3,8,768]{3,2,1,0:T(8,128)(2,1)} %get-tuple-element.28), calls=%async_computation.2 | async-start | bytes 2359296 | tf_op jit(solution)/shard_map/all_to_all | solution.py:372

commit v5 on v4

--- a/solution.py
+++ b/solution.py
@@ -174,49 +174,6 @@
     return depth, pltpu.VMEM((lanes // LANES, depth * pitch_of(arrays[0].shape[2]), LANES), jnp.float32)
 
 
-def regroup_kernel(rolled, *refs):
-    sources = len(rolled)
-    wide_ref, tall_ref, scratch = refs[sources:]
-    rows = refs[0].shape[2]
-    depth = wide_ref.shape[1] // 2
-    spread(refs[:sources], rolled, scratch)
-    for channel in range(rows // 2):
-        for part in range(2):
-            deep = slice(part * depth, (part + 1) * depth)
-            for tile in range(scratch.shape[0]):
-                across = slice(tile * LANES, (tile + 1) * LANES)
-                values = scratch[tile, pl.ds(2 * channel + part, depth, stride=pitch_of(rows)), :]
-                wide_ref[channel, deep, across] = values.astype(jnp.bfloat16)
-                tall_ref[channel, across, deep] = values.T.astype(jnp.bfloat16)
-
-
-def regroup(arrays, begins, rolled, inputs, block):
-    rows = arrays[0].shape[2]
-    channels = rows // 2
-    depth, scratch = spread_shape(arrays, block)
-    in_specs = [
-        pl.BlockSpec((*a.shape[:3], block), functools.partial(lambda b, i: (0, 0, 0, i + b), b))
-        for a, b in zip(arrays, begins)
-    ]
-    return pl.pallas_call(
-        functools.partial(regroup_kernel, rolled),
-        grid=(inputs // block,),
-        in_specs=in_specs,
-        out_specs=[
-            pl.BlockSpec((channels, 2 * depth, block), lambda i: (0, 0, i)),
-            pl.BlockSpec((channels, block, 2 * depth), lambda i: (0, i, 0)),
-        ],
-        out_shape=[
-            jax.ShapeDtypeStruct((channels, 2 * depth, inputs), jnp.bfloat16),
-            jax.ShapeDtypeStruct((channels, inputs, 2 * depth), jnp.bfloat16),
-        ],
-        scratch_shapes=[scratch],
-        compiler_params=pltpu.CompilerParams(vmem_limit_bytes=VMEM_LIMIT),
-        cost_estimate=cost(0, 6 * depth * rows * inputs),
-        name="regroup",
-    )(*arrays)
-
-
 def packed_square(scale, block, wide, tall, store):
     half = wide.shape[0] // 2
     inputs = wide.shape[1]
@@ -240,46 +197,12 @@
     return jnp.concatenate([rows[:, half:], -rows[:, :half]], 1)
 
 
-def correlate_last_kernel(scale, block, wide_ref, tall_ref, out_ref):
-    for channel in range(out_ref.shape[0]):
-
-        def store(row, col, values, channel=channel):
-            height, width = values.shape
-            out_ref[channel, row : row + height, col : col + width] = values
-
-        packed_square(scale, block, wide_ref[channel], tall_ref[channel], store)
-
-
-def correlate_last(wide, tall, block, total, spectra_count):
-    channels, depth, inputs = wide.shape
-    return pl.pallas_call(
-        functools.partial(correlate_last_kernel, 1.0 / spectra_count, block),
-        grid=(channels // 2,),
-        in_specs=[
-            pl.BlockSpec((2, depth, inputs), lambda c: (c, 0, 0)),
-            pl.BlockSpec((2, inputs, depth), lambda c: (c, 0, 0)),
-        ],
-        out_specs=pl.BlockSpec((2, inputs, inputs), lambda c: (c, total // inputs - 1, total // inputs - 1)),
-        out_shape=jax.ShapeDtypeStruct((channels, total, total), jnp.float32),
-        compiler_params=pltpu.CompilerParams(vmem_limit_bytes=VMEM_LIMIT),
-        cost_estimate=cost(
-            2 * channels * depth * inputs * inputs, channels * inputs * (4 * depth + 4 * inputs)
-        ),
-        name="correlate_last",
-    )(wide, tall)
-
-
-def correlate_rest_kernel(scale, block, first_channel, rolled, *refs):
+def correlate_kernel(scale, block, first_channel, rolled, *refs):
     sources = len(rolled)
-    wide_ref, tall_ref = refs[:2]
-    spectra_refs = refs[2 : 2 + sources]
-    out_ref, *scratches, above, corner, sems = refs[3 + sources :]
-    sets = spectra_refs[:-1], spectra_refs[-1:]
+    sets = refs[: sources - 1], refs[sources - 1 : sources]
+    out_ref, *scratches, square, sems = refs[-5:]
     heights = [refs_of[0].shape[2] for refs_of in sets]
     firsts = first_channel, 0
-    depth = wide_ref.shape[1] // 2
-    after = wide_ref.shape[2]
-    inputs = above.shape[1]
     step = pl.program_id(0)
     slot = step % 2
 
@@ -296,76 +219,62 @@
             pieces.append(scratch[tile, pl.ds(start, scratch.shape[1] // pitch, stride=pitch), :])
         return jnp.concatenate(pieces, 0)
 
-    def copies(slot, channel):
-        return (
-            pltpu.make_async_copy(
-                above.at[slot], out_ref.at[channel, pl.ds(0, inputs), :], sems.at[slot, 0]
-            ),
-            pltpu.make_async_copy(
-                corner.at[slot], out_ref.at[channel, pl.ds(inputs, after), pl.ds(0, inputs)], sems.at[slot, 1]
-            ),
-        )
+    def copy(slot, step):
+        return pltpu.make_async_copy(square.at[slot], out_ref.at[first_channel + step], sems.at[slot])
 
     @pl.when(step >= 2)
     def _():
-        for copy in copies(slot, first_channel + step - 2):
-            copy.wait()
+        copy(slot, step - 2).wait()
 
     parts = [[values(tile, part) for tile in range(scratches[0].shape[0])] for part in range(2)]
     wide = jnp.concatenate([jnp.concatenate(p, 1) for p in parts], 0).astype(jnp.bfloat16)
     tall = jnp.concatenate([jnp.concatenate([t.T for t in p], 0) for p in parts], 1).astype(jnp.bfloat16)
 
-    above[slot, :, inputs:] = jnp.dot(tall, wide_ref[0], preferred_element_type=jnp.float32) * scale
-    im_rows = imaginary_rows(tall_ref[0], depth)
-    corner[slot] = jnp.dot(im_rows, wide, preferred_element_type=jnp.float32) * scale
-
     def store(row, col, values):
         height, width = values.shape
-        above[slot, row : row + height, col : col + width] = values
+        square[slot, row : row + height, col : col + width] = values
 
     packed_square(scale, block, wide, tall, store)
-    for copy in copies(slot, first_channel + step):
-        copy.start()
+    copy(slot, step).start()
 
     @pl.when(step == pl.num_programs(0) - 1)
     def _():
-        for copy in copies(1 - slot, first_channel + step - 1):
-            copy.wait()
-        for copy in copies(slot, first_channel + step):
-            copy.wait()
-
-
-def correlate_rest(wide, tall, arrays, rolled, block, first_channel, spectra_count, out):
-    _, double, last = wide.shape
+        copy(1 - slot, step - 1).wait()
+        copy(slot, step).wait()
+
+
+def correlate(arrays, rolled, block, total_channels, first_channel, spectra_count, out=None):
     rows, inputs = arrays[-1].shape[2:]
     channels = rows // 2
-    in_specs = [
-        pl.BlockSpec((1, double, last), lambda c: (c + first_channel, 0, 0)),
-        pl.BlockSpec((1, last, double), lambda c: (c + first_channel, 0, 0)),
-    ]
-    in_specs += [pl.BlockSpec((*a.shape[:3], inputs), lambda c: (0, 0, 0, 0)) for a in arrays]
-    in_specs.append(pl.BlockSpec(memory_space=pl.ANY))
-    scratches = [spread_shape(some, inputs)[1] for some in (arrays[:-1], arrays[-1:])]
+    in_specs = [pl.BlockSpec(a.shape, lambda c: (0, 0, 0, 0)) for a in arrays]
+    args, aliases = list(arrays), {}
+    if out is not None:
+        in_specs.append(pl.BlockSpec(memory_space=pl.ANY))
+        aliases = {len(args): 0}
+        args.append(out)
+    scratches, depths = [], 0
+    for some in (arrays[:-1], arrays[-1:]):
+        depth, scratch = spread_shape(some, inputs)
+        scratches.append(scratch)
+        depths += depth
     return pl.pallas_call(
-        functools.partial(correlate_rest_kernel, 1.0 / spectra_count, block, first_channel, rolled),
+        functools.partial(correlate_kernel, 1.0 / spectra_count, block, first_channel, rolled),
         grid=(channels,),
         in_specs=in_specs,
         out_specs=pl.BlockSpec(memory_space=pl.ANY),
-        out_shape=jax.ShapeDtypeStruct(out.shape, out.dtype),
+        out_shape=jax.ShapeDtypeStruct((total_channels, inputs, inputs), jnp.float32),
         scratch_shapes=[
             *scratches,
-            pltpu.VMEM((2, inputs, inputs + last), jnp.float32),
-            pltpu.VMEM((2, last, inputs), jnp.float32),
-            pltpu.SemaphoreType.DMA((2, 2)),
+            pltpu.VMEM((2, inputs, inputs), jnp.float32),
+            pltpu.SemaphoreType.DMA((2,)),
         ],
-        input_output_aliases={2 + len(arrays): 0},
+        input_output_aliases=aliases,
         compiler_params=pltpu.CompilerParams(vmem_limit_bytes=VMEM_LIMIT),
         cost_estimate=cost(
-            2 * channels * double * inputs * (2 * last + inputs),
-            channels * inputs * (4 * double + 8 * last + 4 * inputs),
+            4 * channels * depths * inputs * inputs, channels * inputs * (4 * depths + 4 * inputs)
         ),
-        name="correlate_rest",
-    )(wide, tall, *arrays, out)
+        name="correlate",
+    )(*args)
 
 
 def turn(block):
@@ -398,11 +307,7 @@
     place = jnp.stack([me // PLANE, me % PLANE]).astype(jnp.int32)
     own = {f: (0, f) for f in range(local)}
     inner = [(tuple(range(past, local)), own)]
-    groups = [3], [0, 1, 2]
-    rolled = [
-        (((0,),) * (local - past),) * PLANE + (((0,), tuple(int(later[b] == 2) for b in some), (0,)),)
-        for some in groups
-    ]
+    rolled = (((0,),) * (local - past),) * PLANE + (((0,), tuple(int(b == 2) for b in later), (0,)),)
 
     def around(some):
         ahead, back, variants = [], [], []
@@ -427,27 +332,19 @@
             arrays, begins, variants, local, follows, place, tap_weights, table, devices, splits, planes, rows, block
         )
 
-    whole = [2 * channels]
     shares = [channels - channels // 4, channels // 4]
-    sent, variants = around([3, 0, 1, 2])
+    sent, variants = around(range(blocks))
     arounds = neighbours(*sent)
-    inner_blocks = spectra([voltage], [0], inner, whole, inputs, devices // PLANE)
+    inner_blocks = spectra([voltage], [0], inner, [2 * channels], inputs, devices // PLANE)
     arrived = [b if k == 0 else exchanged(b, k * PLANE) for k, b in enumerate(inner_blocks)]
-    first = spectra([voltage, *arounds], [3, 0, 0], variants[:1], whole, block)[0]
-    turned = turn(after(first, arrived))
+    parts = spectra([voltage, *arounds], [0, 0, 0], variants, [2 * c for c in shares], inputs)
+    first_turned = turn(after(parts[0], arrived))
     stacks = [jnp.concatenate([a[j : j + 1] for a in arrived], 0) for j in range(PLANE)]
     inner_turned = [s if j == 0 else exchanged(s, j) for j, s in enumerate(stacks)]
-    parts = spectra([voltage, *arounds], [0, 0, 0], variants[1:], [2 * c for c in shares], inputs - block)
-    wide, tall = regroup([*inner_turned, turned], [3] * PLANE + [0], rolled[0], block, block)
-    result = correlate_last(wide, tall, block, inputs, count)
-    first_turned = turn(after(parts[0], turned))
-    part, result, first_turned = lax.optimization_barrier((parts[1], result, first_turned))
-    second_turned = turn(part)
-    begin = 0
+    second_turned = turn(after(parts[1], (first_turned, inner_turned)))
+    result, begin = None, 0
     for share, turned in zip(shares, (first_turned, second_turned)):
-        result = correlate_rest(
-            wide, tall, [*inner_turned, turned], rolled[1], block, begin, count, result
-        )
+        result = correlate([*inner_turned, turned], rolled, block, channels, begin, count, result)
         begin += share
     return result
 
@@ -505,7 +402,7 @@
     out_specs = P("chan", "tile", None)
     devices = mesh.shape["chan"]
     planes = devices // PLANE
-    fits = devices == planes * PLANE and planes and planes & (planes - 1) == 0
+    fits = devices == planes * PLANE and planes and planes & (planes - 1) == 0 and CHAN // devices % 16 == 0
     body = per_device if mesh.shape["tile"] == 1 and fits else per_device_tiled
     return jax.shard_map(
         body, mesh=mesh, in_specs=in_specs, out_specs=out_specs, check_vma=False

time: 265 us -> 260 us (0.981)
  Pallas kernels: 70.9 us -> 58.1 us
  waiting for transfers between devices: 140 us -> 152 us
    pallas_call x4 -> x2, Pallas kernels: 42.2 us -> 33.1 us  [correlate(): pl.pallas_call(functools.partial(correlate_kernel, 1.0 / spectra_count, b...]
    all_to_all x3 -> x2, waiting for transfers between devices: 39.4 us -> 48.2 us  [turn(): lax.all_to_all(block, 'chan', split_axis=0, concat_axis=0, tiled=True)]
    pallas_call x3 -> x2, Pallas kernels: 28.7 us -> 25 us  [filter_transform(): pl.pallas_call(functools.partial(filter_transform_kernel, variants, local...]
    ppermute x10, waiting for transfers between devices: 62 us -> 64.8 us  [exchanged(): return lax.ppermute(block, 'chan', route)]
    all_to_all x3 -> x2, starting transfers between devices: 15.4 us -> 13.7 us  [turn(): lax.all_to_all(block, 'chan', split_axis=0, concat_axis=0, tiled=True)]
  transfers between devices with their start and end apart: 15 -> 14, of which waited for: 10 -> 8; matrix products, arithmetic and copies ran while one was open for 3% -> 3% of each run, Pallas kernels for 23% -> 19%
where the time goes in v5:
time: 260 us; the launch traced here: 259 us
  waiting for transfers between devices  152 us (58%)
  Pallas kernels  58.1 us (22%)
  starting transfers between devices  36 us (14%)
  local copies, waits for them, and re-layouts  9.03 us (3%)
  other arithmetic  3.78 us (1%)
    ppermute x10, waiting for transfers between devices, exchanged(): return lax.ppermute(block, 'chan', route)  64.8 us
    all_to_all x2, waiting for transfers between devices, turn(): lax.all_to_all(block, 'chan', split_axis=0, concat_axis=0, tiled=True)  48.2 us
    ppermute x1, waiting for transfers between devices, passed_back_round(): lax.ppermute(block, axis, [(i, (i - 1) % devices) for i in range(devices)])  38.9 us
    pallas_call x2, Pallas kernels, correlate(): pl.pallas_call(functools.partial(correlate_kernel, 1.0 / spectra_count, b...  33.1 us
    pallas_call x2, Pallas kernels, filter_transform(): pl.pallas_call(functools.partial(filter_transform_kernel, variants, local...  25 us
    ppermute x10, starting transfers between devices, exchanged(): return lax.ppermute(block, 'chan', route)  14.7 us
    all_to_all x2, starting transfers between devices, turn(): lax.all_to_all(block, 'chan', split_axis=0, concat_axis=0, tiled=True)  13.7 us
  transfers between devices with their start and end apart: 14, of which 8 were waited for; matrix products, arithmetic and copies ran while one was open for 3% of the time, Pallas kernels for 19%

profile of v5, /device:TPU:0, one launch (start us, length us, event | category | flops | bytes accessed | tf_op | source)
XLA Modules:
  0.0 259.1 jit_solution(3352510296755614295)
XLA Ops:
  0.0 1.7 fusion
  1.7 2.8 %fusion.1 = (bf16[256,2048]{1,0:T(8,128)(2,1)S(1)}, bf16[256,2048]{1,0:T(8,128)(2,1)S(1)}, bf16[256,2048]{1,0:T(8,128)(2,1)S(1)}, bf16[256,2048]{1,0:T(8,128)(2,1)S(1)}) fusion(bf16[1024,4096]{1,0:T(8,128)(2,1)} %refs_2_.3), kind=kLoop, calls=%fused_computation.12 | loop fusion | bytes 8388608 | tf_op jit(solution)/shard_map/slice | solution.py:322
  4.5 0.3 pad_maximum_fusion
  4.8 4.0 %collective-permute-start.10 = (bf16[256,6144]{1,0:T(8,128)(2,1)S(1)}, bf16[256,6144]{1,0:T(8,128)(2,1)}, u32[]{:S(2)}, u32[]{:S(2)}) collective-permute-start(bf16[256,6144]{1,0:T(8,128)(2,1)S(1)} %pad_maximum_fusion), channel_id=1, source_target_pairs={{0,1},{1,2},{2,3},{3,4},{4,5},{5,6},{6,7},{7,8},{8,9},{9,10},{10,1... | collective-permute-start | bytes 9437192 | tf_op jit(solution)/shard_map/ppermute | solution.py:24
  8.8 1.8 pad_maximum_fusion.1
  10.6 3.7 %collective-permute-start.11 = (bf16[256,6144]{1,0:T(8,128)(2,1)}, bf16[256,6144]{1,0:T(8,128)(2,1)}, u32[]{:S(2)}, u32[]{:S(2)}) collective-permute-start(bf16[256,6144]{1,0:T(8,128)(2,1)} %pad_maximum_fusion.1), channel_id=1, source_target_pairs={{0,31},{1,0},{2,1},{3,2},{4,3},{5,4},{6,5},{7,6},{8,7},{9,8},{10,9... | collective-permute-start | bytes 9437192 | tf_op jit(solution)/shard_map/ppermute | solution.py:29
  14.3 0.7 pad_add_fusion.refs_1_
  14.9 8.0 %filter_transform.2 = (bf16[8,1,32,1024]{3,2,1,0:T(8,128)(2,1)}, bf16[8,1,32,1024]{3,2,1,0:T(8,128)(2,1)}, bf16[8,1,32,1024]{3,2,1,0:T(8,128)(2,1)}, bf16[8,1,32,1024]{3,2,1,0:T(8,128)(2,1)}) custom-call(f32[1]{0:T(128)} %bitcast.refs_0_, s32[2]{0:T(128)} %pad_add_fusion.refs_1_, bf16[1024,4096]{1,0:T(8,128)(2,1)} %refs_2_.3, f32[4,1024]{1,0:T(4,128)} %refs_5_.1, ...), custom_call_target="tpu_custom_call" | custom-call | flops 2147483648 | bytes 12582912 | tf_op jit(solution)/shard_map/filter_transform/pallas_call | solution.py:134
  23.0 0.8 collective-permute-start
  23.8 2.6 collective-permute-start.1
  26.4 1.0 collective-permute-start.2
  27.4 0.0 collective-permute-done.10.refs_3_
  27.4 38.9 %collective-permute-done.11.refs_4_ = bf16[256,6144]{1,0:T(8,128)(2,1)} collective-permute-done((bf16[256,6144]{1,0:T(8,128)(2,1)}, bf16[256,6144]{1,0:T(8,128)(2,1)}, u32[]{:S(2)}, u32[]{:S(2)}) %collective-permute-start.11) | collective-permute-done | bytes 3145760 | tf_op jit(solution)/shard_map/ppermute | solution.py:29
  66.2 17.0 %filter_transform.3 = (bf16[32,3,24,1024]{3,2,1,0:T(8,128)(2,1)}, bf16[32,3,8,1024]{3,2,1,0:T(8,128)(2,1)}) custom-call(f32[1]{0:T(128)} %bitcast.refs_0_, s32[2]{0:T(128)} %pad_add_fusion.refs_1_, bf16[1024,4096]{1,0:T(8,128)(2,1)} %refs_2_.3, bf16[256,6144]{1,0:T(8,128)(2,1)} %collective-permute-done.10.refs_3_, ...), custom_call_target="tpu_custom_call" | custom-call | flops 6442450944 | bytes 41943040 | tf_op jit(solution)/shard_map/filter_transform/pallas_call | solution.py:134
  83.2 0.0 copy-start.8
  83.2 0.0 collective-permute-done
  83.2 7.8 %collective-permute-done.1 = bf16[8,1,32,1024]{3,2,1,0:T(8,128)(2,1)} collective-permute-done((bf16[8,1,32,1024]{3,2,1,0:T(8,128)(2,1)}, bf16[8,1,32,1024]{3,2,1,0:T(8,128)(2,1)}, u32[]{:S(2)}, u32[]{:S(2)}) %collective-permute-start.1) | collective-permute-done | bytes 524320 | tf_op jit(solution)/shard_map/ppermute | solution.py:286
  91.0 0.0 collective-permute-done.2
  91.0 10.0 %all-to-all-start = ((bf16[32,3,24,1024]{3,2,1,0:T(8,128)(2,1)}), bf16[32,3,24,1024]{3,2,1,0:T(8,128)(2,1)}, u32[]{:S(2)}, u32[]{:S(2)}) async-start(bf16[32,3,24,1024]{3,2,1,0:T(8,128)(2,1)} %get-tuple-element.19), calls=%async_computation | async-start | bytes 9437184 | tf_op jit(solution)/shard_map/all_to_all | solution.py:281
  101.0 0.0 copy-done.8
  101.1 1.1 fusion.3
  102.2 1.1 fusion.4
  103.3 1.1 fusion.5
  104.5 0.3 collective-permute-start.3
  104.8 1.7 collective-permute-start.4
  106.6 0.1 collective-permute-start.5
  106.7 1.7 collective-permute-start.6
  108.5 0.2 collective-permute-start.7
  108.7 0.0 collective-permute-done.3.refs_1_
  108.8 0.0 copy-start.1
  108.8 2.6 %collective-permute-start.8 = (bf16[4,1,32,1024]{3,2,1,0:T(8,128)(2,1)S(1)}, bf16[4,1,32,1024]{3,2,1,0:T(8,128)(2,1)S(1)}, u32[]{:S(2)}, u32[]{:S(2)}) collective-permute-start(bf16[4,1,32,1024]{3,2,1,0:T(8,128)(2,1)S(1)} %pad_maximum_fusion.8), channel_id=1, source_target_pairs={{0,6},{1,7},{2,4},{3,5},{4,2},{5,3},{6,0},{7,1},{8,14},{9,15},{10,... | collective-permute-start | bytes 786440 | tf_op jit(solution)/shard_map/ppermute | solution.py:286
  111.4 28.7 %collective-permute-done.4.refs_2_ = bf16[4,1,32,1024]{3,2,1,0:T(8,128)(2,1)S(1)} collective-permute-done((bf16[4,1,32,1024]{3,2,1,0:T(8,128)(2,1)S(1)}, bf16[4,1,32,1024]{3,2,1,0:T(8,128)(2,1)S(1)}, u32[]{:S(2)}, u32[]{:S(2)}) %collective-permute-start.4) | collective-permute-done | bytes 262176 | tf_op jit(solution)/shard_map/ppermute | solution.py:286
  140.1 0.0 copy-start.2
  140.1 3.6 %collective-permute-start.9 = (bf16[4,1,32,1024]{3,2,1,0:T(8,128)(2,1)S(1)}, bf16[4,1,32,1024]{3,2,1,0:T(8,128)(2,1)S(1)}, u32[]{:S(2)}, u32[]{:S(2)}) collective-permute-start(bf16[4,1,32,1024]{3,2,1,0:T(8,128)(2,1)S(1)} %pad_maximum_fusion.9), channel_id=1, source_target_pairs={{0,7},{1,6},{2,5},{3,4},{4,3},{5,2},{6,1},{7,0},{8,15},{9,14},{10,... | collective-permute-start | bytes 786440 | tf_op jit(solution)/shard_map/ppermute | solution.py:286
  143.7 0.8 pad_maximum_fusion.2.refs_0_
  144.5 10.4 %collective-permute-done.5.refs_3_ = bf16[4,1,32,1024]{3,2,1,0:T(8,128)(2,1)S(1)} collective-permute-done((bf16[4,1,32,1024]{3,2,1,0:T(8,128)(2,1)S(1)}, bf16[4,1,32,1024]{3,2,1,0:T(8,128)(2,1)S(1)}, u32[]{:S(2)}, u32[]{:S(2)}) %collective-permute-start.5) | collective-permute-done | bytes 262176 | tf_op jit(solution)/shard_map/ppermute | solution.py:286
  154.8 0.0 copy-start.3
  154.8 0.0 collective-permute-done.6.refs_4_
  154.8 0.0 copy-start.4
  154.8 0.0 collective-permute-done.7.refs_5_
  154.8 0.0 copy-start.5
  154.9 11.6 %collective-permute-done.8.refs_6_ = bf16[4,1,32,1024]{3,2,1,0:T(8,128)(2,1)S(1)} collective-permute-done((bf16[4,1,32,1024]{3,2,1,0:T(8,128)(2,1)S(1)}, bf16[4,1,32,1024]{3,2,1,0:T(8,128)(2,1)S(1)}, u32[]{:S(2)}, u32[]{:S(2)}) %collective-permute-start.8) | collective-permute-done | bytes 262176 | tf_op jit(solution)/shard_map/ppermute | solution.py:286
  166.5 0.0 copy-start.6
  166.5 6.3 %collective-permute-done.9.refs_7_ = bf16[4,1,32,1024]{3,2,1,0:T(8,128)(2,1)S(1)} collective-permute-done((bf16[4,1,32,1024]{3,2,1,0:T(8,128)(2,1)S(1)}, bf16[4,1,32,1024]{3,2,1,0:T(8,128)(2,1)S(1)}, u32[]{:S(2)}, u32[]{:S(2)}) %collective-permute-start.9) | collective-permute-done | bytes 262176 | tf_op jit(solution)/shard_map/ppermute | solution.py:286
  172.8 0.0 copy-start.7
  172.8 33.9 %all-to-all-done.refs_8_ = bf16[32,3,24,1024]{3,2,1,0:T(8,128)(2,1)} async-done(((bf16[32,3,24,1024]{3,2,1,0:T(8,128)(2,1)}), bf16[32,3,24,1024]{3,2,1,0:T(8,128)(2,1)}, u32[]{:S(2)}, u32[]{:S(2)}) %all-to-all-start) | async-done | bytes 4718624 | tf_op jit(solution)/shard_map/all_to_all | solution.py:281
  206.6 3.7 %all-to-all-start.1 = ((bf16[32,3,8,1024]{3,2,1,0:T(8,128)(2,1)}), bf16[32,3,8,1024]{3,2,1,0:T(8,128)(2,1)S(1)}, u32[]{:S(2)}, u32[]{:S(2)}) async-start(bf16[32,3,8,1024]{3,2,1,0:T(8,128)(2,1)} %get-tuple-element.20), calls=%async_computation.1 | async-start | bytes 3145728 | tf_op jit(solution)/shard_map/all_to_all | solution.py:281
  210.3 0.0 copy-done.1
  210.3 0.0 copy-done.2
  210.3 0.0 copy-done.3
  210.3 0.0 copy-done.4
  210.3 0.0 copy-done.5
  210.4 0.0 copy-done.6
  210.4 0.0 copy-done.7
  210.4 23.2 %correlate.2.refs_9_ = f32[16,1024,1024]{2,1,0:T(8,128)} custom-call(bf16[4,1,32,1024]{3,2,1,0:T(8,128)(2,1)} %pad_maximum_fusion.2.refs_0_, bf16[4,1,32,1024]{3,2,1,0:T(8,128)(2,1)} %copy-done.1, bf16[4,1,32,1024]{3,2,1,0:T(8,128)(2,1)} %copy-done.2, bf16[4,1,32,1024]{3,2,1,0:T(8,128)(2,1)} %copy-done.3, bf16[4,1,32,1024]{3,2,1,0:T(8,128)(2,1)} %copy-done.4, ...), custom_call_target="tpu_custom_call" | custom-call | flops 6442450944 | bytes 56623104 | tf_op jit(solution)/shard_map/correlate/pallas_call | solution.py:260
  233.6 14.3 %all-to-all-done.1.refs_8_ = bf16[32,3,8,1024]{3,2,1,0:T(8,128)(2,1)S(1)} async-done(((bf16[32,3,8,1024]{3,2,1,0:T(8,128)(2,1)}), bf16[32,3,8,1024]{3,2,1,0:T(8,128)(2,1)S(1)}, u32[]{:S(2)}, u32[]{:S(2)}) %all-to-all-start.1) | async-done | bytes 1572896 | tf_op jit(solution)/shard_map/all_to_all | solution.py:281
  247.9 0.0 copy-start
  247.9 1.2 copy-done
  249.1 9.9 %correlate.3 = f32[16,1024,1024]{2,1,0:T(8,128)} custom-call(bf16[4,1,32,1024]{3,2,1,0:T(8,128)(2,1)} %pad_maximum_fusion.2.refs_0_, bf16[4,1,32,1024]{3,2,1,0:T(8,128)(2,1)} %copy-done.1, bf16[4,1,32,1024]{3,2,1,0:T(8,128)(2,1)} %copy-done.2, bf16[4,1,32,1024]{3,2,1,0:T(8,128)(2,1)} %copy-done.3, ...), custom_call_target="tpu_custom_call", output_to_operand_aliasing={{}: (9, {})} | custom-call | flops 2147483648 | bytes 18874368 | tf_op jit(solution)/shard_map/correlate/pallas_call | solution.py:260
  (8 shorter events, 0.3 us)
Async XLA Ops:
  4.8 22.6 %collective-permute-start.10 = (bf16[256,6144]{1,0:T(8,128)(2,1)S(1)}, bf16[256,6144]{1,0:T(8,128)(2,1)}, u32[]{:S(2)}, u32[]{:S(2)}) collective-permute-start(bf16[256,6144]{1,0:T(8,128)(2,1)S(1)} %pad_maximum_fusion), channel_id=1, source_target_pairs={{0,1},{1,2},{2,3},{3,4},{4,5},{5,6},{6,7},{7,8},{8,9},{9,10},{10,1... | collective-permute-start | bytes 9437192 | tf_op jit(solution)/shard_map/ppermute | solution.py:24
  10.6 55.7 %collective-permute-start.11 = (bf16[256,6144]{1,0:T(8,128)(2,1)}, bf16[256,6144]{1,0:T(8,128)(2,1)}, u32[]{:S(2)}, u32[]{:S(2)}) collective-permute-start(bf16[256,6144]{1,0:T(8,128)(2,1)} %pad_maximum_fusion.1), channel_id=1, source_target_pairs={{0,31},{1,0},{2,1},{3,2},{4,3},{5,4},{6,5},{7,6},{8,7},{9,8},{10,9... | collective-permute-start | bytes 9437192 | tf_op jit(solution)/shard_map/ppermute | solution.py:29
  23.0 60.2 %collective-permute-start = (bf16[8,1,32,1024]{3,2,1,0:T(8,128)(2,1)}, bf16[8,1,32,1024]{3,2,1,0:T(8,128)(2,1)}, u32[]{:S(2)}, u32[]{:S(2)}) collective-permute-start(bf16[8,1,32,1024]{3,2,1,0:T(8,128)(2,1)} %get-tuple-element.14), channel_id=1, source_target_pairs={{0,8},{1,9},{2,10},{3,11},{4,12},{5,13},{6,14},{7,15},{8,0},{9,1},... | collective-permute-start | bytes 1572872 | tf_op jit(solution)/shard_map/ppermute | solution.py:286
  23.8 67.2 %collective-permute-start.1 = (bf16[8,1,32,1024]{3,2,1,0:T(8,128)(2,1)}, bf16[8,1,32,1024]{3,2,1,0:T(8,128)(2,1)}, u32[]{:S(2)}, u32[]{:S(2)}) collective-permute-start(bf16[8,1,32,1024]{3,2,1,0:T(8,128)(2,1)} %get-tuple-element.15), channel_id=1, source_target_pairs={{0,16},{1,17},{2,18},{3,19},{4,20},{5,21},{6,22},{7,23},{8,24},{9,... | collective-permute-start | bytes 1572872 | tf_op jit(solution)/shard_map/ppermute | solution.py:286
  26.4 64.6 %collective-permute-start.2 = (bf16[8,1,32,1024]{3,2,1,0:T(8,128)(2,1)}, bf16[8,1,32,1024]{3,2,1,0:T(8,128)(2,1)}, u32[]{:S(2)}, u32[]{:S(2)}) collective-permute-start(bf16[8,1,32,1024]{3,2,1,0:T(8,128)(2,1)} %get-tuple-element.16), channel_id=1, source_target_pairs={{0,24},{1,25},{2,26},{3,27},{4,28},{5,29},{6,30},{7,31},{8,16},{9,... | collective-permute-start | bytes 1572872 | tf_op jit(solution)/shard_map/ppermute | solution.py:286
  83.2 17.8 %copy-start.8 = (bf16[8,1,32,1024]{3,2,1,0:T(8,128)(2,1)S(1)}, bf16[8,1,32,1024]{3,2,1,0:T(8,128)(2,1)}, u32[]{:S(2)}) copy-start(bf16[8,1,32,1024]{3,2,1,0:T(8,128)(2,1)} %get-tuple-element.13) | copy-start | bytes 1572868
  91.0 115.6 %all-to-all-start = ((bf16[32,3,24,1024]{3,2,1,0:T(8,128)(2,1)}), bf16[32,3,24,1024]{3,2,1,0:T(8,128)(2,1)}, u32[]{:S(2)}, u32[]{:S(2)}) async-start(bf16[32,3,24,1024]{3,2,1,0:T(8,128)(2,1)} %get-tuple-element.19), calls=%async_computation | async-start | bytes 9437184 | tf_op jit(solution)/shard_map/all_to_all | solution.py:281
  104.5 4.2 %collective-permute-start.3 = (bf16[4,1,32,1024]{3,2,1,0:T(8,128)(2,1)S(1)}, bf16[4,1,32,1024]{3,2,1,0:T(8,128)(2,1)S(1)}, u32[]{:S(2)}, u32[]{:S(2)}) collective-permute-start(bf16[4,1,32,1024]{3,2,1,0:T(8,128)(2,1)S(1)} %pad_maximum_fusion.3), channel_id=1, source_target_pairs={{0,1},{1,0},{2,3},{3,2},{4,5},{5,4},{6,7},{7,6},{8,9},{9,8},{10,11... | collective-permute-start | bytes 786440 | tf_op jit(solution)/shard_map/ppermute | solution.py:286
  104.8 35.3 %collective-permute-start.4 = (bf16[4,1,32,1024]{3,2,1,0:T(8,128)(2,1)S(1)}, bf16[4,1,32,1024]{3,2,1,0:T(8,128)(2,1)S(1)}, u32[]{:S(2)}, u32[]{:S(2)}) collective-permute-start(bf16[4,1,32,1024]{3,2,1,0:T(8,128)(2,1)S(1)} %pad_maximum_fusion.4), channel_id=1, source_target_pairs={{0,2},{1,3},{2,0},{3,1},{4,6},{5,7},{6,4},{7,5},{8,10},{9,11},{10,... | collective-permute-start | bytes 786440 | tf_op jit(solution)/shard_map/ppermute | solution.py:286
  106.6 48.3 %collective-permute-start.5 = (bf16[4,1,32,1024]{3,2,1,0:T(8,128)(2,1)S(1)}, bf16[4,1,32,1024]{3,2,1,0:T(8,128)(2,1)S(1)}, u32[]{:S(2)}, u32[]{:S(2)}) collective-permute-start(bf16[4,1,32,1024]{3,2,1,0:T(8,128)(2,1)S(1)} %pad_maximum_fusion.5), channel_id=1, source_target_pairs={{0,3},{1,2},{2,1},{3,0},{4,7},{5,6},{6,5},{7,4},{8,11},{9,10},{10,... | collective-permute-start | bytes 786440 | tf_op jit(solution)/shard_map/ppermute | solution.py:286
  106.7 48.1 %collective-permute-start.6 = (bf16[4,1,32,1024]{3,2,1,0:T(8,128)(2,1)S(1)}, bf16[4,1,32,1024]{3,2,1,0:T(8,128)(2,1)S(1)}, u32[]{:S(2)}, u32[]{:S(2)}) collective-permute-start(bf16[4,1,32,1024]{3,2,1,0:T(8,128)(2,1)S(1)} %pad_maximum_fusion.6), channel_id=1, source_target_pairs={{0,4},{1,5},{2,6},{3,7},{4,0},{5,1},{6,2},{7,3},{8,12},{9,13},{10,... | collective-permute-start | bytes 786440 | tf_op jit(solution)/shard_map/ppermute | solution.py:286
  108.5 46.4 %collective-permute-start.7 = (bf16[4,1,32,1024]{3,2,1,0:T(8,128)(2,1)S(1)}, bf16[4,1,32,1024]{3,2,1,0:T(8,128)(2,1)S(1)}, u32[]{:S(2)}, u32[]{:S(2)}) collective-permute-start(bf16[4,1,32,1024]{3,2,1,0:T(8,128)(2,1)S(1)} %pad_maximum_fusion.7), channel_id=1, source_target_pairs={{0,5},{1,4},{2,7},{3,6},{4,1},{5,0},{6,3},{7,2},{8,13},{9,12},{10,... | collective-permute-start | bytes 786440 | tf_op jit(solution)/shard_map/ppermute | solution.py:286
  108.8 101.6 %copy-start.1 = (bf16[4,1,32,1024]{3,2,1,0:T(8,128)(2,1)}, bf16[4,1,32,1024]{3,2,1,0:T(8,128)(2,1)S(1)}, u32[]{:S(2)}) copy-start(bf16[4,1,32,1024]{3,2,1,0:T(8,128)(2,1)S(1)} %collective-permute-done.3.refs_1_) | copy-start | bytes 786436
  108.8 57.7 %collective-permute-start.8 = (bf16[4,1,32,1024]{3,2,1,0:T(8,128)(2,1)S(1)}, bf16[4,1,32,1024]{3,2,1,0:T(8,128)(2,1)S(1)}, u32[]{:S(2)}, u32[]{:S(2)}) collective-permute-start(bf16[4,1,32,1024]{3,2,1,0:T(8,128)(2,1)S(1)} %pad_maximum_fusion.8), channel_id=1, source_target_pairs={{0,6},{1,7},{2,4},{3,5},{4,2},{5,3},{6,0},{7,1},{8,14},{9,15},{10,... | collective-permute-start | bytes 786440 | tf_op jit(solution)/shard_map/ppermute | solution.py:286
  140.1 70.2 %copy-start.2 = (bf16[4,1,32,1024]{3,2,1,0:T(8,128)(2,1)}, bf16[4,1,32,1024]{3,2,1,0:T(8,128)(2,1)S(1)}, u32[]{:S(2)}) copy-start(bf16[4,1,32,1024]{3,2,1,0:T(8,128)(2,1)S(1)} %collective-permute-done.4.refs_2_) | copy-start | bytes 786436
  140.1 32.7 %collective-permute-start.9 = (bf16[4,1,32,1024]{3,2,1,0:T(8,128)(2,1)S(1)}, bf16[4,1,32,1024]{3,2,1,0:T(8,128)(2,1)S(1)}, u32[]{:S(2)}, u32[]{:S(2)}) collective-permute-start(bf16[4,1,32,1024]{3,2,1,0:T(8,128)(2,1)S(1)} %pad_maximum_fusion.9), channel_id=1, source_target_pairs={{0,7},{1,6},{2,5},{3,4},{4,3},{5,2},{6,1},{7,0},{8,15},{9,14},{10,... | collective-permute-start | bytes 786440 | tf_op jit(solution)/shard_map/ppermute | solution.py:286
  154.8 55.5 %copy-start.3 = (bf16[4,1,32,1024]{3,2,1,0:T(8,128)(2,1)}, bf16[4,1,32,1024]{3,2,1,0:T(8,128)(2,1)S(1)}, u32[]{:S(2)}) copy-start(bf16[4,1,32,1024]{3,2,1,0:T(8,128)(2,1)S(1)} %collective-permute-done.5.refs_3_) | copy-start | bytes 786436
  154.8 55.5 %copy-start.4 = (bf16[4,1,32,1024]{3,2,1,0:T(8,128)(2,1)}, bf16[4,1,32,1024]{3,2,1,0:T(8,128)(2,1)S(1)}, u32[]{:S(2)}) copy-start(bf16[4,1,32,1024]{3,2,1,0:T(8,128)(2,1)S(1)} %collective-permute-done.6.refs_4_) | copy-start | bytes 786436
  154.8 55.5 %copy-start.5 = (bf16[4,1,32,1024]{3,2,1,0:T(8,128)(2,1)}, bf16[4,1,32,1024]{3,2,1,0:T(8,128)(2,1)S(1)}, u32[]{:S(2)}) copy-start(bf16[4,1,32,1024]{3,2,1,0:T(8,128)(2,1)S(1)} %collective-permute-done.7.refs_5_) | copy-start | bytes 786436
  166.5 43.9 %copy-start.6 = (bf16[4,1,32,1024]{3,2,1,0:T(8,128)(2,1)}, bf16[4,1,32,1024]{3,2,1,0:T(8,128)(2,1)S(1)}, u32[]{:S(2)}) copy-start(bf16[4,1,32,1024]{3,2,1,0:T(8,128)(2,1)S(1)} %collective-permute-done.8.refs_6_) | copy-start | bytes 786436
  172.8 37.6 %copy-start.7 = (bf16[4,1,32,1024]{3,2,1,0:T(8,128)(2,1)}, bf16[4,1,32,1024]{3,2,1,0:T(8,128)(2,1)S(1)}, u32[]{:S(2)}) copy-start(bf16[4,1,32,1024]{3,2,1,0:T(8,128)(2,1)S(1)} %collective-permute-done.9.refs_7_) | copy-start | bytes 786436
  206.6 41.2 %all-to-all-start.1 = ((bf16[32,3,8,1024]{3,2,1,0:T(8,128)(2,1)}), bf16[32,3,8,1024]{3,2,1,0:T(8,128)(2,1)S(1)}, u32[]{:S(2)}, u32[]{:S(2)}) async-start(bf16[32,3,8,1024]{3,2,1,0:T(8,128)(2,1)} %get-tuple-element.20), calls=%async_computation.1 | async-start | bytes 3145728 | tf_op jit(solution)/shard_map/all_to_all | solution.py:281
  247.9 1.2 copy-start

commit v6 on v5

--- a/solution.py
+++ b/solution.py
@@ -83,7 +83,7 @@
             )
 
     per_dest = table_ref.shape[0] // dests
-    dest_block = dests // planes if planes else max(1, min(dests, 256 // per_dest))
+    dest_block = dests // planes if planes else min(dests, 1 << (256 // per_dest).bit_length() - 1)
     height = dest_block * per_dest
     for slot in range(count):
         filtered = filtered_ref[slot]
@@ -297,7 +297,7 @@
     devices = lax.axis_size("chan")
     channels = CHAN // devices
     count = devices * local
-    table = jnp.asarray(transform_table(frame_len, CHAN))
+    table = transform_table(frame_len, CHAN)
     past = TAPS - 1
     blocks = 4
     block = inputs // blocks
@@ -327,17 +327,20 @@
     def neighbours(ahead, back):
         return passed_along(ahead, "chan", 1), passed_back_round(back, "chan")
 
-    def spectra(arrays, begins, variants, splits, rows, planes=0):
+    def spectra(arrays, begins, variants, table, rows, planes=0):
         return filter_transform(
-            arrays, begins, variants, local, follows, place, tap_weights, table, devices, splits, planes, rows, block
+            arrays, begins, variants, local, follows, place, tap_weights, jnp.asarray(table), devices, [table.shape[0] // devices], planes, rows, block
         )
 
     shares = [channels - channels // 4, channels // 4]
     sent, variants = around(range(blocks))
     arounds = neighbours(*sent)
-    inner_blocks = spectra([voltage], [0], inner, [2 * channels], inputs, devices // PLANE)
+    inner_blocks = spectra([voltage], [0], inner, table, inputs, devices // PLANE)
     arrived = [b if k == 0 else exchanged(b, k * PLANE) for k, b in enumerate(inner_blocks)]
-    parts = spectra([voltage, *arounds], [0, 0, 0], variants, [2 * c for c in shares], inputs)
+    by_device = table.reshape(devices, 2 * channels, frame_len)
+    parts = []
+    for own in np.split(by_device, [2 * shares[0]], 1):
+        parts += spectra([voltage, *arounds], [0, 0, 0], variants, own.reshape(-1, frame_len), inputs)
     first_turned = turn(after(parts[0], arrived))
     stacks = [jnp.concatenate([a[j : j + 1] for a in arrived], 0) for j in range(PLANE)]
     inner_turned = [s if j == 0 else exchanged(s, j) for j, s in enumerate(stacks)]

time: 260 us -> 264 us (1.015)
  Pallas kernels: 58.1 us -> 70.3 us
  waiting for transfers between devices: 152 us -> 140 us
    ppermute x10, waiting for transfers between devices: 64.8 us -> 52.4 us  [exchanged(): return lax.ppermute(block, 'chan', route)]
    pallas_call x2 -> x3, Pallas kernels: 25 us -> 37.2 us  [filter_transform(): pl.pallas_call(functools.partial(filter_transform_kernel, variants, local...]
  transfers between devices with their start and end apart: 14 -> 14, of which waited for: 8 -> 7; matrix products, arithmetic and copies ran while one was open for 3% -> 3% of each run, Pallas kernels for 19% -> 23%
where the time goes in v6:
time: 264 us; the launch traced here: 263 us
  waiting for transfers between devices  140 us (53%)
  Pallas kernels  70.3 us (27%)
  starting transfers between devices  38.4 us (15%)
  local copies, waits for them, and re-layouts  9.02 us (3%)
  other arithmetic  5.26 us (2%)
    ppermute x10, waiting for transfers between devices, exchanged(): return lax.ppermute(block, 'chan', route)  52.4 us
    all_to_all x2, waiting for transfers between devices, turn(): lax.all_to_all(block, 'chan', split_axis=0, concat_axis=0, tiled=True)  48.4 us
    ppermute x1, waiting for transfers between devices, passed_back_round(): lax.ppermute(block, axis, [(i, (i - 1) % devices) for i in range(devices)])  38.9 us
    pallas_call x3, Pallas kernels, filter_transform(): pl.pallas_call(functools.partial(filter_transform_kernel, variants, local...  37.2 us
    pallas_call x2, Pallas kernels, correlate(): pl.pallas_call(functools.partial(correlate_kernel, 1.0 / spectra_count, b...  33.1 us
    all_to_all x2, starting transfers between devices, turn(): lax.all_to_all(block, 'chan', split_axis=0, concat_axis=0, tiled=True)  16.3 us
    ppermute x10, starting transfers between devices, exchanged(): return lax.ppermute(block, 'chan', route)  14.5 us
  transfers between devices with their start and end apart: 14, of which 7 were waited for; matrix products, arithmetic and copies ran while one was open for 3% of the time, Pallas kernels for 23%

profile of v6, /device:TPU:0, one launch (start us, length us, event | category | flops | bytes accessed | tf_op | source)
XLA Modules:
  0.0 263.1 jit_solution(7458636341602359645)
XLA Ops:
  0.0 1.7 fusion
  1.7 2.8 %fusion.1 = (bf16[256,2048]{1,0:T(8,128)(2,1)S(1)}, bf16[256,2048]{1,0:T(8,128)(2,1)S(1)}, bf16[256,2048]{1,0:T(8,128)(2,1)S(1)}, bf16[256,2048]{1,0:T(8,128)(2,1)S(1)}) fusion(bf16[1024,4096]{1,0:T(8,128)(2,1)} %refs_2_.5), kind=kLoop, calls=%fused_computation.12 | loop fusion | bytes 8388608 | tf_op jit(solution)/shard_map/slice | solution.py:322
  4.5 1.8 pad_maximum_fusion
  6.3 2.5 collective-permute-start.10
  8.8 1.8 pad_maximum_fusion.1
  10.6 5.1 %collective-permute-start.11 = (bf16[256,6144]{1,0:T(8,128)(2,1)}, bf16[256,6144]{1,0:T(8,128)(2,1)}, u32[]{:S(2)}, u32[]{:S(2)}) collective-permute-start(bf16[256,6144]{1,0:T(8,128)(2,1)} %pad_maximum_fusion.1), channel_id=1, source_target_pairs={{0,31},{1,0},{2,1},{3,2},{4,3},{5,4},{6,5},{7,6},{8,7},{9,8},{10,9... | collective-permute-start | bytes 9437192 | tf_op jit(solution)/shard_map/ppermute | solution.py:29
  15.7 0.6 pad_add_fusion.refs_1_
  16.4 8.0 %filter_transform.3 = (bf16[8,1,32,1024]{3,2,1,0:T(8,128)(2,1)}, bf16[8,1,32,1024]{3,2,1,0:T(8,128)(2,1)}, bf16[8,1,32,1024]{3,2,1,0:T(8,128)(2,1)}, bf16[8,1,32,1024]{3,2,1,0:T(8,128)(2,1)}) custom-call(f32[1]{0:T(128)} %bitcast.refs_0_, s32[2]{0:T(128)} %pad_add_fusion.refs_1_, bf16[1024,4096]{1,0:T(8,128)(2,1)} %refs_2_.5, f32[4,1024]{1,0:T(4,128)} %refs_5_.3, ...), custom_call_target="tpu_custom_call" | custom-call | flops 2147483648 | bytes 12582912 | tf_op jit(solution)/shard_map/filter_transform/pallas_call | solution.py:134
  24.4 0.8 collective-permute-start
  25.2 2.6 collective-permute-start.1
  27.8 1.0 collective-permute-start.2
  28.8 0.0 collective-permute-done.10.refs_3_
  28.8 0.0 copy-start
  28.8 38.9 %collective-permute-done.11.refs_4_ = bf16[256,6144]{1,0:T(8,128)(2,1)} collective-permute-done((bf16[256,6144]{1,0:T(8,128)(2,1)}, bf16[256,6144]{1,0:T(8,128)(2,1)}, u32[]{:S(2)}, u32[]{:S(2)}) %collective-permute-start.11) | collective-permute-done | bytes 3145760 | tf_op jit(solution)/shard_map/ppermute | solution.py:29
  67.7 0.0 copy-done
  67.7 18.0 %filter_transform.5 = bf16[32,3,24,1024]{3,2,1,0:T(8,128)(2,1)} custom-call(f32[1]{0:T(128)} %bitcast.refs_0_, s32[2]{0:T(128)} %pad_add_fusion.refs_1_, bf16[1024,4096]{1,0:T(8,128)(2,1)} %refs_2_.5, bf16[256,6144]{1,0:T(8,128)(2,1)} %copy-done, bf16[256,6144]{1,0:T(8,128)(2,1)} %collective-permute-done.11.refs_4_, f32[4,1024]{1,0:T(4,128)} %refs_5_.3, ...), custom_call_target="tpu_custom_call" | custom-call | flops 4831838208 | bytes 39845888 | tf_op jit(solution)/shard_map/filter_transform/pallas_call | solution.py:134
  85.7 0.0 collective-permute-done
  85.7 6.8 %collective-permute-done.1 = bf16[8,1,32,1024]{3,2,1,0:T(8,128)(2,1)} collective-permute-done((bf16[8,1,32,1024]{3,2,1,0:T(8,128)(2,1)}, bf16[8,1,32,1024]{3,2,1,0:T(8,128)(2,1)}, u32[]{:S(2)}, u32[]{:S(2)}) %collective-permute-start.1) | collective-permute-done | bytes 524320 | tf_op jit(solution)/shard_map/ppermute | solution.py:286
  92.5 0.0 collective-permute-done.2
  92.5 0.0 copy-start.9
  92.5 12.7 %all-to-all-start = ((bf16[32,3,24,1024]{3,2,1,0:T(8,128)(2,1)}), bf16[32,3,24,1024]{3,2,1,0:T(8,128)(2,1)}, u32[]{:S(2)}, u32[]{:S(2)}) async-start(bf16[32,3,24,1024]{3,2,1,0:T(8,128)(2,1)} %filter_transform.5), calls=%async_computation | async-start | bytes 9437184 | tf_op jit(solution)/shard_map/all_to_all | solution.py:281
  105.2 0.0 copy-done.9
  105.3 1.1 fusion.3
  106.4 1.1 fusion.4
  107.5 1.1 fusion.5
  108.7 0.1 collective-permute-start.3
  108.8 1.7 collective-permute-start.4
  110.6 0.2 collective-permute-start.5
  110.9 1.6 collective-permute-start.6
  112.5 0.2 collective-permute-start.7
  112.8 0.0 collective-permute-done.3.refs_1_
  112.8 0.0 copy-start.2
  112.8 2.6 %collective-permute-start.8 = (bf16[4,1,32,1024]{3,2,1,0:T(8,128)(2,1)S(1)}, bf16[4,1,32,1024]{3,2,1,0:T(8,128)(2,1)S(1)}, u32[]{:S(2)}, u32[]{:S(2)}) collective-permute-start(bf16[4,1,32,1024]{3,2,1,0:T(8,128)(2,1)S(1)} %pad_maximum_fusion.8), channel_id=1, source_target_pairs={{0,6},{1,7},{2,4},{3,5},{4,2},{5,3},{6,0},{7,1},{8,14},{9,15},{10,... | collective-permute-start | bytes 786440 | tf_op jit(solution)/shard_map/ppermute | solution.py:286
  115.4 28.7 %collective-permute-done.4.refs_2_ = bf16[4,1,32,1024]{3,2,1,0:T(8,128)(2,1)S(1)} collective-permute-done((bf16[4,1,32,1024]{3,2,1,0:T(8,128)(2,1)S(1)}, bf16[4,1,32,1024]{3,2,1,0:T(8,128)(2,1)S(1)}, u32[]{:S(2)}, u32[]{:S(2)}) %collective-permute-start.4) | collective-permute-done | bytes 262176 | tf_op jit(solution)/shard_map/ppermute | solution.py:286
  144.1 0.0 copy-start.3
  144.1 3.6 %collective-permute-start.9 = (bf16[4,1,32,1024]{3,2,1,0:T(8,128)(2,1)S(1)}, bf16[4,1,32,1024]{3,2,1,0:T(8,128)(2,1)S(1)}, u32[]{:S(2)}, u32[]{:S(2)}) collective-permute-start(bf16[4,1,32,1024]{3,2,1,0:T(8,128)(2,1)S(1)} %pad_maximum_fusion.9), channel_id=1, source_target_pairs={{0,7},{1,6},{2,5},{3,4},{4,3},{5,2},{6,1},{7,0},{8,15},{9,14},{10,... | collective-permute-start | bytes 786440 | tf_op jit(solution)/shard_map/ppermute | solution.py:286
  147.7 0.8 pad_maximum_fusion.2.refs_0_
  148.5 11.2 %filter_transform.4 = bf16[32,3,8,1024]{3,2,1,0:T(8,128)(2,1)} custom-call(f32[1]{0:T(128)} %bitcast.refs_0_, s32[2]{0:T(128)} %pad_add_fusion.refs_1_, bf16[1024,4096]{1,0:T(8,128)(2,1)} %refs_2_.5, bf16[256,6144]{1,0:T(8,128)(2,1)} %copy-done, bf16[256,6144]{1,0:T(8,128)(2,1)} %collective-permute-done.11.refs_4_, f32[4,1024]{1,0:T(4,128)} %refs_5_.3, ...), custom_call_target="tpu_custom_call" | custom-call | flops 1610612736 | bytes 35651584 | tf_op jit(solution)/shard_map/filter_transform/pallas_call | solution.py:134
  159.7 0.0 copy-done.2
  159.7 0.0 copy-done.3
  159.7 0.0 collective-permute-done.5.refs_3_
  159.7 0.0 copy-start.4
  159.7 0.0 collective-permute-done.6.refs_4_
  159.7 0.0 copy-start.5
  159.7 0.0 collective-permute-done.7.refs_5_
  159.7 0.0 copy-start.6
  159.7 10.8 %collective-permute-done.8.refs_6_ = bf16[4,1,32,1024]{3,2,1,0:T(8,128)(2,1)S(1)} collective-permute-done((bf16[4,1,32,1024]{3,2,1,0:T(8,128)(2,1)S(1)}, bf16[4,1,32,1024]{3,2,1,0:T(8,128)(2,1)S(1)}, u32[]{:S(2)}, u32[]{:S(2)}) %collective-permute-start.8) | collective-permute-done | bytes 262176 | tf_op jit(solution)/shard_map/ppermute | solution.py:286
  170.5 0.0 copy-start.7
  170.5 6.2 %collective-permute-done.9.refs_7_ = bf16[4,1,32,1024]{3,2,1,0:T(8,128)(2,1)S(1)} collective-permute-done((bf16[4,1,32,1024]{3,2,1,0:T(8,128)(2,1)S(1)}, bf16[4,1,32,1024]{3,2,1,0:T(8,128)(2,1)S(1)}, u32[]{:S(2)}, u32[]{:S(2)}) %collective-permute-start.9) | collective-permute-done | bytes 262176 | tf_op jit(solution)/shard_map/ppermute | solution.py:286
  176.7 0.0 copy-start.8
  176.7 33.9 %all-to-all-done.refs_8_ = bf16[32,3,24,1024]{3,2,1,0:T(8,128)(2,1)} async-done(((bf16[32,3,24,1024]{3,2,1,0:T(8,128)(2,1)}), bf16[32,3,24,1024]{3,2,1,0:T(8,128)(2,1)}, u32[]{:S(2)}, u32[]{:S(2)}) %all-to-all-start) | async-done | bytes 4718624 | tf_op jit(solution)/shard_map/all_to_all | solution.py:281
  210.6 3.5 %all-to-all-start.1 = ((bf16[32,3,8,1024]{3,2,1,0:T(8,128)(2,1)}), bf16[32,3,8,1024]{3,2,1,0:T(8,128)(2,1)S(1)}, u32[]{:S(2)}, u32[]{:S(2)}) async-start(bf16[32,3,8,1024]{3,2,1,0:T(8,128)(2,1)} %filter_transform.4), calls=%async_computation.1 | async-start | bytes 3145728 | tf_op jit(solution)/shard_map/all_to_all | solution.py:281
  214.1 0.0 copy-done.4
  214.1 0.0 copy-done.5
  214.2 0.0 copy-done.6
  214.2 0.0 copy-done.7
  214.2 0.0 copy-done.8
  214.2 23.2 %correlate.2.refs_9_ = f32[16,1024,1024]{2,1,0:T(8,128)} custom-call(bf16[4,1,32,1024]{3,2,1,0:T(8,128)(2,1)} %pad_maximum_fusion.2.refs_0_, bf16[4,1,32,1024]{3,2,1,0:T(8,128)(2,1)} %copy-done.2, bf16[4,1,32,1024]{3,2,1,0:T(8,128)(2,1)} %copy-done.3, bf16[4,1,32,1024]{3,2,1,0:T(8,128)(2,1)} %copy-done.4, bf16[4,1,32,1024]{3,2,1,0:T(8,128)(2,1)} %copy-done.5, ...), custom_call_target="tpu_custom_call" | custom-call | flops 6442450944 | bytes 56623104 | tf_op jit(solution)/shard_map/correlate/pallas_call | solution.py:260
  237.4 14.5 %all-to-all-done.1.refs_8_ = bf16[32,3,8,1024]{3,2,1,0:T(8,128)(2,1)S(1)} async-done(((bf16[32,3,8,1024]{3,2,1,0:T(8,128)(2,1)}), bf16[32,3,8,1024]{3,2,1,0:T(8,128)(2,1)S(1)}, u32[]{:S(2)}, u32[]{:S(2)}) %all-to-all-start.1) | async-done | bytes 1572896 | tf_op jit(solution)/shard_map/all_to_all | solution.py:281
  251.9 0.0 copy-start.1
  251.9 1.2 copy-done.1
  253.1 9.9 %correlate.3 = f32[16,1024,1024]{2,1,0:T(8,128)} custom-call(bf16[4,1,32,1024]{3,2,1,0:T(8,128)(2,1)} %pad_maximum_fusion.2.refs_0_, bf16[4,1,32,1024]{3,2,1,0:T(8,128)(2,1)} %copy-done.2, bf16[4,1,32,1024]{3,2,1,0:T(8,128)(2,1)} %copy-done.3, bf16[4,1,32,1024]{3,2,1,0:T(8,128)(2,1)} %copy-done.4, ...), custom_call_target="tpu_custom_call", output_to_operand_aliasing={{}: (9, {})} | custom-call | flops 2147483648 | bytes 18874368 | tf_op jit(solution)/shard_map/correlate/pallas_call | solution.py:260
  (8 shorter events, 0.3 us)
Async XLA Ops:
  6.3 22.5 %collective-permute-start.10 = (bf16[256,6144]{1,0:T(8,128)(2,1)}, bf16[256,6144]{1,0:T(8,128)(2,1)S(1)}, u32[]{:S(2)}, u32[]{:S(2)}) collective-permute-start(bf16[256,6144]{1,0:T(8,128)(2,1)} %pad_maximum_fusion), channel_id=1, source_target_pairs={{0,1},{1,2},{2,3},{3,4},{4,5},{5,6},{6,7},{7,8},{8,9},{9,10},{10,1... | collective-permute-start | bytes 9437192 | tf_op jit(solution)/shard_map/ppermute | solution.py:24
  10.6 57.1 %collective-permute-start.11 = (bf16[256,6144]{1,0:T(8,128)(2,1)}, bf16[256,6144]{1,0:T(8,128)(2,1)}, u32[]{:S(2)}, u32[]{:S(2)}) collective-permute-start(bf16[256,6144]{1,0:T(8,128)(2,1)} %pad_maximum_fusion.1), channel_id=1, source_target_pairs={{0,31},{1,0},{2,1},{3,2},{4,3},{5,4},{6,5},{7,6},{8,7},{9,8},{10,9... | collective-permute-start | bytes 9437192 | tf_op jit(solution)/shard_map/ppermute | solution.py:29
  24.4 61.3 %collective-permute-start = (bf16[8,1,32,1024]{3,2,1,0:T(8,128)(2,1)}, bf16[8,1,32,1024]{3,2,1,0:T(8,128)(2,1)}, u32[]{:S(2)}, u32[]{:S(2)}) collective-permute-start(bf16[8,1,32,1024]{3,2,1,0:T(8,128)(2,1)} %get-tuple-element.12), channel_id=1, source_target_pairs={{0,8},{1,9},{2,10},{3,11},{4,12},{5,13},{6,14},{7,15},{8,0},{9,1},... | collective-permute-start | bytes 1572872 | tf_op jit(solution)/shard_map/ppermute | solution.py:286
  25.2 67.3 %collective-permute-start.1 = (bf16[8,1,32,1024]{3,2,1,0:T(8,128)(2,1)}, bf16[8,1,32,1024]{3,2,1,0:T(8,128)(2,1)}, u32[]{:S(2)}, u32[]{:S(2)}) collective-permute-start(bf16[8,1,32,1024]{3,2,1,0:T(8,128)(2,1)} %get-tuple-element.13), channel_id=1, source_target_pairs={{0,16},{1,17},{2,18},{3,19},{4,20},{5,21},{6,22},{7,23},{8,24},{9,... | collective-permute-start | bytes 1572872 | tf_op jit(solution)/shard_map/ppermute | solution.py:286
  27.8 64.7 %collective-permute-start.2 = (bf16[8,1,32,1024]{3,2,1,0:T(8,128)(2,1)}, bf16[8,1,32,1024]{3,2,1,0:T(8,128)(2,1)}, u32[]{:S(2)}, u32[]{:S(2)}) collective-permute-start(bf16[8,1,32,1024]{3,2,1,0:T(8,128)(2,1)} %get-tuple-element.14), channel_id=1, source_target_pairs={{0,24},{1,25},{2,26},{3,27},{4,28},{5,29},{6,30},{7,31},{8,16},{9,... | collective-permute-start | bytes 1572872 | tf_op jit(solution)/shard_map/ppermute | solution.py:286
  28.8 38.9 %copy-start = (bf16[256,6144]{1,0:T(8,128)(2,1)}, bf16[256,6144]{1,0:T(8,128)(2,1)S(1)}, u32[]{:S(2)}) copy-start(bf16[256,6144]{1,0:T(8,128)(2,1)S(1)} %collective-permute-done.10.refs_3_) | copy-start | bytes 9437188
  92.5 12.8 %copy-start.9 = (bf16[8,1,32,1024]{3,2,1,0:T(8,128)(2,1)S(1)}, bf16[8,1,32,1024]{3,2,1,0:T(8,128)(2,1)}, u32[]{:S(2)}) copy-start(bf16[8,1,32,1024]{3,2,1,0:T(8,128)(2,1)} %get-tuple-element.11) | copy-start | bytes 1572868
  92.5 118.1 %all-to-all-start = ((bf16[32,3,24,1024]{3,2,1,0:T(8,128)(2,1)}), bf16[32,3,24,1024]{3,2,1,0:T(8,128)(2,1)}, u32[]{:S(2)}, u32[]{:S(2)}) async-start(bf16[32,3,24,1024]{3,2,1,0:T(8,128)(2,1)} %filter_transform.5), calls=%async_computation | async-start | bytes 9437184 | tf_op jit(solution)/shard_map/all_to_all | solution.py:281
  108.7 4.1 %collective-permute-start.3 = (bf16[4,1,32,1024]{3,2,1,0:T(8,128)(2,1)S(1)}, bf16[4,1,32,1024]{3,2,1,0:T(8,128)(2,1)S(1)}, u32[]{:S(2)}, u32[]{:S(2)}) collective-permute-start(bf16[4,1,32,1024]{3,2,1,0:T(8,128)(2,1)S(1)} %pad_maximum_fusion.3), channel_id=1, source_target_pairs={{0,1},{1,0},{2,3},{3,2},{4,5},{5,4},{6,7},{7,6},{8,9},{9,8},{10,11... | collective-permute-start | bytes 786440 | tf_op jit(solution)/shard_map/ppermute | solution.py:286
  108.8 35.3 %collective-permute-start.4 = (bf16[4,1,32,1024]{3,2,1,0:T(8,128)(2,1)S(1)}, bf16[4,1,32,1024]{3,2,1,0:T(8,128)(2,1)S(1)}, u32[]{:S(2)}, u32[]{:S(2)}) collective-permute-start(bf16[4,1,32,1024]{3,2,1,0:T(8,128)(2,1)S(1)} %pad_maximum_fusion.4), channel_id=1, source_target_pairs={{0,2},{1,3},{2,0},{3,1},{4,6},{5,7},{6,4},{7,5},{8,10},{9,11},{10,... | collective-permute-start | bytes 786440 | tf_op jit(solution)/shard_map/ppermute | solution.py:286
  110.6 49.1 %collective-permute-start.5 = (bf16[4,1,32,1024]{3,2,1,0:T(8,128)(2,1)S(1)}, bf16[4,1,32,1024]{3,2,1,0:T(8,128)(2,1)S(1)}, u32[]{:S(2)}, u32[]{:S(2)}) collective-permute-start(bf16[4,1,32,1024]{3,2,1,0:T(8,128)(2,1)S(1)} %pad_maximum_fusion.5), channel_id=1, source_target_pairs={{0,3},{1,2},{2,1},{3,0},{4,7},{5,6},{6,5},{7,4},{8,11},{9,10},{10,... | collective-permute-start | bytes 786440 | tf_op jit(solution)/shard_map/ppermute | solution.py:286
  110.9 48.8 %collective-permute-start.6 = (bf16[4,1,32,1024]{3,2,1,0:T(8,128)(2,1)S(1)}, bf16[4,1,32,1024]{3,2,1,0:T(8,128)(2,1)S(1)}, u32[]{:S(2)}, u32[]{:S(2)}) collective-permute-start(bf16[4,1,32,1024]{3,2,1,0:T(8,128)(2,1)S(1)} %pad_maximum_fusion.6), channel_id=1, source_target_pairs={{0,4},{1,5},{2,6},{3,7},{4,0},{5,1},{6,2},{7,3},{8,12},{9,13},{10,... | collective-permute-start | bytes 786440 | tf_op jit(solution)/shard_map/ppermute | solution.py:286
  112.5 47.2 %collective-permute-start.7 = (bf16[4,1,32,1024]{3,2,1,0:T(8,128)(2,1)S(1)}, bf16[4,1,32,1024]{3,2,1,0:T(8,128)(2,1)S(1)}, u32[]{:S(2)}, u32[]{:S(2)}) collective-permute-start(bf16[4,1,32,1024]{3,2,1,0:T(8,128)(2,1)S(1)} %pad_maximum_fusion.7), channel_id=1, source_target_pairs={{0,5},{1,4},{2,7},{3,6},{4,1},{5,0},{6,3},{7,2},{8,13},{9,12},{10,... | collective-permute-start | bytes 786440 | tf_op jit(solution)/shard_map/ppermute | solution.py:286
  112.8 46.9 %copy-start.2 = (bf16[4,1,32,1024]{3,2,1,0:T(8,128)(2,1)}, bf16[4,1,32,1024]{3,2,1,0:T(8,128)(2,1)S(1)}, u32[]{:S(2)}) copy-start(bf16[4,1,32,1024]{3,2,1,0:T(8,128)(2,1)S(1)} %collective-permute-done.3.refs_1_) | copy-start | bytes 786436
  112.8 57.7 %collective-permute-start.8 = (bf16[4,1,32,1024]{3,2,1,0:T(8,128)(2,1)S(1)}, bf16[4,1,32,1024]{3,2,1,0:T(8,128)(2,1)S(1)}, u32[]{:S(2)}, u32[]{:S(2)}) collective-permute-start(bf16[4,1,32,1024]{3,2,1,0:T(8,128)(2,1)S(1)} %pad_maximum_fusion.8), channel_id=1, source_target_pairs={{0,6},{1,7},{2,4},{3,5},{4,2},{5,3},{6,0},{7,1},{8,14},{9,15},{10,... | collective-permute-start | bytes 786440 | tf_op jit(solution)/shard_map/ppermute | solution.py:286
  144.1 15.6 %copy-start.3 = (bf16[4,1,32,1024]{3,2,1,0:T(8,128)(2,1)}, bf16[4,1,32,1024]{3,2,1,0:T(8,128)(2,1)S(1)}, u32[]{:S(2)}) copy-start(bf16[4,1,32,1024]{3,2,1,0:T(8,128)(2,1)S(1)} %collective-permute-done.4.refs_2_) | copy-start | bytes 786436
  144.1 32.6 %collective-permute-start.9 = (bf16[4,1,32,1024]{3,2,1,0:T(8,128)(2,1)S(1)}, bf16[4,1,32,1024]{3,2,1,0:T(8,128)(2,1)S(1)}, u32[]{:S(2)}, u32[]{:S(2)}) collective-permute-start(bf16[4,1,32,1024]{3,2,1,0:T(8,128)(2,1)S(1)} %pad_maximum_fusion.9), channel_id=1, source_target_pairs={{0,7},{1,6},{2,5},{3,4},{4,3},{5,2},{6,1},{7,0},{8,15},{9,14},{10,... | collective-permute-start | bytes 786440 | tf_op jit(solution)/shard_map/ppermute | solution.py:286
  159.7 54.5 %copy-start.4 = (bf16[4,1,32,1024]{3,2,1,0:T(8,128)(2,1)}, bf16[4,1,32,1024]{3,2,1,0:T(8,128)(2,1)S(1)}, u32[]{:S(2)}) copy-start(bf16[4,1,32,1024]{3,2,1,0:T(8,128)(2,1)S(1)} %collective-permute-done.5.refs_3_) | copy-start | bytes 786436
  159.7 54.4 %copy-start.5 = (bf16[4,1,32,1024]{3,2,1,0:T(8,128)(2,1)}, bf16[4,1,32,1024]{3,2,1,0:T(8,128)(2,1)S(1)}, u32[]{:S(2)}) copy-start(bf16[4,1,32,1024]{3,2,1,0:T(8,128)(2,1)S(1)} %collective-permute-done.6.refs_4_) | copy-start | bytes 786436
  159.7 54.4 %copy-start.6 = (bf16[4,1,32,1024]{3,2,1,0:T(8,128)(2,1)}, bf16[4,1,32,1024]{3,2,1,0:T(8,128)(2,1)S(1)}, u32[]{:S(2)}) copy-start(bf16[4,1,32,1024]{3,2,1,0:T(8,128)(2,1)S(1)} %collective-permute-done.7.refs_5_) | copy-start | bytes 786436
  170.5 43.7 %copy-start.7 = (bf16[4,1,32,1024]{3,2,1,0:T(8,128)(2,1)}, bf16[4,1,32,1024]{3,2,1,0:T(8,128)(2,1)S(1)}, u32[]{:S(2)}) copy-start(bf16[4,1,32,1024]{3,2,1,0:T(8,128)(2,1)S(1)} %collective-permute-done.8.refs_6_) | copy-start | bytes 786436
  176.7 37.5 %copy-start.8 = (bf16[4,1,32,1024]{3,2,1,0:T(8,128)(2,1)}, bf16[4,1,32,1024]{3,2,1,0:T(8,128)(2,1)S(1)}, u32[]{:S(2)}) copy-start(bf16[4,1,32,1024]{3,2,1,0:T(8,128)(2,1)S(1)} %collective-permute-done.9.refs_7_) | copy-start | bytes 786436
  210.6 41.3 %all-to-all-start.1 = ((bf16[32,3,8,1024]{3,2,1,0:T(8,128)(2,1)}), bf16[32,3,8,1024]{3,2,1,0:T(8,128)(2,1)S(1)}, u32[]{:S(2)}, u32[]{:S(2)}) async-start(bf16[32,3,8,1024]{3,2,1,0:T(8,128)(2,1)} %filter_transform.4), calls=%async_computation.1 | async-start | bytes 3145728 | tf_op jit(solution)/shard_map/all_to_all | solution.py:281
  251.9 1.2 copy-start.1
